TPU v7x, 32 devices: a whole 2x2x4 slice. The times are simulated.
32 devices in a mesh: comp: 2 (over core), tile: 4 (over y, x), row: 4 (over z).
Axes of the slice: x: 2, y: 2, z: 4, core: 2. Of those that a mesh axis runs over, the one named last changes fastest.
Arguments:
- state: bfloat16 [2, 4, 512, 12288], P('comp', 'tile', 'row'), may hold values from -8 to 8
- pairs: int32 [2, 512], replicated, may hold values from 0 to 511, as said below
- wet: int32 [4], P('tile'), may hold values 0 or 1
- mix_weight: bfloat16 [2, 8, 32, 16], replicated, may hold values from -1 to 1
- depth_weight: float32 [3, 7, 7, 192], replicated, may hold values from -0.875 to 0.875
- norm_gain: float32 [3, 192], replicated, may hold values from 0.1 to 1.9
- inner_weight: bfloat16 [3, 192, 768], replicated, may hold values from -0.4375 to 0.4375
- outer_weight: bfloat16 [3, 768, 192], replicated, may hold values from -0.21875 to 0.21875
Outputs:
- next_state: bfloat16 [2, 4, 512, 12288], P('comp', 'tile', 'row')
Inputs may be any that keep to these rules, and one draw needn't show every extreme that they name: Each row pairs[s] is a permutation of the 512 blocks of the other section, and a block's partner lies in the same band of 128 tile rows. Within one band, the 32 blocks of tile q of one section receive exactly 8 blocks from that band of each tile of the other section.
All inputs are finite; a program needn't handle non-finite values. No bound on the sum of `wet` on one device may be relied on, other than what follows from the above.
Results may differ from a plain program's by a relative error of at most 0.0053.
Values may be sent and summed in bfloat16 or wider, within the bound.
No kernel may reach another device: no remote copies, remote signals or barrier semaphores. Data moves between devices by JAX's collectives and lax.ppermute only.
A program may use at most 64 MiB of HBM per device.

v0:
```python
import jax
import jax.numpy as jnp
from jax import lax
from jax.experimental import pallas as pl
from jax.experimental.pallas import tpu as pltpu
from jax.sharding import PartitionSpec as P

VM = pltpu.VMEM
PC = 8
LG = 16
LN = 128


def lane_bit(shape, bit):
    return (lax.broadcasted_iota(jnp.int32, shape, 1) & bit) == 0


def lroll(x, shift):
    return pltpu.roll(x, shift % LN, 1)


def swap_stage(a, b, bit, m):
    return jnp.where(m, a, lroll(b, bit)), jnp.where(m, lroll(a, -bit), b)


def to_patch(v):
    half = len(v) // 2
    shape = v[0].shape
    m64, m32, m16 = (lane_bit(shape, b) for b in (64, 32, 16))
    per = 3
    u = {}
    for j in range(4):
        for t in range(per):
            q = per * j + t
            a, b = v[q // 2], v[q // 2 + half]
            if q % 2 == 0:
                u[j, t] = jnp.where(m64, a, lroll(b, 64))
            else:
                u[j, t] = jnp.where(m64, lroll(a, 64), b)
    out = []
    for t in range(per):
        a0, b0 = swap_stage(u[0, t], u[2, t], 32, m32)
        a1, b1 = swap_stage(u[1, t], u[3, t], 32, m32)
        out += swap_stage(a0, a1, 16, m16)
        out += swap_stage(b0, b1, 16, m16)
    return out


def from_patch(z):
    half = len(z) // 2
    shape = z[0].shape
    m64, m32, m16 = (lane_bit(shape, b) for b in (64, 32, 16))
    per = len(z) // 4
    u = {}
    for t in range(per):
        a0, a1 = swap_stage(z[4 * t], z[4 * t + 1], 16, m16)
        b0, b1 = swap_stage(z[4 * t + 2], z[4 * t + 3], 16, m16)
        u[0, t], u[2, t] = swap_stage(a0, b0, 32, m32)
        u[1, t], u[3, t] = swap_stage(a1, b1, 32, m32)
    lo, hi = {}, {}
    for j in range(4):
        for t in range(per):
            q = per * j + t
            lo[q] = u[j, t]
            hi[q] = u[j, t]
    v = []
    for n in range(half):
        e, o = u[divmod(2 * n, per)], u[divmod(2 * n + 1, per)]
        v.append(jnp.where(m64, e, lroll(o, 64)))
    for n in range(half):
        e, o = u[divmod(2 * n, per)], u[divmod(2 * n + 1, per)]
        v.append(jnp.where(m64, lroll(e, 64), o))
    return v


def gelu(v):
    return 0.5 * v * (1.0 + jnp.tanh(0.7978845608028654 * (v + 0.044715 * v * v * v)))


def pack_kernel(pairs, place, x_ref, z_ref, out_ref, count):
    section, tile, band = place[0], place[1], place[2]
    nz, rows, _ = z_ref.shape
    width = x_ref.shape[1]
    per = LN * 12
    nj = width // per
    ng = nz // nj
    hold, tiles = out_ref.shape[0], count.shape[0]
    peer = hold // tiles
    of_tile = pairs.shape[1] // tiles
    ncb = nj // 2

    for j in range(nj):
        v = [x_ref[:, j * per + n * LN:j * per + (n + 1) * LN] for n in range(12)]
        for g, zz in enumerate(to_patch(v)):
            z_ref[g * nj + j] = zz
    for q in range(tiles):
        count[q] = 0

    @pl.loop(0, tiles)
    def _(q):
        @pl.loop(0, hold)
        def _(slot):
            source = pairs[1 - section, q * of_tile + band * hold + slot]

            @pl.when(source // of_tile == tile)
            def _():
                local = source % of_tile - band * hold
                rank = count[q]
                count[q] = rank + 1
                row = pl.ds(pl.multiple_of(local // ncb * 16, 16), 16)
                for g in range(out_ref.shape[1] // 2):
                    for h in range(2):
                        out_ref[q * peer + rank, 2 * g + h] = z_ref[g * nj + 2 * (local % ncb) + h, row, :]


def pack(pairs, place, x, tiles, mixed):
    rows, width = x.shape
    nj = width // (LN * 12)
    hold = rows // 16 * (nj // 2)
    vm = pl.BlockSpec(memory_space=VM)
    sm = pl.BlockSpec(memory_space=pltpu.SMEM)
    return pl.pallas_call(
        pack_kernel,
        out_shape=(
            jax.ShapeDtypeStruct((12 * nj, rows, LN), jnp.bfloat16),
            jax.ShapeDtypeStruct((hold, 2 * mixed, 16, LN), jnp.bfloat16),
        ),
        in_specs=[sm, sm, vm],
        out_specs=(vm, vm),
        scratch_shapes=[pltpu.SMEM((tiles,), jnp.int32)],
        compiler_params=pltpu.CompilerParams(vmem_limit_bytes=56 * 2**20),
        name="pack",
    )(pairs, place, x)


def mix_kernel(pairs, place, z_ref, got_ref, w_ref, out_ref, top_ref, bot_ref, zp, count):
    section, tile, band = place[0], place[1], place[2]
    nz, rows, _ = z_ref.shape
    hold, tiles = got_ref.shape[0], count.shape[0]
    mixed = w_ref.shape[0]
    nj = zp.shape[0] // mixed
    peer = hold // tiles
    of_tile = pairs.shape[1] // tiles
    ncb = nj // 2
    for q in range(tiles):
        count[q] = 0

    @pl.loop(0, hold)
    def _(slot):
        q = pairs[section, tile * of_tile + band * hold + slot] // of_tile
        rank = count[q]
        count[q] = rank + 1
        row = pl.ds(pl.multiple_of(slot // ncb * 16, 16), 16)
        for g in range(mixed):
            for h in range(2):
                zp[g * nj + 2 * (slot % ncb) + h, row, :] = got_ref[q * peer + rank, 2 * g + h]

    @pl.loop(0, mixed)
    def _(g):
        gs = pl.ds(g * nj, nj)
        own = z_ref[gs].reshape(nj * rows, LN)
        both = jnp.concatenate([own, zp[gs].reshape(nj * rows, LN)], 1)
        new = own.astype(jnp.float32) + jnp.dot(both, w_ref[g], preferred_element_type=jnp.float32)
        new = new.astype(jnp.bfloat16).reshape(nj, rows, LN)
        out_ref[gs] = new
        top_ref[gs] = new[:, :3]
        bot_ref[gs] = new[:, rows - 3:]

    for n in range(mixed * nj, nz):
        out_ref[n] = z_ref[n]
        top_ref[n] = z_ref[n, :3]
        bot_ref[n] = z_ref[n, rows - 3:]


def mix(pairs, place, z, got, w, tiles):
    nz, rows, _ = z.shape
    nj = nz // 12
    mixed = w.shape[0]
    vm = pl.BlockSpec(memory_space=VM)
    sm = pl.BlockSpec(memory_space=pltpu.SMEM)
    edge = jax.ShapeDtypeStruct((nz, 3, LN), jnp.bfloat16)
    return pl.pallas_call(
        mix_kernel,
        out_shape=(jax.ShapeDtypeStruct(z.shape, jnp.bfloat16), edge, edge),
        in_specs=[sm, sm, vm, vm, vm],
        out_specs=(vm, vm, vm),
        scratch_shapes=[VM((mixed * nj, rows, LN), jnp.bfloat16), pltpu.SMEM((tiles,), jnp.int32)],
        compiler_params=pltpu.CompilerParams(vmem_limit_bytes=56 * 2**20),
        name="mix",
    )(pairs, place, z, got, w)


def layer_kernel(z_ref, top_ref, bot_ref, fac_ref, e_ref, gain_ref, wie_ref, wio_ref, woe_ref, woo_ref,
                 out_ref, outz_ref, otop_ref, obot_ref, zf, lhs, wk, spr, nz, ssum, upd):
    ng = e_ref.shape[0]
    nj = z_ref.shape[0] // ng
    rows = z_ref.shape[1]
    hr = rows // 2
    pad = 8
    m64 = lane_bit((hr, LN), 64)
    delta = lax.broadcasted_iota(jnp.int32, (LG, LN), 0) == lax.broadcasted_iota(jnp.int32, (LG, LN), 1) % LG
    chunk = lax.broadcasted_iota(jnp.int32, (8, LN), 1) // LG

    wk[...] = jnp.zeros_like(wk)
    ssum[...] = jnp.zeros_like(ssum)

    @pl.loop(0, ng)
    def _(g):
        e = e_ref[g]
        for pos, jr in enumerate(list(range(8)) + list(range(8, 12)) + list(range(-4, 0))):
            s = jr - 3
            if abs(s) >= 8 or jr == -4 or jr == 11:
                continue
            r = lroll(e, s * LG)
            r = jnp.where((chunk >= s) & (chunk < 8 + s), r, 0.0)
            for k in range(7):
                tile = jnp.where(delta, jnp.broadcast_to(r[k:k + 1], (LG, LN)), 0.0).astype(jnp.bfloat16)
                wk[pl.ds(k * 256 + pos * LG, LG), 0:LN] = tile
                wk[pl.ds((k + 1) * 256 + pos * LG, LG), LN:2 * LN] = tile
        for j in range(nj):
            zf[j, pl.ds(pad, rows), :] = z_ref[g * nj + j].astype(jnp.float32)
            zf[j, pl.ds(pad - 3, 3), :] = top_ref[g * nj + j].astype(jnp.float32)
            zf[j, pl.ds(pad + rows, 3), :] = bot_ref[g * nj + j].astype(jnp.float32)
        zero = jnp.zeros((hr, LN), jnp.bfloat16)
        for a in range(8):
            v = [zf[j, pl.ds(pad - 3 + a, hr, stride=2), :].astype(jnp.bfloat16) for j in range(nj)]
            for j in range(nj):
                nxt = v[j + 1] if j + 1 < nj else zero
                prv = v[j - 1] if j > 0 else zero
                lhs[pl.ds(j * hr, hr), a * 256:a * 256 + LN] = v[j]
                lhs[pl.ds(j * hr, hr), a * 256 + LN:a * 256 + 256] = jnp.where(m64, nxt, prv)
        sp = jnp.dot(lhs[...], wk[...], preferred_element_type=jnp.float32)
        spr[g] = sp
        ssum[...] += sp

    count = ng * LG
    ones = (lax.broadcasted_iota(jnp.int32, (256, 256), 0) // LG == lax.broadcasted_iota(jnp.int32, (256, 256), 1) // LG)
    ones = ones.astype(jnp.float32).astype(jnp.bfloat16)

    def lane_sum(s):
        hi = s.astype(jnp.bfloat16)
        lo = (s - hi.astype(jnp.float32)).astype(jnp.bfloat16)
        return (jnp.dot(hi, ones, preferred_element_type=jnp.float32)
                + jnp.dot(lo, ones, preferred_element_type=jnp.float32))

    @pl.loop(0, nj)
    def _(j):
        js = pl.ds(pl.multiple_of(j * hr, hr), hr)
        mean = lane_sum(ssum[js, :]) * (1.0 / count)
        q = jnp.zeros((hr, 256), jnp.float32)
        for g in range(ng):
            c = spr[g, js, :] - mean
            q = q + c * c
        rstd = lax.rsqrt(lane_sum(q) * (1.0 / count) + 1e-06)
        for g in range(ng):
            nz[g, js, :] = ((spr[g, js, :] - mean) * rstd * gain_ref[g:g + 1, :]).astype(jnp.bfloat16)

        nat = [[], []]
        for p in range(2):
            nat[p] = from_patch([nz[g, js, p * LN:(p + 1) * LN] for g in range(ng)])
        nat = [jnp.concatenate([a, b], 0) for a, b in zip(*nat)]
        npair = len(nat) // 3
        xe = jnp.concatenate([jnp.concatenate([nat[3 * i], nat[3 * i + 1]], 1) for i in range(npair)], 0)
        xo = jnp.concatenate([jnp.concatenate([nat[3 * i + 1], nat[3 * i + 2]], 1) for i in range(npair)], 0)

        def mlp(x, wi, wo):
            h = gelu(jnp.dot(x, wi[...], preferred_element_type=jnp.float32)).astype(jnp.bfloat16)
            return jnp.dot(h, wo[...], preferred_element_type=jnp.float32)
        ue = mlp(xe, wie_ref, woe_ref)
        uo = mlp(xo, wio_ref, woo_ref)
        for i in range(npair):
            e = ue[i * rows:(i + 1) * rows]
            o = uo[i * rows:(i + 1) * rows]
            for t, val in enumerate((e[:, :LN], e[:, LN:] + o[:, :LN], o[:, LN:])):
                for p in range(2):
                    upd[3 * i + t, pl.ds(p, hr, stride=2), :] = val[p * hr:(p + 1) * hr]
        fac = fac_ref[0, 0]
        res = []
        own = from_patch([z_ref[g * nj + j] for g in range(ng)])
        for n in range(3 * npair):
            ls = pl.ds(pl.multiple_of(j * (3 * npair * LN) + n * LN, LN), LN)
            y = (own[n].astype(jnp.float32) + fac * upd[n]).astype(jnp.bfloat16)
            out_ref[:, ls] = y
            res.append(y)
        for g, zz in enumerate(to_patch(res)):
            outz_ref[g * nj + j] = zz
            otop_ref[g * nj + j] = zz[:3]
            obot_ref[g * nj + j] = zz[rows - 3:]


def layer(z, top, bot, fac, e, gain, wie, wio, woe, woo):
    ng = e.shape[0]
    nj = z.shape[0] // ng
    rows = z.shape[1]
    hr = rows // 2
    vm = pl.BlockSpec(memory_space=VM)
    f32, bf = jnp.float32, jnp.bfloat16
    edge = jax.ShapeDtypeStruct(top.shape, bf)
    return pl.pallas_call(
        layer_kernel,
        out_shape=(jax.ShapeDtypeStruct((rows, nj * 12 * LN), bf), jax.ShapeDtypeStruct(z.shape, bf), edge, edge),
        in_specs=[vm] * 3 + [pl.BlockSpec(memory_space=pltpu.SMEM)] + [vm] * 6,
        out_specs=(vm,) * 4,
        scratch_shapes=[
            VM((nj, rows + 16, LN), f32),
            VM((nj * hr, 2048), bf),
            VM((2048, 256), bf),
            VM((ng, nj * hr, 256), f32),
            VM((ng, nj * hr, 256), bf),
            VM((nj * hr, 256), f32),
            VM((12, rows, LN), f32),
        ],
        compiler_params=pltpu.CompilerParams(vmem_limit_bytes=56 * 2**20),
        name="layer",
    )(z, top, bot, fac, e, gain, wie, wio, woe, woo)


def prep(depth, gain, inner, outer):
    c = gain.shape[0]
    ng = c // LG
    e = jnp.pad(depth[:, ::-1, :], ((0, 1), (0, 1), (0, 0))).reshape(8, 8, ng, LG)
    e = e.transpose(2, 0, 1, 3).reshape(ng, 8, LN)
    gl = jnp.tile(gain.reshape(ng, 1, LG), (1, 16, 1)).reshape(ng, 256)
    wie = jnp.pad(inner, ((0, 64), (0, 0)))
    wio = jnp.pad(inner, ((64, 0), (0, 0)))
    woe = jnp.pad(outer, ((0, 0), (0, 64)))
    woo = jnp.pad(outer, ((0, 0), (64, 0)))
    return e, gl, wie, wio, woe, woo


def halo(top, bot):
    n = lax.axis_size("row")
    return (
        lax.ppermute(bot, "row", [(i, i + 1) for i in range(n - 1)]),
        lax.ppermute(top, "row", [(i + 1, i) for i in range(n - 1)]),
    )


def mix_prep(w):
    groups = w.shape[0]
    parts = w.reshape(groups, 2, 1, LG, 1, LG)
    eye = jnp.eye(PC, dtype=jnp.bool_).reshape(1, 1, PC, 1, PC, 1)
    return jnp.where(eye, parts, jnp.zeros((), w.dtype)).reshape(groups, 2 * LN, LN)


def on_device(state, pairs, wet, mix_weight, depth_weight, norm_gain, inner_weight, outer_weight):
    section = lax.axis_index("comp")
    tiles = lax.axis_size("tile")
    place = jnp.stack([section, lax.axis_index("tile"), lax.axis_index("row")]).astype(jnp.int32)
    x = state[0, 0]
    pick = lambda w, i: lax.dynamic_index_in_dim(w, i, 0, keepdims=False)
    z, outgoing = pack(pairs, place, x, tiles, mix_weight.shape[1])
    crossed = lax.ppermute(outgoing, "comp", [(0, 1), (1, 0)])
    received = lax.all_to_all(crossed, "tile", split_axis=0, concat_axis=0, tiled=True)
    z, top, bot = mix(pairs, place, z, received, mix_prep(pick(mix_weight, section)), tiles)
    top, bot = halo(top, bot)
    which = jnp.where(section == 0, 0, 2)
    weights = prep(pick(depth_weight, which), pick(norm_gain, which), pick(inner_weight, which), pick(outer_weight, which))
    factor = jnp.where(section == 0, 1.0, wet[0].astype(jnp.float32)).reshape(1, 1)
    _, z, top, bot = layer(z, top, bot, factor, *weights)
    top, bot = halo(top, bot)
    weights = prep(depth_weight[1], norm_gain[1], inner_weight[1], outer_weight[1])
    factor = jnp.where(section == 0, 1.0, 0.0).reshape(1, 1)
    out, _, _, _ = layer(z, top, bot, factor, *weights)
    return out[None, None]


def solution(mesh):
    return jax.shard_map(
        on_device,
        mesh=mesh,
        in_specs=(P("comp", "tile", "row", None), P(), P("tile"), P(), P(), P(), P(), P()),
        out_specs=P("comp", "tile", "row", None),
        check_vma=False,
    )
```

profile of v0, /device:TPU:0, one launch (start us, length us, event | category | flops | bytes accessed | tf_op | source)
XLA Modules:
  0.0 154.3 jit_solution(10416512483198177949)
XLA Ops:
  0.6 11.9 %pack.1 = (bf16[96,128,128]{2,1,0:T(8,128)(2,1)}, bf16[32,16,16,128]{3,2,1,0:T(8,128)(2,1)}) custom-call(s32[2,512]{1,0:T(2,128)} %pairs.3, s32[3]{0:T(128)} %pad_add_fusion.place, bf16[128,12288]{1,0:T(8,128)(2,1)} %bitcast.37), custom_call_target="tpu_custom_call" | custom-call | tf_op jit(solution)/shard_map/pack/pallas_call | solution.py:122
  13.0 4.1 %collective-permute-done = bf16[32,16,16,128]{3,2,1,0:T(8,128)(2,1)} collective-permute-done((bf16[32,16,16,128]{3,2,1,0:T(8,128)(2,1)}, bf16[32,16,16,128]{3,2,1,0:T(8,128)(2,1)}, u32[]{:S(2)}, u32[]{:S(2)}) %collective-permute-start) | collective-permute-done | bytes 2097184 | tf_op jit(solution)/shard_map/ppermute | solution.py:353
  17.1 5.1 %all-to-all-start = ((bf16[32,16,16,128]{3,2,1,0:T(8,128)(2,1)}), bf16[32,16,16,128]{3,2,1,0:T(8,128)(2,1)S(1)}, u32[]{:S(2)}, u32[]{:S(2)}) async-start(bf16[32,16,16,128]{3,2,1,0:T(8,128)(2,1)} %collective-permute-done), calls=%async_computation | async-start | bytes 4194304 | tf_op jit(solution)/shard_map/all_to_all | solution.py:354
  22.3 3.0 %broadcast_in_dim.35 = bf16[8,2,8,16,8,16]{5,4,3,2,1,0:T(8,128)(2,1)} broadcast(bf16[8,2,16,16]{3,2,1,0:T(8,128)(2,1)S(1)} %bitcast.42), dimensions={0,1,3,5} | broadcast | bytes 532480 | tf_op jit(solution)/shard_map/jit(_where)/broadcast_in_dim | solution.py:343
  25.3 5.1 %broadcast_in_dim.36 = bf16[8,256,128]{2,1,0:T(8,128)(2,1)S(1)} reshape(bf16[8,2,8,16,8,16]{5,4,3,2,1,0:T(8,128)(2,1)} %broadcast_in_dim.35) | data formatting | bytes 1048576 | tf_op jit(solution)/shard_map/jit(_where)/broadcast_in_dim | solution.py:343
  31.0 1.1 fusion.1
  34.3 1.0 reshape.43
  36.2 1.8 %reshape.44.e_ref = f32[12,8,128]{2,1,0:T(8,128)} reshape(f32[12,8,8,16]{3,2,1,0:T(8,128)} %copy.13) | data formatting | bytes 98304 | tf_op jit(solution)/shard_map/reshape | solution.py:322
  42.3 1.8 %reshape.47.e_ref = f32[12,8,128]{2,1,0:T(8,128)} reshape(f32[12,8,8,16]{3,2,1,0:T(8,128)} %copy.15) | data formatting | bytes 98304 | tf_op jit(solution)/shard_map/reshape | solution.py:322
  44.9 2.2 %fusion.3 = (bf16[768,256]{1,0:T(8,128)(2,1)}, bf16[768,256]{1,0:T(8,128)(2,1)}) fusion(bf16[768,192]{1,0:T(8,128)(2,1)} %bitcast.41), kind=kLoop, calls=%fused_computation.14 | loop fusion | bytes 1081344 | tf_op jit(solution)/shard_map/jit(_pad)/pad | solution.py:327
  47.1 1.1 slice_bitcast_fusion
  48.2 1.0 fusion.5
  50.0 1.3 copy-done.1
  51.3 7.7 %mix.1 = (bf16[96,128,128]{2,1,0:T(8,128)(2,1)}, bf16[96,3,128]{2,1,0:T(4,128)(2,1)}, bf16[96,3,128]{2,1,0:T(4,128)(2,1)}) custom-call(s32[2,512]{1,0:T(2,128)} %pairs.3, s32[3]{0:T(128)} %pad_add_fusion.place, bf16[96,128,128]{2,1,0:T(8,128)(2,1)} %get-tuple-element.14.z_ref, bf16[32,16,16,128]{3,2,1,0:T(8,128)(2,1)} %copy-done.1, ...), custom_call_target="tpu_custom_call" | custom-call | tf_op jit(solution)/shard_map/mix/pallas_call | solution.py:182
  59.0 3.4 %collective-permute-start.1 = (bf16[96,3,128]{2,1,0:T(4,128)(2,1)}, bf16[96,3,128]{2,1,0:T(4,128)(2,1)S(1)}, u32[]{:S(2)}, u32[]{:S(2)}) collective-permute-start(bf16[96,3,128]{2,1,0:T(4,128)(2,1)} %get-tuple-element.17), channel_id=1, source_target_pairs={{0,1},{1,2},{2,3},{4,5},{5,6},{6,7},{8,9},{9,10},{10,11},{12,13},{... | collective-permute-start | bytes 221192 | tf_op jit(solution)/shard_map/ppermute | solution.py:334
  62.4 1.3 collective-permute-start.2
  63.7 1.1 fusion.2
  65.0 4.2 %collective-permute-done.2.bot_ref = bf16[96,3,128]{2,1,0:T(4,128)(2,1)S(1)} collective-permute-done((bf16[96,3,128]{2,1,0:T(4,128)(2,1)}, bf16[96,3,128]{2,1,0:T(4,128)(2,1)S(1)}, u32[]{:S(2)}, u32[]{:S(2)}) %collective-permute-start.2) | collective-permute-done | bytes 73760 | tf_op jit(solution)/shard_map/ppermute | solution.py:335
  69.8 36.8 %layer.2 = (bf16[128,12288]{1,0:T(8,128)(2,1)}, bf16[96,128,128]{2,1,0:T(8,128)(2,1)}, bf16[96,3,128]{2,1,0:T(4,128)(2,1)}, bf16[96,3,128]{2,1,0:T(4,128)(2,1)}) custom-call(bf16[96,128,128]{2,1,0:T(8,128)(2,1)} %get-tuple-element.16.z_ref, bf16[96,3,128]{2,1,0:T(4,128)(2,1)} %copy-done.3, bf16[96,3,128]{2,1,0:T(4,128)(2,1)} %copy-done.5, ...), custom_call_target="tpu_custom_call" | custom-call | tf_op jit(solution)/shard_map/layer/pallas_call | solution.py:299
  106.6 3.5 %collective-permute-start.3 = (bf16[96,3,128]{2,1,0:T(4,128)(2,1)}, bf16[96,3,128]{2,1,0:T(4,128)(2,1)S(1)}, u32[]{:S(2)}, u32[]{:S(2)}) collective-permute-start(bf16[96,3,128]{2,1,0:T(4,128)(2,1)} %get-tuple-element.20), channel_id=1, source_target_pairs={{0,1},{1,2},{2,3},{4,5},{5,6},{6,7},{8,9},{9,10},{10,11},{12,13},{... | collective-permute-start | bytes 221192 | tf_op jit(solution)/shard_map/ppermute | solution.py:334
  110.1 1.5 collective-permute-start.4
  111.6 0.9 fusion.4
  112.6 4.2 %collective-permute-done.4.bot_ref = bf16[96,3,128]{2,1,0:T(4,128)(2,1)S(1)} collective-permute-done((bf16[96,3,128]{2,1,0:T(4,128)(2,1)}, bf16[96,3,128]{2,1,0:T(4,128)(2,1)S(1)}, u32[]{:S(2)}, u32[]{:S(2)}) %collective-permute-start.4) | collective-permute-done | bytes 73760 | tf_op jit(solution)/shard_map/ppermute | solution.py:335
  117.5 36.8 %layer.3 = (bf16[128,12288]{1,0:T(8,128)(2,1)}, bf16[96,128,128]{2,1,0:T(8,128)(2,1)}, bf16[96,3,128]{2,1,0:T(4,128)(2,1)}, bf16[96,3,128]{2,1,0:T(4,128)(2,1)}) custom-call(bf16[96,128,128]{2,1,0:T(8,128)(2,1)} %get-tuple-element.19.z_ref, bf16[96,3,128]{2,1,0:T(4,128)(2,1)} %copy-done.4, bf16[96,3,128]{2,1,0:T(4,128)(2,1)} %copy-done.6, ...), custom_call_target="tpu_custom_call" | custom-call | tf_op jit(solution)/shard_map/layer/pallas_call | solution.py:299
  (45 shorter events, 11.6 us)
Async XLA Ops:
  0.0 22.2 %copy-start = (bf16[2,8,32,16]{2,3,1,0:T(8,128)(2,1)S(1)}, bf16[2,8,32,16]{2,3,1,0:T(8,128)(2,1)}, u32[]{:S(2)}) copy-start(bf16[2,8,32,16]{2,3,1,0:T(8,128)(2,1)} %param.11) | copy-start | bytes 49156
  12.5 4.6 %collective-permute-start = (bf16[32,16,16,128]{3,2,1,0:T(8,128)(2,1)}, bf16[32,16,16,128]{3,2,1,0:T(8,128)(2,1)}, u32[]{:S(2)}, u32[]{:S(2)}) collective-permute-start(bf16[32,16,16,128]{3,2,1,0:T(8,128)(2,1)} %get-tuple-element.15), channel_id=1, source_target_pairs={{0,16},{16,0},{1,17},{17,1},{2,18},{18,2},{3,19},{19,3},{4,20},{20... | collective-permute-start | bytes 6291464 | tf_op jit(solution)/shard_map/ppermute | solution.py:353
  17.1 32.9 %all-to-all-start = ((bf16[32,16,16,128]{3,2,1,0:T(8,128)(2,1)}), bf16[32,16,16,128]{3,2,1,0:T(8,128)(2,1)S(1)}, u32[]{:S(2)}, u32[]{:S(2)}) async-start(bf16[32,16,16,128]{3,2,1,0:T(8,128)(2,1)} %collective-permute-done), calls=%async_computation | async-start | bytes 4194304 | tf_op jit(solution)/shard_map/all_to_all | solution.py:354
  25.3 7.7 %copy-start.7 = (f32[3,7,7,192]{3,2,1,0:T(8,128)S(1)}, f32[3,7,7,192]{3,2,1,0:T(8,128)}, u32[]{:S(2)}) copy-start(f32[3,7,7,192]{3,2,1,0:T(8,128)} %param.12) | copy-start | bytes 338692
  30.4 7.6 %copy-start.8 = (f32[3,192]{1,0:T(4,128)S(1)}, f32[3,192]{1,0:T(4,128)}, u32[]{:S(2)}) copy-start(f32[3,192]{1,0:T(4,128)} %param.13) | copy-start | bytes 6916
  50.0 13.7 %copy-start.2 = (bf16[1,768,192]{2,1,0:T(8,128)(2,1)S(1)}, bf16[1,768,192]{2,1,0:T(8,128)(2,1)}, u32[]{:S(2)}) copy-start(bf16[1,768,192]{2,1,0:T(8,128)(2,1)} %copy.18) | copy-start | bytes 884740
  50.0 1.3 copy-start.1
  59.0 6.0 %collective-permute-start.1 = (bf16[96,3,128]{2,1,0:T(4,128)(2,1)}, bf16[96,3,128]{2,1,0:T(4,128)(2,1)S(1)}, u32[]{:S(2)}, u32[]{:S(2)}) collective-permute-start(bf16[96,3,128]{2,1,0:T(4,128)(2,1)} %get-tuple-element.17), channel_id=1, source_target_pairs={{0,1},{1,2},{2,3},{4,5},{5,6},{6,7},{8,9},{9,10},{10,11},{12,13},{... | collective-permute-start | bytes 221192 | tf_op jit(solution)/shard_map/ppermute | solution.py:334
  62.4 6.7 %collective-permute-start.2 = (bf16[96,3,128]{2,1,0:T(4,128)(2,1)}, bf16[96,3,128]{2,1,0:T(4,128)(2,1)S(1)}, u32[]{:S(2)}, u32[]{:S(2)}) collective-permute-start(bf16[96,3,128]{2,1,0:T(4,128)(2,1)} %get-tuple-element.18), channel_id=1, source_target_pairs={{1,0},{2,1},{3,2},{5,4},{6,5},{7,6},{9,8},{10,9},{11,10},{13,12},{... | collective-permute-start | bytes 221192 | tf_op jit(solution)/shard_map/ppermute | solution.py:335
  65.0 4.2 %copy-start.3 = (bf16[96,3,128]{2,1,0:T(4,128)(2,1)}, bf16[96,3,128]{2,1,0:T(4,128)(2,1)S(1)}, u32[]{:S(2)}) copy-start(bf16[96,3,128]{2,1,0:T(4,128)(2,1)S(1)} %collective-permute-done.1.top_ref) | copy-start | bytes 221188
  69.1 0.7 copy-start.5
  106.6 6.0 %collective-permute-start.3 = (bf16[96,3,128]{2,1,0:T(4,128)(2,1)}, bf16[96,3,128]{2,1,0:T(4,128)(2,1)S(1)}, u32[]{:S(2)}, u32[]{:S(2)}) collective-permute-start(bf16[96,3,128]{2,1,0:T(4,128)(2,1)} %get-tuple-element.20), channel_id=1, source_target_pairs={{0,1},{1,2},{2,3},{4,5},{5,6},{6,7},{8,9},{9,10},{10,11},{12,13},{... | collective-permute-start | bytes 221192 | tf_op jit(solution)/shard_map/ppermute | solution.py:334
  110.1 6.7 %collective-permute-start.4 = (bf16[96,3,128]{2,1,0:T(4,128)(2,1)}, bf16[96,3,128]{2,1,0:T(4,128)(2,1)S(1)}, u32[]{:S(2)}, u32[]{:S(2)}) collective-permute-start(bf16[96,3,128]{2,1,0:T(4,128)(2,1)} %get-tuple-element.21), channel_id=1, source_target_pairs={{1,0},{2,1},{3,2},{5,4},{6,5},{7,6},{9,8},{10,9},{11,10},{13,12},{... | collective-permute-start | bytes 221192 | tf_op jit(solution)/shard_map/ppermute | solution.py:335
  112.6 4.2 %copy-start.4 = (bf16[96,3,128]{2,1,0:T(4,128)(2,1)}, bf16[96,3,128]{2,1,0:T(4,128)(2,1)S(1)}, u32[]{:S(2)}) copy-start(bf16[96,3,128]{2,1,0:T(4,128)(2,1)S(1)} %collective-permute-done.3.top_ref) | copy-start | bytes 221188
  116.8 0.7 copy-start.6
where the time goes:
time: 155 us; the launch traced here: 154 us
  Pallas kernels  93.2 us (60%)
  local copies, waits for them, and re-layouts  30.9 us (20%)
  starting transfers between devices  15.2 us (10%)
  waiting for transfers between devices  12.7 us (8%)
    pallas_call x2, Pallas kernels, layer(): pl.pallas_call(layer_kernel, out_shape=(jax.ShapeDtypeStruct((rows, nj *...  73.7 us
    pallas_call x1, Pallas kernels, pack(): pl.pallas_call(pack_kernel, out_shape=(jax.ShapeDtypeStruct((12 * nj, row...  11.9 us
    broadcast_in_dim x5, local copies, waits for them, and re-layouts, mix_prep(): jnp.where(eye, parts, jnp.zeros((), w.dtype)).reshape(groups, 2 * LN, LN)  8.72 us
    ppermute x2, waiting for transfers between devices, halo(): lax.ppermute(top, 'row', [(i + 1, i) for i in range(n - 1)])  8.36 us
    pallas_call x1, Pallas kernels, mix(): pl.pallas_call(mix_kernel, out_shape=(jax.ShapeDtypeStruct(z.shape, jnp.b...  7.65 us
    ppermute x2, starting transfers between devices, halo(): lax.ppermute(bot, 'row', [(i, i + 1) for i in range(n - 1)])  6.9 us
    all_to_all x1, starting transfers between devices, on_device(): lax.all_to_all(crossed, 'tile', split_axis=0, concat_axis=0, tiled=True)  5.08 us
    ppermute x1, waiting for transfers between devices, on_device(): crossed = lax.ppermute(outgoing, 'comp', [(0, 1), (1, 0)])  4.13 us
  transfers between devices with their start and end apart: 6, of which 5 were waited for; matrix products, arithmetic and copies ran while one was open for 19% of the time, Pallas kernels for 0%

commit v1 on v0

v1 whole, which is shorter than its diff:
```python
import functools
import jax
import jax.numpy as jnp
from jax import lax
from jax.experimental import pallas as pl
from jax.experimental.pallas import tpu as pltpu
from jax.sharding import PartitionSpec as P

VM = pltpu.VMEM
PC = 8
LG = 16
LN = 128
bf, f32 = jnp.bfloat16, jnp.float32
PARAMS = pltpu.CompilerParams(vmem_limit_bytes=56 * 2**20)


def lane_bit(shape, bit):
    return (lax.broadcasted_iota(jnp.int32, shape, 1) & bit) == 0


def lroll(x, shift):
    return pltpu.roll(x, shift % LN, 1)


def swap_stage(a, b, bit, m):
    return jnp.where(m, a, lroll(b, bit)), jnp.where(m, lroll(a, -bit), b)


def to_patch(v):
    half = len(v) // 2
    shape = v[0].shape
    m64, m32, m16 = (lane_bit(shape, b) for b in (64, 32, 16))
    per = 3
    u = {}
    for j in range(4):
        for t in range(per):
            q = per * j + t
            a, b = v[q // 2], v[q // 2 + half]
            if q % 2 == 0:
                u[j, t] = jnp.where(m64, a, lroll(b, 64))
            else:
                u[j, t] = jnp.where(m64, lroll(a, 64), b)
    out = []
    for t in range(per):
        a0, b0 = swap_stage(u[0, t], u[2, t], 32, m32)
        a1, b1 = swap_stage(u[1, t], u[3, t], 32, m32)
        out += swap_stage(a0, a1, 16, m16)
        out += swap_stage(b0, b1, 16, m16)
    return out


def from_patch(z):
    half = len(z) // 2
    shape = z[0].shape
    m64, m32, m16 = (lane_bit(shape, b) for b in (64, 32, 16))
    per = len(z) // 4
    u = {}
    for t in range(per):
        a0, a1 = swap_stage(z[4 * t], z[4 * t + 1], 16, m16)
        b0, b1 = swap_stage(z[4 * t + 2], z[4 * t + 3], 16, m16)
        u[0, t], u[2, t] = swap_stage(a0, b0, 32, m32)
        u[1, t], u[3, t] = swap_stage(a1, b1, 32, m32)
    lo, hi = {}, {}
    for j in range(4):
        for t in range(per):
            q = per * j + t
            lo[q] = u[j, t]
            hi[q] = u[j, t]
    v = []
    for n in range(half):
        e, o = u[divmod(2 * n, per)], u[divmod(2 * n + 1, per)]
        v.append(jnp.where(m64, e, lroll(o, 64)))
    for n in range(half):
        e, o = u[divmod(2 * n, per)], u[divmod(2 * n + 1, per)]
        v.append(jnp.where(m64, lroll(e, 64), o))
    return v


def gelu(h):
    c = 0.7978845608028654
    inside = h * (jnp.asarray(2 * c, bf) + jnp.asarray(8 * 0.044715 * c, bf) * (h * h))
    return h + h * jnp.tanh(inside)


def part(i, n):
    if n & (n - 1) == 0:
        return lax.shift_right_logical(i, n.bit_length() - 1), i & (n - 1)
    return lax.div(i, n), lax.rem(i, n)


def pack_kernel(pairs, place, x_hbm, z_hbm, top_ref, bot_ref, *rest, mixed, tiles):
    outs = rest[:tiles]
    xs, zs, send, order, xsem, zsem, ssem = rest[tiles:]
    ng, nj, rows, _ = zs.shape
    per = x_hbm.shape[1] // nj
    hold = send.shape[0]
    peer = hold // tiles
    of_tile = pairs.shape[1] // tiles
    ncb = nj // 2
    section, tile, band_at = place[0], place[1], place[2]

    def xcopy(j):
        return pltpu.make_async_copy(x_hbm.at[:, pl.ds(pl.multiple_of(j * per, LN), per)], xs.at[j], xsem.at[j])

    def zcopy(j):
        return pltpu.make_async_copy(zs.at[:, j], z_hbm.at[:, j], zsem.at[j])

    for j in range(nj):
        xcopy(j).start()

    @pl.loop(0, tiles)
    def _(q):
        first = lax.bitwise_xor(q, tile) * peer

        def one(slot, rank):
            src_tile, src = part(pairs[1 - section, q * of_tile + band_at * hold + slot], of_tile)
            mine = src_tile == tile
            order[jnp.where(mine, first + rank, hold)] = src - band_at * hold
            return rank + mine.astype(jnp.int32)
        lax.fori_loop(0, hold, one, jnp.int32(0), unroll=8)

    @pl.loop(0, nj)
    def _(j):
        xcopy(j).wait()
        zz = to_patch([xs[j, :, n * LN:(n + 1) * LN] for n in range(12)])
        for g in range(ng):
            zs[g, j] = zz[g]
        for g in range(mixed, ng):
            for r in range(3):
                top_ref[r, pl.ds((g - mixed) * nj + j, 1), :] = zz[g][r:r + 1].astype(f32)
                bot_ref[r, pl.ds((g - mixed) * nj + j, 1), :] = zz[g][rows - 3 + r:rows - 2 + r].astype(f32)
        zcopy(j).start()

    @pl.loop(0, hold)
    def _(at):
        up, side = part(order[at], ncb)
        row = pl.ds(pl.multiple_of(up * 16, 16), 16)
        for g in range(mixed):
            for h in range(2):
                send[at, 2 * g + h] = zs[g, 2 * side + h, row, :]

    copies = [pltpu.make_async_copy(send.at[pl.ds(d * peer, peer)], outs[d], ssem.at[d]) for d in range(tiles)]
    for c in copies:
        c.start()
    for c in copies:
        c.wait()
    for j in range(nj):
        zcopy(j).wait()


def pack(pairs, place, x, tiles, mixed, ng):
    rows, width = x.shape
    per = ng * LG * PC
    nj = width // per
    hold = rows // 16 * (nj // 2)
    vm = pl.BlockSpec(memory_space=VM)
    sm = pl.BlockSpec(memory_space=pltpu.SMEM)
    hbm = pl.BlockSpec(memory_space=pl.ANY)
    edge = jax.ShapeDtypeStruct((3, (ng - mixed) * nj, LN), f32)
    return pl.pallas_call(
        functools.partial(pack_kernel, mixed=mixed, tiles=tiles),
        out_shape=(jax.ShapeDtypeStruct((ng, nj, rows, LN), bf), edge, edge)
        + (jax.ShapeDtypeStruct((hold // tiles, 2 * mixed, 16, LN), bf),) * tiles,
        in_specs=[sm, sm, hbm],
        out_specs=(hbm, vm, vm) + (hbm,) * tiles,
        scratch_shapes=[
            VM((nj, rows, per), bf),
            VM((ng, nj, rows, LN), bf),
            VM((hold, 2 * mixed, 16, LN), bf),
            pltpu.SMEM((hold + 1,), jnp.int32),
            pltpu.SemaphoreType.DMA((nj,)),
            pltpu.SemaphoreType.DMA((nj,)),
            pltpu.SemaphoreType.DMA((tiles,)),
        ],
        compiler_params=PARAMS,
        name="pack",
    )(pairs, place, x)


def mix_kernel(pairs, place, z_hbm, etop_ref, ebot_ref, w_ref, *rest, mixed, tiles):
    gots = rest[:tiles]
    out_hbm, otop_ref, obot_ref, zs, zp, got, wm, top_ref, bot_ref, count, zsem, gsem, osem = rest[tiles:]
    _, nj, rows, _ = zs.shape
    hold = got.shape[0]
    peer = hold // tiles
    of_tile = pairs.shape[1] // tiles
    ncb = nj // 2
    section, tile, band_at = place[0], place[1], place[2]

    gcopy = [pltpu.make_async_copy(gots[d], got.at[pl.ds(d * peer, peer)], gsem.at[d]) for d in range(tiles)]
    for c in gcopy:
        c.start()

    def zcopy(g):
        return pltpu.make_async_copy(z_hbm.at[g], zs.at[g], zsem.at[g])

    def ocopy(g):
        return pltpu.make_async_copy(zs.at[g], out_hbm.at[g], osem.at[g])

    for g in range(mixed):
        zcopy(g).start()
    block = lax.broadcasted_iota(jnp.int32, (LG, LN), 1) // LG

    @pl.loop(0, mixed)
    def _(g):
        for h in range(2):
            w = w_ref[g, h * LG:(h + 1) * LG, :]
            for c in range(PC):
                at = h * LN + c * LG
                wm[g, at:at + LG] = jnp.where(block == c, w, 0.0).astype(bf)
    for q in range(tiles):
        count[q] = 0
    for c in gcopy:
        c.wait()

    @pl.loop(0, hold)
    def _(slot):
        q, _ = part(pairs[section, tile * of_tile + band_at * hold + slot], of_tile)
        rank = count[q]
        count[q] = rank + 1
        at = lax.bitwise_xor(q, tile) * peer + rank
        up, side = part(slot, ncb)
        row = pl.ds(pl.multiple_of(up * 16, 16), 16)
        for g in range(mixed):
            for h in range(2):
                zp[g, 2 * side + h, row, :] = got[at, 2 * g + h]

    @pl.loop(0, mixed)
    def _(g):
        zcopy(g).wait()
        own = zs[g].reshape(nj * rows, LN)
        both = jnp.concatenate([own, zp[g].reshape(nj * rows, LN)], 1)
        new = own.astype(f32) + jnp.dot(both, wm[g], preferred_element_type=f32)
        new = new.astype(bf).reshape(nj, rows, LN)
        zs[g] = new
        ocopy(g).start()
        for j in range(nj):
            for r in range(3):
                top_ref[r, pl.ds(g * nj + j, 1), :] = new[j, r:r + 1].astype(f32)
                bot_ref[r, pl.ds(g * nj + j, 1), :] = new[j, rows - 3 + r:rows - 2 + r].astype(f32)

    top_ref[:, mixed * nj:, :] = etop_ref[...]
    bot_ref[:, mixed * nj:, :] = ebot_ref[...]
    otop_ref[...] = top_ref[...].astype(bf)
    obot_ref[...] = bot_ref[...].astype(bf)
    for g in range(mixed):
        ocopy(g).wait()


def mix(pairs, place, z, etop, ebot, w, gots):
    ng, nj, rows, _ = z.shape
    mixed = w.shape[0]
    tiles = len(gots)
    hold = gots[0].shape[0] * tiles
    vm = pl.BlockSpec(memory_space=VM)
    sm = pl.BlockSpec(memory_space=pltpu.SMEM)
    hbm = pl.BlockSpec(memory_space=pl.ANY)
    edge = jax.ShapeDtypeStruct((3, ng * nj, LN), bf)
    return pl.pallas_call(
        functools.partial(mix_kernel, mixed=mixed, tiles=tiles),
        out_shape=(jax.ShapeDtypeStruct((mixed, nj, rows, LN), bf), edge, edge),
        in_specs=[sm, sm, hbm, vm, vm, vm] + [hbm] * tiles,
        out_specs=(hbm, vm, vm),
        scratch_shapes=[
            VM((mixed, nj, rows, LN), bf),
            VM((mixed, nj, rows, LN), bf),
            VM((hold,) + gots[0].shape[1:], bf),
            VM((mixed, 2 * LN, LN), bf),
            VM(edge.shape, f32),
            VM(edge.shape, f32),
            pltpu.SMEM((tiles,), jnp.int32),
            pltpu.SemaphoreType.DMA((mixed,)),
            pltpu.SemaphoreType.DMA((tiles,)),
            pltpu.SemaphoreType.DMA((mixed,)),
        ],
        compiler_params=PARAMS,
        name="mix",
    )(pairs, place, z, etop, ebot, w, *gots)


def band_kernel(e_ref, w_ref):
    delta = lax.broadcasted_iota(jnp.int32, (LG, LN), 0) == lax.broadcasted_iota(jnp.int32, (LG, LN), 1) % LG
    chunk = lax.broadcasted_iota(jnp.int32, (8, LN), 1) // LG
    zero = jnp.zeros((LG, LN), bf)

    @pl.loop(0, e_ref.shape[0])
    def _(g):
        e = e_ref[g]
        w_ref[g, 0:256] = jnp.zeros((256, LN), bf)
        w_ref[g, 2048:2304] = jnp.zeros((256, LN), bf)
        for pos, jr in enumerate(list(range(12)) + list(range(-4, 0))):
            s = jr - 3
            r = lroll(e, s * LG)
            r = jnp.where((chunk >= s) & (chunk < 8 + s), r, 0.0)
            for k in range(7):
                row = (k + 1) * 256 + pos * LG
                if jr in (-4, 11):
                    w_ref[g, row:row + LG] = zero
                else:
                    w_ref[g, row:row + LG] = jnp.where(delta, jnp.broadcast_to(r[k:k + 1], (LG, LN)), 0.0).astype(bf)


def band(e):
    vm = pl.BlockSpec(memory_space=VM)
    n = e.shape[0]
    return pl.pallas_call(
        band_kernel,
        out_shape=jax.ShapeDtypeStruct((n, 2304, LN), bf),
        in_specs=[vm], out_specs=vm,
        compiler_params=PARAMS,
        name="band",
    )(e)


def block_kernel(*refs, parts, want_out, want_z):
    z_hbm, rest = refs[:parts], list(refs[parts:])
    top_ref, bot_ref, fac_ref, w_hbm, gain_ref, wi_hbm, woe_hbm, woo_hbm = rest[:8]
    rest = rest[8:]
    out_hbm = rest.pop(0) if want_out else None
    outz_hbm, otop_ref, obot_ref = (rest.pop(0) for _ in range(3)) if want_z else (None,) * 3
    zs, zf, lhs, wt, spr, ssum, nrm, xe, xo, upd, out, outz, wi_ref, woe_ref, woo_ref, tops, bots, zsem, wsem, osem, msem = rest
    ng, nj, rows, _ = zs.shape
    hr = rows // 2
    pad = 8
    count = ng * LG
    npair = xe.shape[0] // rows
    per = 3 * npair * LN

    def zcopy(g):
        src = z_hbm[0] if isinstance(g, int) and g < z_hbm[0].shape[0] else z_hbm[-1]
        return pltpu.make_async_copy(src.at[g], zs.at[g], zsem.at[g])

    def wcopy(g):
        return pltpu.make_async_copy(w_hbm.at[g], wt.at[g], wsem.at[g])

    for g in range(ng):
        zcopy(g).start()
        wcopy(g).start()
    weights = [pltpu.make_async_copy(a, b, msem.at[i])
               for i, (a, b) in enumerate(((wi_hbm, wi_ref), (woe_hbm, woe_ref), (woo_hbm, woo_ref)))]
    for c in weights:
        c.start()
    ssum[...] = jnp.zeros_like(ssum)

    @pl.loop(0, ng)
    def _(g):
        zcopy(g).wait()
        wcopy(g).wait()

        for j in range(nj):
            zf[j, pl.ds(pad, rows), :] = zs[g, j].astype(f32)
        for r in range(3):
            hs = pl.ds(pl.multiple_of(g * nj, nj), nj)
            zf[:, pad - 3 + r, :] = top_ref[r, hs, :].astype(f32)
            zf[:, pad + rows + r, :] = bot_ref[r, hs, :].astype(f32)
        m64 = lane_bit((hr, LN), 64)
        zero = jnp.zeros((hr, LN), bf)
        for a in range(8):
            v = [zf[j, pl.ds(pad - 3 + a, hr, stride=2), :].astype(bf) for j in range(nj)]
            for j in range(nj):
                nxt = v[j + 1] if j + 1 < nj else zero
                prv = v[j - 1] if j > 0 else zero
                lhs[j * hr:(j + 1) * hr, a * 256:a * 256 + LN] = v[j]
                lhs[j * hr:(j + 1) * hr, a * 256 + LN:a * 256 + 256] = jnp.where(m64, nxt, prv)

        rhs = jnp.concatenate([wt[g, 256:2304], wt[g, 0:2048]], 1)
        sp = jnp.dot(lhs[...], rhs, preferred_element_type=f32)
        spr[g] = sp
        ssum[...] += sp

    for c in weights:
        c.wait()
    ones = (lax.broadcasted_iota(jnp.int32, (256, 256), 0) // LG == lax.broadcasted_iota(jnp.int32, (256, 256), 1) // LG)
    ones = ones.astype(f32).astype(bf)

    def lane_mean(s):
        hi = s.astype(bf)
        lo = (s - hi.astype(f32)).astype(bf)
        return (jnp.dot(hi, ones, preferred_element_type=f32) + jnp.dot(lo, ones, preferred_element_type=f32)) * (1.0 / count)

    nrm[...] = lane_mean(ssum[...])

    @pl.loop(0, nj)
    def _(j):
        js = pl.ds(pl.multiple_of(j * hr, hr), hr)
        mean = nrm[js, :]
        q = jnp.zeros((hr, 256), f32)
        for g in range(ng):
            c = spr[g, js, :] - mean
            q = q + c * c
        ssum[js, :] = q
    ssum[...] = lax.rsqrt(lane_mean(ssum[...]) + 1e-06)

    def outcopy(j):
        ls = pl.ds(pl.multiple_of(j * per, LN), per)
        cs = []
        if want_out:
            cs.append(pltpu.make_async_copy(out.at[j], out_hbm.at[:, ls], osem.at[0, j]))
        if want_z:
            cs.append(pltpu.make_async_copy(outz.at[:, j], outz_hbm.at[:, j], osem.at[1, j]))
        return cs

    @pl.loop(0, nj)
    def _(j):
        js = pl.ds(pl.multiple_of(j * hr, hr), hr)

        mean, rstd = nrm[js, :], ssum[js, :]
        zz = [((spr[g, js, :] - mean) * rstd * gain_ref[g:g + 1, :]).astype(bf) for g in range(ng)]
        for p in range(2):
            nat = from_patch([t[:, p * LN:(p + 1) * LN] for t in zz])
            for i in range(npair):
                rs = slice(i * rows + p * hr, i * rows + (p + 1) * hr)
                xe[rs, :LN] = nat[3 * i]
                xe[rs, LN:] = nat[3 * i + 1]
                xo[rs, :LN] = nat[3 * i + 1]
                xo[rs, LN:] = nat[3 * i + 2]

        def mlp(x, wi, wo):
            h = gelu(jnp.dot(x, wi, preferred_element_type=f32).astype(bf))
            return jnp.dot(h, wo, preferred_element_type=f32)
        ue = mlp(xe[...], wi_ref[64:, :], woe_ref[...])
        uo = mlp(xo[...], wi_ref[:256, :], woo_ref[...])
        for i in range(npair):
            e = ue[i * rows:(i + 1) * rows]
            o = uo[i * rows:(i + 1) * rows]
            for t, val in enumerate((e[:, :LN], e[:, LN:] + o[:, :LN], o[:, LN:])):
                for p in range(2):
                    upd[3 * i + t, pl.ds(p, hr, stride=2), :] = val[p * hr:(p + 1) * hr]

        fac = fac_ref[0, 0]
        own = from_patch([zs[g, j] for g in range(ng)])
        res = []
        for n in range(3 * npair):
            y = (own[n].astype(f32) + fac * upd[n]).astype(bf)
            if want_out:
                out[j, :, n * LN:(n + 1) * LN] = y
            res.append(y)
        if want_z:
            for g, zz in enumerate(to_patch(res)):
                outz[g, j] = zz
                for r in range(3):
                    tops[r, pl.ds(g * nj + j, 1), :] = zz[r:r + 1].astype(f32)
                    bots[r, pl.ds(g * nj + j, 1), :] = zz[rows - 3 + r:rows - 2 + r].astype(f32)
        for c in outcopy(j):
            c.start()

    if want_z:
        otop_ref[...] = tops[...].astype(bf)
        obot_ref[...] = bots[...].astype(bf)

    @pl.loop(0, nj)
    def _(j):
        for c in outcopy(j):
            c.wait()


def block(zs, top, bot, fac, w, gain, wi, woe, woo, want_out=True, want_z=True):
    ng, nj, rows, _ = zs[-1].shape
    hr = rows // 2
    per = ng * LG * PC
    vm = pl.BlockSpec(memory_space=VM)
    hbm = pl.BlockSpec(memory_space=pl.ANY)
    shapes = []
    if want_out:
        shapes.append(jax.ShapeDtypeStruct((rows, nj * per), bf))
    if want_z:
        edge = jax.ShapeDtypeStruct(top.shape, bf)
        shapes += [jax.ShapeDtypeStruct((ng, nj, rows, LN), bf), edge, edge]
    return pl.pallas_call(
        functools.partial(block_kernel, parts=len(zs), want_out=want_out, want_z=want_z),
        out_shape=tuple(shapes),
        in_specs=[hbm] * len(zs) + [vm, vm, pl.BlockSpec(memory_space=pltpu.SMEM), hbm, vm, hbm, hbm, hbm],
        out_specs=((hbm,) if want_out else ()) + ((hbm, vm, vm) if want_z else ()),
        scratch_shapes=[
            VM((ng, nj, rows, LN), bf),
            VM((nj, rows + 16, LN), f32),
            VM((nj * hr, 2048), bf),
            VM((ng, 2304, LN), bf),
            VM((ng, nj * hr, 256), f32),
            VM((nj * hr, 256), f32),
            VM((nj * hr, 256), f32),
            VM((4 * rows, 256), bf), VM((4 * rows, 256), bf),
            VM((12, rows, LN), f32),
            VM((nj, rows, per), bf) if want_out else VM((8, LN), bf),
            VM((ng, nj, rows, LN), bf) if want_z else VM((8, LN), bf),
            VM(wi.shape, bf),
            VM(woe.shape, bf),
            VM(woo.shape, bf),
            VM(top.shape, f32),
            VM(top.shape, f32),
            pltpu.SemaphoreType.DMA((ng,)),
            pltpu.SemaphoreType.DMA((ng,)),
            pltpu.SemaphoreType.DMA((2, nj)),
            pltpu.SemaphoreType.DMA((3,)),
        ],
        compiler_params=PARAMS,
        name="block",
    )(*zs, top, bot, fac, w, gain, wi, woe, woo)


def prep_all(depth, gain, inner, outer):
    nl, c = gain.shape
    ng = c // LG
    e = jnp.pad(depth[:, :, ::-1, :], ((0, 0), (0, 1), (0, 1), (0, 0))).reshape(nl, 8, 8, ng, LG)
    e = e.transpose(0, 3, 1, 2, 4).reshape(nl, ng, 8, LN)
    gl = jnp.tile(gain.reshape(nl, ng, 1, LG), (1, 1, 16, 1)).reshape(nl, ng, 256)
    wi = jnp.pad(0.5 * inner, ((0, 0), (64, 64), (0, 0)))
    woe = jnp.pad(outer, ((0, 0), (0, 0), (0, 64)))
    woo = jnp.pad(outer, ((0, 0), (0, 0), (64, 0)))
    return e, gl, wi, woe, woo


def halo(top, bot):
    n = lax.axis_size("row")
    return (
        lax.ppermute(bot, "row", [(i, i + 1) for i in range(n - 1)]),
        lax.ppermute(top, "row", [(i + 1, i) for i in range(n - 1)]),
    )


def exchange(outs):
    n = len(outs)
    assert n & (n - 1) == 0
    return [
        lax.ppermute(o, ("comp", "tile"), [(s * n + t, (1 - s) * n + (t ^ d)) for s in range(2) for t in range(n)])
        for d, o in enumerate(outs)
    ]


def on_device(state, pairs, wet, mix_weight, depth_weight, norm_gain, inner_weight, outer_weight):
    assert state.shape[1] == 1
    section = lax.axis_index("comp")
    tiles = lax.axis_size("tile")
    place = jnp.stack([section, lax.axis_index("tile"), lax.axis_index("row")]).astype(jnp.int32)
    pick = lambda w, i: lax.dynamic_index_in_dim(w, i, 0, keepdims=False)
    z, etop, ebot, *outs = pack(pairs, place, state[0, 0], tiles, mix_weight.shape[1], norm_gain.shape[1] // LG)
    gots = exchange(outs)
    e, *weights = prep_all(depth_weight, norm_gain, inner_weight, outer_weight)
    which = jnp.where(section == 0, 0, 2)
    wmix = jnp.tile(pick(mix_weight, section).astype(f32), (1, 1, PC))
    wone, wtwo = band(pick(e, which)), band(e[1])
    zc, top, bot = mix(pairs, place, z, etop, ebot, wmix, gots)
    top, bot = halo(top, bot)
    factor = jnp.where(section == 0, 1.0, wet[0].astype(f32)).reshape(1, 1)
    _, z, top, bot = block([zc, z], top, bot, factor, wone, *(pick(w, which) for w in weights))
    top, bot = halo(top, bot)
    factor = jnp.where(section == 0, 1.0, 0.0).reshape(1, 1)
    out, = block([z], top, bot, factor, wtwo, *(w[1] for w in weights), want_z=False)
    return out[None, None]


def solution(mesh):
    return jax.shard_map(
        on_device,
        mesh=mesh,
        in_specs=(P("comp", "tile", "row", None), P(), P("tile"), P(), P(), P(), P(), P()),
        out_specs=P("comp", "tile", "row", None),
        check_vma=False,
    )
```

time: 155 us -> 124 us (0.80)
  local copies, waits for them, and re-layouts: 30.9 us -> 10.8 us
  Pallas kernels: 93.2 us -> 82.1 us
  waiting for transfers between devices: 12.7 us -> 15.5 us
    pallas_call x4 -> x6, Pallas kernels: 93.2 us -> 82.1 us  [the longest x2 55.1 us: block(): pl.pallas_call(functools.partial(block_kernel, parts=len(zs), want_out=wa...]
    broadcast_in_dim x5 -> x0, local copies, waits for them, and re-layouts: 8.72 us -> none  [mix_prep(): jnp.where(eye, parts, jnp.zeros((), w.dtype)).reshape(groups, 2 * LN, LN)]
    ppermute x1 -> x4, waiting for transfers between devices: 4.13 us -> 11 us  [exchange(): lax.ppermute(o, ('comp', 'tile'), [(s * n + t, (1 - s) * n + (t ^ d)) for...]
    pad x6 -> x1, local copies, waits for them, and re-layouts: 5.89 us -> 0.02 us  [prep_all(): jnp.pad(depth[:, :, ::-1, :], ((0, 0), (0, 1), (0, 1), (0, 0)))]
    all_to_all x1 -> x0, starting transfers between devices: 5.08 us -> none  [on_device(): lax.all_to_all(crossed, 'tile', split_axis=0, concat_axis=0, tiled=True)]
    ppermute x2, waiting for transfers between devices: 8.36 us -> 4.18 us  [halo(): lax.ppermute(top, 'row', [(i + 1, i) for i in range(n - 1)])]
    reshape x4 -> x2, local copies, waits for them, and re-layouts: 4.74 us -> 0.79 us  [the longest x1 0.45 us: prep_all(): jnp.pad(depth[:, :, ::-1, :], ((0, 0), (0, 1), (0, 1), (0, 0)))]
    ppermute x1 -> x4, starting transfers between devices: 0.45 us -> 4.34 us  [exchange(): lax.ppermute(o, ('comp', 'tile'), [(s * n + t, (1 - s) * n + (t ^ d)) for...]
  transfers between devices with their start and end apart: 6 -> 8, of which waited for: 5 -> 3; matrix products, arithmetic and copies ran while one was open for 19% -> 8% of each run, Pallas kernels for 0% -> 9%
where the time goes in v1:
time: 124 us
  Pallas kernels  82.1 us (66%)
  waiting for transfers between devices  15.5 us (12%)
  starting transfers between devices  13.9 us (11%)
  local copies, waits for them, and re-layouts  10.8 us (9%)
    pallas_call x2, Pallas kernels, block(): pl.pallas_call(functools.partial(block_kernel, parts=len(zs), want_out=wa...  55.1 us
    ppermute x4, waiting for transfers between devices, exchange(): lax.ppermute(o, ('comp', 'tile'), [(s * n + t, (1 - s) * n + (t ^ d)) for...  11 us
    pallas_call x2, Pallas kernels, band(): pl.pallas_call(band_kernel, out_shape=jax.ShapeDtypeStruct((n, 2304, LN),...  10.6 us
    pallas_call x1, Pallas kernels, pack(): pl.pallas_call(functools.partial(pack_kernel, mixed=mixed, tiles=tiles),...  8.89 us
    pallas_call x1, Pallas kernels, mix(): pl.pallas_call(functools.partial(mix_kernel, mixed=mixed, tiles=tiles), o...  7.5 us
    ppermute x2, starting transfers between devices, halo(): lax.ppermute(bot, 'row', [(i, i + 1) for i in range(n - 1)])  7 us
    ppermute x4, starting transfers between devices, exchange(): lax.ppermute(o, ('comp', 'tile'), [(s * n + t, (1 - s) * n + (t ^ d)) for...  4.34 us
    ppermute x2, waiting for transfers between devices, halo(): lax.ppermute(top, 'row', [(i + 1, i) for i in range(n - 1)])  4.18 us
  transfers between devices with their start and end apart: 8, of which 3 were waited for; matrix products, arithmetic and copies ran while one was open for 8% of the time, Pallas kernels for 9%

profile of v1, /device:TPU:0, one launch (start us, length us, event | category | flops | bytes accessed | tf_op | source)
XLA Modules:
  0.0 123.9 jit_solution(8380307315859891210)
XLA Ops:
  0.0 0.7 pad_add_fusion.place
  0.7 8.9 %pack.1 = (bf16[12,8,128,128]{3,2,1,0:T(8,128)(2,1)}, f32[3,32,128]{2,1,0:T(8,128)}, f32[3,32,128]{2,1,0:T(8,128)}, bf16[8,16,16,128]{3,2,1,0:T(8,128)(2,1)}, bf...) custom-call(s32[2,512]{1,0:T(2,128)} %pairs.3, ...), custom_call_target="tpu_custom_call" | custom-call | tf_op jit(solution)/shard_map/pack/pallas_call | solution.py:160
  10.1 2.6 %collective-permute-start.1 = (bf16[8,16,16,128]{3,2,1,0:T(8,128)(2,1)}, bf16[8,16,16,128]{3,2,1,0:T(8,128)(2,1)}, u32[]{:S(2)}, u32[]{:S(2)}) collective-permute-start(bf16[8,16,16,128]{3,2,1,0:T(8,128)(2,1)} %get-tuple-element.22), channel_id=1, source_target_pairs={{0,20},{4,16},{8,28},{12,24},{16,4},{20,0},{24,12},{28,8},{1,21},{... | collective-permute-start | bytes 1572872 | tf_op jit(solution)/shard_map/ppermute | solution.py:525
  12.7 1.2 collective-permute-start.2
  16.0 0.8 copy.17.w_ref
  16.8 1.5 %copy.19 = bf16[3,768,192]{2,1,0:T(8,128)(2,1)S(1)} copy(bf16[3,768,192]{1,2,0:T(8,128)(2,1)} %param.15) | data formatting | bytes 1769472 | tf_op args[7]
  18.7 0.6 dynamic-slice_bitcast_fusion.e_ref
  19.3 5.3 %band.2.refs_5_ = bf16[12,2304,128]{2,1,0:T(8,128)(2,1)} custom-call(f32[12,8,128]{2,1,0:T(8,128)} %dynamic-slice_bitcast_fusion.e_ref), custom_call_target="tpu_custom_call" | custom-call | tf_op jit(solution)/shard_map/band/pallas_call | solution.py:306
  24.7 1.1 fusion.1
  25.8 1.5 %fusion.5 = (bf16[768,256]{1,0:T(8,128)(2,1)}, bf16[768,256]{1,0:T(8,128)(2,1)}, bf16[768,256]{1,0:T(8,128)(2,1)}, bf16[768,256]{1,0:T(8,128)(2,1)}) fusion(bf16[3,768,192]{2,1,0:T(8,128)(2,1)S(1)} %copy.19, s32[]{:T(128)S(6)} %select_n.27), kind=kLoop, calls=%fused_computation.12 | loop fusion | bytes 2457604 | tf_op jit(solution)/shard_map/squeeze | solution.py:548
  27.3 11.0 %collective-permute-done.2.rest_2_ = bf16[8,16,16,128]{3,2,1,0:T(8,128)(2,1)} collective-permute-done((bf16[8,16,16,128]{3,2,1,0:T(8,128)(2,1)}, bf16[8,16,16,128]{3,2,1,0:T(8,128)(2,1)}, u32[]{:S(2)}, u32[]{:S(2)}) %collective-permute-start.2) | collective-permute-done | bytes 524320 | tf_op jit(solution)/shard_map/ppermute | solution.py:525
  38.2 7.5 %mix.1 = (bf16[8,8,128,128]{3,2,1,0:T(8,128)(2,1)}, bf16[3,96,128]{2,1,0:T(8,128)(2,1)}, bf16[3,96,128]{2,1,0:T(8,128)(2,1)}) custom-call(s32[2,512]{1,0:T(2,128)} %pairs.3, s32[3]{0:T(128)} %pad_add_fusion.place, bf16[12,8,128,128]{3,2,1,0:T(8,128)(2,1)} %get-tuple-element.18.z_hbm.refs_1_, f32[3,32,128]{2,1,0:T(8,128)} %get-tuple-element.19.etop_ref, ...), custom_call_target="tpu_custom_call" | custom-call | tf_op jit(solution)/shard_map/mix/pallas_call | solution.py:259
  45.7 3.5 %collective-permute-start.4 = (bf16[3,96,128]{2,1,0:T(8,128)(2,1)}, bf16[3,96,128]{2,1,0:T(8,128)(2,1)S(1)}, u32[]{:S(2)}, u32[]{:S(2)}) collective-permute-start(bf16[3,96,128]{2,1,0:T(8,128)(2,1)} %get-tuple-element.26), channel_id=1, source_target_pairs={{0,1},{1,2},{2,3},{4,5},{5,6},{6,7},{8,9},{9,10},{10,11},{12,13},{... | collective-permute-start | bytes 221192 | tf_op jit(solution)/shard_map/ppermute | solution.py:516
  49.2 1.3 %collective-permute-start.5 = (bf16[3,96,128]{2,1,0:T(8,128)(2,1)}, bf16[3,96,128]{2,1,0:T(8,128)(2,1)S(1)}, u32[]{:S(2)}, u32[]{:S(2)}) collective-permute-start(bf16[3,96,128]{2,1,0:T(8,128)(2,1)} %get-tuple-element.27), channel_id=1, source_target_pairs={{1,0},{2,1},{3,2},{5,4},{6,5},{7,6},{9,8},{10,9},{11,10},{13,12},{... | collective-permute-start | bytes 221192 | tf_op jit(solution)/shard_map/ppermute | solution.py:517
  50.5 0.6 dynamic-slice_bitcast_fusion.1.refs_6_
  51.5 4.2 %collective-permute-done.5.refs_3_ = bf16[3,96,128]{2,1,0:T(8,128)(2,1)S(1)} collective-permute-done((bf16[3,96,128]{2,1,0:T(8,128)(2,1)}, bf16[3,96,128]{2,1,0:T(8,128)(2,1)S(1)}, u32[]{:S(2)}, u32[]{:S(2)}) %collective-permute-start.5) | collective-permute-done | bytes 73760 | tf_op jit(solution)/shard_map/ppermute | solution.py:517
  55.7 0.6 copy-done.5
  56.3 29.4 %block.2 = (bf16[128,12288]{1,0:T(8,128)(2,1)}, bf16[12,8,128,128]{3,2,1,0:T(8,128)(2,1)}, bf16[3,96,128]{2,1,0:T(8,128)(2,1)}, bf16[3,96,128]{2,1,0:T(8,128)(2,1)}) custom-call(bf16[8,8,128,128]{3,2,1,0:T(8,128)(2,1)} %get-tuple-element.25.refs_0_, bf16[12,8,128,128]{3,2,1,0:T(8,128)(2,1)} %get-tuple-element.18.z_hbm.refs_1_, ...), custom_call_target="tpu_custom_call" | custom-call | tf_op jit(solution)/shard_map/block/pallas_call | solution.py:469
  85.7 3.5 %collective-permute-start.6 = (bf16[3,96,128]{2,1,0:T(8,128)(2,1)}, bf16[3,96,128]{2,1,0:T(8,128)(2,1)S(1)}, u32[]{:S(2)}, u32[]{:S(2)}) collective-permute-start(bf16[3,96,128]{2,1,0:T(8,128)(2,1)} %get-tuple-element.29), channel_id=1, source_target_pairs={{0,1},{1,2},{2,3},{4,5},{5,6},{6,7},{8,9},{9,10},{10,11},{12,13},{... | collective-permute-start | bytes 221192 | tf_op jit(solution)/shard_map/ppermute | solution.py:516
  89.3 1.3 %collective-permute-start.7 = (bf16[3,96,128]{2,1,0:T(8,128)(2,1)}, bf16[3,96,128]{2,1,0:T(8,128)(2,1)S(1)}, u32[]{:S(2)}, u32[]{:S(2)}) collective-permute-start(bf16[3,96,128]{2,1,0:T(8,128)(2,1)} %get-tuple-element.30), channel_id=1, source_target_pairs={{1,0},{2,1},{3,2},{5,4},{6,5},{7,6},{9,8},{10,9},{11,10},{13,12},{... | collective-permute-start | bytes 221192 | tf_op jit(solution)/shard_map/ppermute | solution.py:517
  90.7 0.7 tile.28.refs_5_
  91.5 0.8 squeeze.44.e_ref
  92.3 5.2 %band.3.refs_4_ = bf16[12,2304,128]{2,1,0:T(8,128)(2,1)} custom-call(f32[12,8,128]{2,1,0:T(8,128)} %squeeze.44.e_ref), custom_call_target="tpu_custom_call" | custom-call | tf_op jit(solution)/shard_map/band/pallas_call | solution.py:306
  98.2 25.7 %block.3 = bf16[128,12288]{1,0:T(8,128)(2,1)} custom-call(bf16[12,8,128,128]{3,2,1,0:T(8,128)(2,1)} %get-tuple-element.28.refs_0_, bf16[3,96,128]{2,1,0:T(8,128)(2,1)} %copy-done.2, bf16[3,96,128]{2,1,0:T(8,128)(2,1)} %copy-done.3, f32[1,1]{1,0:T(1,128)} %bitcast.14.refs_3_, bf16[12,2304,128]{2,1,0:T(8,128)(2,1)} %band.3.refs_4_, f32[12,256]{1,0:T(8,128)} %tile.28.refs_5_, ...), custom_call_target="tpu_custom_call" | custom-call | tf_op jit(solution)/shard_map/block/pallas_call | solution.py:469
  (39 shorter events, 3.6 us)
Async XLA Ops:
  0.7 13.2 %copy-start.1 = (f32[3,7,7,192]{3,2,1,0:T(8,128)S(1)}, f32[3,7,7,192]{3,2,1,0:T(8,128)}, u32[]{:S(2)}) copy-start(f32[3,7,7,192]{3,2,1,0:T(8,128)} %param.12) | copy-start | bytes 338692
  9.6 17.7 %collective-permute-start = (bf16[8,16,16,128]{3,2,1,0:T(8,128)(2,1)}, bf16[8,16,16,128]{3,2,1,0:T(8,128)(2,1)}, u32[]{:S(2)}, u32[]{:S(2)}) collective-permute-start(bf16[8,16,16,128]{3,2,1,0:T(8,128)(2,1)} %get-tuple-element.21), channel_id=1, source_target_pairs={{0,16},{4,20},{8,24},{12,28},{16,0},{20,4},{24,8},{28,12},{1,17},{... | collective-permute-start | bytes 1572872 | tf_op jit(solution)/shard_map/ppermute | solution.py:525
  10.1 17.2 %collective-permute-start.1 = (bf16[8,16,16,128]{3,2,1,0:T(8,128)(2,1)}, bf16[8,16,16,128]{3,2,1,0:T(8,128)(2,1)}, u32[]{:S(2)}, u32[]{:S(2)}) collective-permute-start(bf16[8,16,16,128]{3,2,1,0:T(8,128)(2,1)} %get-tuple-element.22), channel_id=1, source_target_pairs={{0,20},{4,16},{8,28},{12,24},{16,4},{20,0},{24,12},{28,8},{1,21},{... | collective-permute-start | bytes 1572872 | tf_op jit(solution)/shard_map/ppermute | solution.py:525
  12.7 25.5 %collective-permute-start.2 = (bf16[8,16,16,128]{3,2,1,0:T(8,128)(2,1)}, bf16[8,16,16,128]{3,2,1,0:T(8,128)(2,1)}, u32[]{:S(2)}, u32[]{:S(2)}) collective-permute-start(bf16[8,16,16,128]{3,2,1,0:T(8,128)(2,1)} %get-tuple-element.23), channel_id=1, source_target_pairs={{0,24},{4,28},{8,16},{12,20},{16,8},{20,12},{24,0},{28,4},{1,25},{... | collective-permute-start | bytes 1572872 | tf_op jit(solution)/shard_map/ppermute | solution.py:525
  13.9 24.3 %collective-permute-start.3 = (bf16[8,16,16,128]{3,2,1,0:T(8,128)(2,1)}, bf16[8,16,16,128]{3,2,1,0:T(8,128)(2,1)}, u32[]{:S(2)}, u32[]{:S(2)}) collective-permute-start(bf16[8,16,16,128]{3,2,1,0:T(8,128)(2,1)} %get-tuple-element.24), channel_id=1, source_target_pairs={{0,28},{4,24},{8,20},{12,16},{16,12},{20,8},{24,4},{28,0},{1,29},{... | collective-permute-start | bytes 1572872 | tf_op jit(solution)/shard_map/ppermute | solution.py:525
  14.6 1.1 copy-start.7
  14.6 1.3 %copy-start.6 = (bf16[2,8,32,16]{2,3,1,0:T(8,128)(2,1)S(1)}, bf16[2,8,32,16]{2,3,1,0:T(8,128)(2,1)}, u32[]{:S(2)}) copy-start(bf16[2,8,32,16]{2,3,1,0:T(8,128)(2,1)} %param.11) | copy-start | bytes 49156
  19.3 5.3 %copy-start = (bf16[3,192,768]{2,1,0:T(8,128)(2,1)S(1)}, bf16[3,192,768]{2,1,0:T(8,128)(2,1)}, u32[]{:S(2)}) copy-start(bf16[3,192,768]{2,1,0:T(8,128)(2,1)} %param.14) | copy-start | bytes 2654212
  45.7 5.8 %collective-permute-start.4 = (bf16[3,96,128]{2,1,0:T(8,128)(2,1)}, bf16[3,96,128]{2,1,0:T(8,128)(2,1)S(1)}, u32[]{:S(2)}, u32[]{:S(2)}) collective-permute-start(bf16[3,96,128]{2,1,0:T(8,128)(2,1)} %get-tuple-element.26), channel_id=1, source_target_pairs={{0,1},{1,2},{2,3},{4,5},{5,6},{6,7},{8,9},{9,10},{10,11},{12,13},{... | collective-permute-start | bytes 221192 | tf_op jit(solution)/shard_map/ppermute | solution.py:516
  49.2 6.5 %collective-permute-start.5 = (bf16[3,96,128]{2,1,0:T(8,128)(2,1)}, bf16[3,96,128]{2,1,0:T(8,128)(2,1)S(1)}, u32[]{:S(2)}, u32[]{:S(2)}) collective-permute-start(bf16[3,96,128]{2,1,0:T(8,128)(2,1)} %get-tuple-element.27), channel_id=1, source_target_pairs={{1,0},{2,1},{3,2},{5,4},{6,5},{7,6},{9,8},{10,9},{11,10},{13,12},{... | collective-permute-start | bytes 221192 | tf_op jit(solution)/shard_map/ppermute | solution.py:517
  51.5 4.2 %copy-start.4 = (bf16[3,96,128]{2,1,0:T(8,128)(2,1)}, bf16[3,96,128]{2,1,0:T(8,128)(2,1)S(1)}, u32[]{:S(2)}) copy-start(bf16[3,96,128]{2,1,0:T(8,128)(2,1)S(1)} %collective-permute-done.4.refs_2_) | copy-start | bytes 221188
  55.7 0.6 copy-start.5
  85.7 11.8 %collective-permute-start.6 = (bf16[3,96,128]{2,1,0:T(8,128)(2,1)}, bf16[3,96,128]{2,1,0:T(8,128)(2,1)S(1)}, u32[]{:S(2)}, u32[]{:S(2)}) collective-permute-start(bf16[3,96,128]{2,1,0:T(8,128)(2,1)} %get-tuple-element.29), channel_id=1, source_target_pairs={{0,1},{1,2},{2,3},{4,5},{5,6},{6,7},{8,9},{9,10},{10,11},{12,13},{... | collective-permute-start | bytes 221192 | tf_op jit(solution)/shard_map/ppermute | solution.py:516
  89.3 8.3 %collective-permute-start.7 = (bf16[3,96,128]{2,1,0:T(8,128)(2,1)}, bf16[3,96,128]{2,1,0:T(8,128)(2,1)S(1)}, u32[]{:S(2)}, u32[]{:S(2)}) collective-permute-start(bf16[3,96,128]{2,1,0:T(8,128)(2,1)} %get-tuple-element.30), channel_id=1, source_target_pairs={{1,0},{2,1},{3,2},{5,4},{6,5},{7,6},{9,8},{10,9},{11,10},{13,12},{... | collective-permute-start | bytes 221192 | tf_op jit(solution)/shard_map/ppermute | solution.py:517
  97.5 0.6 copy-start.2
  97.5 0.7 copy-start.3

commit v2 on v1

--- a/solution.py
+++ b/solution.py
@@ -11,6 +11,7 @@
 LG = 16
 LN = 128
 bf, f32 = jnp.bfloat16, jnp.float32
+AHEAD = 3
 PARAMS = pltpu.CompilerParams(vmem_limit_bytes=56 * 2**20)
 
 
@@ -177,10 +178,16 @@
     )(pairs, place, x)
 
 
-def mix_kernel(pairs, place, z_hbm, etop_ref, ebot_ref, w_ref, *rest, mixed, tiles):
-    gots = rest[:tiles]
-    out_hbm, otop_ref, obot_ref, zs, zp, got, wm, top_ref, bot_ref, count, zsem, gsem, osem = rest[tiles:]
+def mix_kernel(pairs, place, z_hbm, *rest, mixed, tiles, edges):
+    w_ref, *rest = rest
+    gots, rest = rest[:tiles], rest[tiles:]
+    if edges:
+        etop_ref, ebot_ref, otop_ref, obot_ref, top_ref, bot_ref, *rest = rest
+    else:
+        out_hbm, *rest = rest
+    zs, zp, got, wm, count, zsem, gsem, osem = rest
     _, nj, rows, _ = zs.shape
+    whole = z_hbm.shape[2]
     hold = got.shape[0]
     peer = hold // tiles
     of_tile = pairs.shape[1] // tiles
@@ -192,13 +199,19 @@
         c.start()
 
     def zcopy(g):
-        return pltpu.make_async_copy(z_hbm.at[g], zs.at[g], zsem.at[g])
+        if not edges:
+            return [pltpu.make_async_copy(z_hbm.at[g], zs.at[g], zsem.at[g, 0])]
+        return [
+            pltpu.make_async_copy(z_hbm.at[g, :, pl.ds(at, 16), :], zs.at[g, :, pl.ds(n * 16, 16), :], zsem.at[g, n])
+            for n, at in enumerate((0, whole - 16))
+        ]
 
     def ocopy(g):
         return pltpu.make_async_copy(zs.at[g], out_hbm.at[g], osem.at[g])
 
     for g in range(mixed):
-        zcopy(g).start()
+        for c in zcopy(g):
+            c.start()
     block = lax.broadcasted_iota(jnp.int32, (LG, LN), 1) // LG
 
     @pl.loop(0, mixed)
@@ -220,35 +233,48 @@
         count[q] = rank + 1
         at = lax.bitwise_xor(q, tile) * peer + rank
         up, side = part(slot, ncb)
-        row = pl.ds(pl.multiple_of(up * 16, 16), 16)
-        for g in range(mixed):
-            for h in range(2):
-                zp[g, 2 * side + h, row, :] = got[at, 2 * g + h]
+
+        def put(up):
+            row = pl.ds(pl.multiple_of(up * 16, 16), 16)
+            for g in range(mixed):
+                for h in range(2):
+                    zp[g, 2 * side + h, row, :] = got[at, 2 * g + h]
+        if edges:
+            pl.when(up == 0)(lambda: put(0))
+            pl.when(up == whole // 16 - 1)(lambda: put(1))
+        else:
+            put(up)
 
     @pl.loop(0, mixed)
     def _(g):
-        zcopy(g).wait()
+        for c in zcopy(g):
+            c.wait()
         own = zs[g].reshape(nj * rows, LN)
         both = jnp.concatenate([own, zp[g].reshape(nj * rows, LN)], 1)
         new = own.astype(f32) + jnp.dot(both, wm[g], preferred_element_type=f32)
         new = new.astype(bf).reshape(nj, rows, LN)
-        zs[g] = new
-        ocopy(g).start()
+        if not edges:
+            zs[g] = new
+            ocopy(g).start()
+            return
         for j in range(nj):
             for r in range(3):
                 top_ref[r, pl.ds(g * nj + j, 1), :] = new[j, r:r + 1].astype(f32)
                 bot_ref[r, pl.ds(g * nj + j, 1), :] = new[j, rows - 3 + r:rows - 2 + r].astype(f32)
 
-    top_ref[:, mixed * nj:, :] = etop_ref[...]
-    bot_ref[:, mixed * nj:, :] = ebot_ref[...]
-    otop_ref[...] = top_ref[...].astype(bf)
-    obot_ref[...] = bot_ref[...].astype(bf)
-    for g in range(mixed):
-        ocopy(g).wait()
-
-
-def mix(pairs, place, z, etop, ebot, w, gots):
+    if edges:
+        top_ref[:, mixed * nj:, :] = etop_ref[...]
+        bot_ref[:, mixed * nj:, :] = ebot_ref[...]
+        otop_ref[...] = top_ref[...].astype(bf)
+        obot_ref[...] = bot_ref[...].astype(bf)
+    else:
+        for g in range(mixed):
+            ocopy(g).wait()
+
+
+def mix(pairs, place, z, w, gots, ends=()):
     ng, nj, rows, _ = z.shape
+    edges = len(ends) > 0
     mixed = w.shape[0]
     tiles = len(gots)
     hold = gots[0].shape[0] * tiles
@@ -256,26 +282,26 @@
     sm = pl.BlockSpec(memory_space=pltpu.SMEM)
     hbm = pl.BlockSpec(memory_space=pl.ANY)
     edge = jax.ShapeDtypeStruct((3, ng * nj, LN), bf)
+    here = 32 if edges else rows
     return pl.pallas_call(
-        functools.partial(mix_kernel, mixed=mixed, tiles=tiles),
-        out_shape=(jax.ShapeDtypeStruct((mixed, nj, rows, LN), bf), edge, edge),
-        in_specs=[sm, sm, hbm, vm, vm, vm] + [hbm] * tiles,
-        out_specs=(hbm, vm, vm),
-        scratch_shapes=[
-            VM((mixed, nj, rows, LN), bf),
-            VM((mixed, nj, rows, LN), bf),
+        functools.partial(mix_kernel, mixed=mixed, tiles=tiles, edges=edges),
+        out_shape=(edge, edge) if edges else jax.ShapeDtypeStruct((mixed, nj, rows, LN), bf),
+        in_specs=[sm, sm, hbm, vm] + [hbm] * tiles + [vm] * len(ends),
+        out_specs=(vm, vm) if edges else hbm,
+        scratch_shapes=([VM(edge.shape, f32)] * 2 if edges else []) + [
+            VM((mixed, nj, here, LN), bf),
+            VM((mixed, nj, here, LN), bf),
             VM((hold,) + gots[0].shape[1:], bf),
             VM((mixed, 2 * LN, LN), bf),
-            VM(edge.shape, f32),
-            VM(edge.shape, f32),
             pltpu.SMEM((tiles,), jnp.int32),
-            pltpu.SemaphoreType.DMA((mixed,)),
+            pltpu.SemaphoreType.DMA((mixed, 2)),
             pltpu.SemaphoreType.DMA((tiles,)),
             pltpu.SemaphoreType.DMA((mixed,)),
         ],
         compiler_params=PARAMS,
-        name="mix",
-    )(pairs, place, z, etop, ebot, w, *gots)
+        cost_estimate=pl.CostEstimate(flops=10**9, bytes_accessed=2**23, transcendentals=0),
+        name="mix_edges" if edges else "mix",
+    )(pairs, place, z, w, *gots, *ends)
 
 
 def band_kernel(e_ref, w_ref):
@@ -286,14 +312,12 @@
     @pl.loop(0, e_ref.shape[0])
     def _(g):
         e = e_ref[g]
-        w_ref[g, 0:256] = jnp.zeros((256, LN), bf)
-        w_ref[g, 2048:2304] = jnp.zeros((256, LN), bf)
         for pos, jr in enumerate(list(range(12)) + list(range(-4, 0))):
             s = jr - 3
             r = lroll(e, s * LG)
             r = jnp.where((chunk >= s) & (chunk < 8 + s), r, 0.0)
             for k in range(7):
-                row = (k + 1) * 256 + pos * LG
+                row = k * 256 + pos * LG
                 if jr in (-4, 11):
                     w_ref[g, row:row + LG] = zero
                 else:
@@ -305,14 +329,15 @@
     n = e.shape[0]
     return pl.pallas_call(
         band_kernel,
-        out_shape=jax.ShapeDtypeStruct((n, 2304, LN), bf),
+        out_shape=jax.ShapeDtypeStruct((n, 1792, LN), bf),
         in_specs=[vm], out_specs=vm,
+        cost_estimate=pl.CostEstimate(flops=10**9, bytes_accessed=n * 1792 * LN * 4, transcendentals=0),
         compiler_params=PARAMS,
         name="band",
     )(e)
 
 
-def block_kernel(*refs, parts, want_out, want_z):
+def block_kernel(*refs, parts, layer, want_out, want_z):
     z_hbm, rest = refs[:parts], list(refs[parts:])
     top_ref, bot_ref, fac_ref, w_hbm, gain_ref, wi_hbm, woe_hbm, woo_hbm = rest[:8]
     rest = rest[8:]
@@ -326,25 +351,36 @@
     npair = xe.shape[0] // rows
     per = 3 * npair * LN
 
-    def zcopy(g):
-        src = z_hbm[0] if isinstance(g, int) and g < z_hbm[0].shape[0] else z_hbm[-1]
-        return pltpu.make_async_copy(src.at[g], zs.at[g], zsem.at[g])
+    def zcopy(g, source):
+        return pltpu.make_async_copy(source.at[g], zs.at[g], zsem.at[g])
 
     def wcopy(g):
-        return pltpu.make_async_copy(w_hbm.at[g], wt.at[g], wsem.at[g])
-
-    for g in range(ng):
-        zcopy(g).start()
+        return pltpu.make_async_copy(w_hbm.at[layer * ng + g], wt.at[g], wsem.at[g])
+
+    def fetch(g):
+        for n, source in enumerate(z_hbm):
+            inside = g < z_hbm[0].shape[0]
+            if len(z_hbm) > 1:
+                pl.when(inside if n == 0 else jnp.logical_not(inside))(zcopy(g, source).start)
+            else:
+                zcopy(g, source).start()
         wcopy(g).start()
+
+    for g in range(AHEAD):
+        fetch(jnp.int32(g))
     weights = [pltpu.make_async_copy(a, b, msem.at[i])
                for i, (a, b) in enumerate(((wi_hbm, wi_ref), (woe_hbm, woe_ref), (woo_hbm, woo_ref)))]
-    for c in weights:
-        c.start()
     ssum[...] = jnp.zeros_like(ssum)
 
     @pl.loop(0, ng)
     def _(g):
-        zcopy(g).wait()
+        pl.when(g + AHEAD < ng)(lambda: fetch(g + AHEAD))
+
+        @pl.when(g == ng // 2)
+        def _():
+            for c in weights:
+                c.start()
+        zcopy(g, z_hbm[-1]).wait()
         wcopy(g).wait()
 
         for j in range(nj):
@@ -363,7 +399,8 @@
                 lhs[j * hr:(j + 1) * hr, a * 256:a * 256 + LN] = v[j]
                 lhs[j * hr:(j + 1) * hr, a * 256 + LN:a * 256 + 256] = jnp.where(m64, nxt, prv)
 
-        rhs = jnp.concatenate([wt[g, 256:2304], wt[g, 0:2048]], 1)
+        band_g, zero_g = wt[g], jnp.zeros((256, LN), bf)
+        rhs = jnp.concatenate([jnp.concatenate([band_g, zero_g], 0), jnp.concatenate([zero_g, band_g], 0)], 1)
         sp = jnp.dot(lhs[...], rhs, preferred_element_type=f32)
         spr[g] = sp
         ssum[...] += sp
@@ -428,15 +465,13 @@
                     upd[3 * i + t, pl.ds(p, hr, stride=2), :] = val[p * hr:(p + 1) * hr]
 
         fac = fac_ref[0, 0]
-        own = from_patch([zs[g, j] for g in range(ng)])
-        res = []
-        for n in range(3 * npair):
-            y = (own[n].astype(f32) + fac * upd[n]).astype(bf)
-            if want_out:
-                out[j, :, n * LN:(n + 1) * LN] = y
-            res.append(y)
+        if want_out:
+            own = from_patch([zs[g, j] for g in range(ng)])
+            for n in range(3 * npair):
+                out[j, :, n * LN:(n + 1) * LN] = (own[n].astype(f32) + fac * upd[n]).astype(bf)
         if want_z:
-            for g, zz in enumerate(to_patch(res)):
+            for g, part_of in enumerate(to_patch([(fac * upd[n]).astype(bf) for n in range(3 * npair)])):
+                zz = (zs[g, j].astype(f32) + part_of.astype(f32)).astype(bf)
                 outz[g, j] = zz
                 for r in range(3):
                     tops[r, pl.ds(g * nj + j, 1), :] = zz[r:r + 1].astype(f32)
@@ -454,7 +489,7 @@
             c.wait()
 
 
-def block(zs, top, bot, fac, w, gain, wi, woe, woo, want_out=True, want_z=True):
+def block(zs, top, bot, fac, w, gain, wi, woe, woo, layer=0, want_out=True, want_z=True):
     ng, nj, rows, _ = zs[-1].shape
     hr = rows // 2
     per = ng * LG * PC
@@ -467,7 +502,7 @@
         edge = jax.ShapeDtypeStruct(top.shape, bf)
         shapes += [jax.ShapeDtypeStruct((ng, nj, rows, LN), bf), edge, edge]
     return pl.pallas_call(
-        functools.partial(block_kernel, parts=len(zs), want_out=want_out, want_z=want_z),
+        functools.partial(block_kernel, parts=len(zs), layer=layer, want_out=want_out, want_z=want_z),
         out_shape=tuple(shapes),
         in_specs=[hbm] * len(zs) + [vm, vm, pl.BlockSpec(memory_space=pltpu.SMEM), hbm, vm, hbm, hbm, hbm],
         out_specs=((hbm,) if want_out else ()) + ((hbm, vm, vm) if want_z else ()),
@@ -475,7 +510,7 @@
             VM((ng, nj, rows, LN), bf),
             VM((nj, rows + 16, LN), f32),
             VM((nj * hr, 2048), bf),
-            VM((ng, 2304, LN), bf),
+            VM((ng, 1792, LN), bf),
             VM((ng, nj * hr, 256), f32),
             VM((nj * hr, 256), f32),
             VM((nj * hr, 256), f32),
@@ -538,14 +573,15 @@
     e, *weights = prep_all(depth_weight, norm_gain, inner_weight, outer_weight)
     which = jnp.where(section == 0, 0, 2)
     wmix = jnp.tile(pick(mix_weight, section).astype(f32), (1, 1, PC))
-    wone, wtwo = band(pick(e, which)), band(e[1])
-    zc, top, bot = mix(pairs, place, z, etop, ebot, wmix, gots)
-    top, bot = halo(top, bot)
+    bands = band(jnp.concatenate([pick(e, which), e[1]]))
+    gots, bands = lax.optimization_barrier((gots, bands))
+    top, bot = halo(*mix(pairs, place, z, wmix, gots, (etop, ebot)))
+    zc = mix(pairs, place, z, wmix, gots)
     factor = jnp.where(section == 0, 1.0, wet[0].astype(f32)).reshape(1, 1)
-    _, z, top, bot = block([zc, z], top, bot, factor, wone, *(pick(w, which) for w in weights))
+    z, top, bot = block([zc, z], top, bot, factor, bands, *(pick(w, which) for w in weights), want_out=False)
     top, bot = halo(top, bot)
     factor = jnp.where(section == 0, 1.0, 0.0).reshape(1, 1)
-    out, = block([z], top, bot, factor, wtwo, *(w[1] for w in weights), want_z=False)
+    out, = block([z], top, bot, factor, bands, *(w[1] for w in weights), layer=1, want_z=False)
     return out[None, None]
 
 

time: 124 us -> 122 us (0.984)
  waiting for transfers between devices: 15.5 us -> 10.6 us
    ppermute x4, waiting for transfers between devices: 11 us -> 6.25 us  [exchange(): lax.ppermute(o, ('comp', 'tile'), [(s * n + t, (1 - s) * n + (t ^ d)) for...]
    pallas_call x5, Pallas kernels: 73.2 us -> 74.4 us  [the longest x2 53.5 us: block(): pl.pallas_call(functools.partial(block_kernel, parts=len(zs), layer=layer...]
    unnamed x17 -> x23, local copies, waits for them, and re-layouts: 2.81 us -> 2.85 us
  transfers between devices with their start and end apart: 8 -> 8, of which waited for: 3 -> 3; matrix products, arithmetic and copies ran while one was open for 8% -> 7% of each run, Pallas kernels for 9% -> 12%
where the time goes in v2:
time: 122 us; the launch traced here: 121 us
  Pallas kernels  83.3 us (68%)
  starting transfers between devices  14.9 us (12%)
  waiting for transfers between devices  10.6 us (9%)
  local copies, waits for them, and re-layouts  10.4 us (9%)
  other arithmetic  1.33 us (1%)
    pallas_call x2, Pallas kernels, block(): pl.pallas_call(functools.partial(block_kernel, parts=len(zs), layer=layer...  53.5 us
    pallas_call x2, Pallas kernels, mix(): pl.pallas_call(functools.partial(mix_kernel, mixed=mixed, tiles=tiles, ed...  12.7 us
    pallas_call x1, Pallas kernels, pack(): pl.pallas_call(functools.partial(pack_kernel, mixed=mixed, tiles=tiles),...  8.9 us
    pallas_call x1, Pallas kernels, band(): pl.pallas_call(band_kernel, out_shape=jax.ShapeDtypeStruct((n, 1792, LN),...  8.24 us
    ppermute x2, starting transfers between devices, halo(): lax.ppermute(bot, 'row', [(i, i + 1) for i in range(n - 1)])  7.96 us
    ppermute x4, waiting for transfers between devices, exchange(): lax.ppermute(o, ('comp', 'tile'), [(s * n + t, (1 - s) * n + (t ^ d)) for...  6.25 us
    ppermute x4, starting transfers between devices, exchange(): lax.ppermute(o, ('comp', 'tile'), [(s * n + t, (1 - s) * n + (t ^ d)) for...  4.34 us
    ppermute x2, waiting for transfers between devices, halo(): lax.ppermute(top, 'row', [(i + 1, i) for i in range(n - 1)])  4.18 us
  transfers between devices with their start and end apart: 8, of which 3 were waited for; matrix products, arithmetic and copies ran while one was open for 7% of the time, Pallas kernels for 12%

profile of v2, /device:TPU:0, one launch (start us, length us, event | category | flops | bytes accessed | tf_op | source)
XLA Modules:
  0.0 121.4 jit_solution(10627221839707376775)
XLA Ops:
  0.0 0.6 pad_add_fusion.place
  0.6 8.9 %pack.1 = (bf16[12,8,128,128]{3,2,1,0:T(8,128)(2,1)}, f32[3,32,128]{2,1,0:T(8,128)}, f32[3,32,128]{2,1,0:T(8,128)}, bf16[8,16,16,128]{3,2,1,0:T(8,128)(2,1)}, bf...) custom-call(s32[2,512]{1,0:T(2,128)} %pairs.5, ...), custom_call_target="tpu_custom_call" | custom-call | tf_op jit(solution)/shard_map/pack/pallas_call | solution.py:161
  10.0 2.6 %collective-permute-start.1 = (bf16[8,16,16,128]{3,2,1,0:T(8,128)(2,1)}, bf16[8,16,16,128]{3,2,1,0:T(8,128)(2,1)}, u32[]{:S(2)}, u32[]{:S(2)}) collective-permute-start(bf16[8,16,16,128]{3,2,1,0:T(8,128)(2,1)} %get-tuple-element.24), channel_id=1, source_target_pairs={{0,20},{4,16},{8,28},{12,24},{16,4},{20,0},{24,12},{28,8},{1,21},{... | collective-permute-start | bytes 1572872 | tf_op jit(solution)/shard_map/ppermute | solution.py:560
  12.6 1.2 collective-permute-start.2
  14.9 0.9 slice.27
  16.1 0.7 copy-done.1
  17.1 0.6 pad_maximum_fusion.e_ref
  17.7 8.2 %band.1.refs_5_.refs_4_ = bf16[24,1792,128]{2,1,0:T(8,128)(2,1)} custom-call(f32[24,8,128]{2,1,0:T(8,128)} %pad_maximum_fusion.e_ref), custom_call_target="tpu_custom_call" | custom-call | flops 1000000000 | bytes 22020096 | tf_op jit(solution)/shard_map/band/pallas_call | solution.py:330
  26.0 0.8 copy.20.rest_0_
  29.4 1.0 fusion.1
  30.4 1.5 %fusion.5 = (bf16[768,256]{1,0:T(8,128)(2,1)}, bf16[768,256]{1,0:T(8,128)(2,1)}, bf16[768,256]{1,0:T(8,128)(2,1)}, bf16[768,256]{1,0:T(8,128)(2,1)}) fusion(bf16[3,768,192]{2,1,0:T(8,128)(2,1)S(1)} %copy.22, s32[]{:T(128)S(6)} %select_n.26), kind=kLoop, calls=%fused_computation.12 | loop fusion | bytes 2457604 | tf_op jit(solution)/shard_map/squeeze | solution.py:584
  31.9 6.2 %collective-permute-done.2.rest_3_ = bf16[8,16,16,128]{3,2,1,0:T(8,128)(2,1)} collective-permute-done((bf16[8,16,16,128]{3,2,1,0:T(8,128)(2,1)}, bf16[8,16,16,128]{3,2,1,0:T(8,128)(2,1)}, u32[]{:S(2)}, u32[]{:S(2)}) %collective-permute-start.2) | collective-permute-done | bytes 524320 | tf_op jit(solution)/shard_map/ppermute | solution.py:560
  38.2 5.8 %mix_edges.1 = (bf16[3,96,128]{2,1,0:T(8,128)(2,1)}, bf16[3,96,128]{2,1,0:T(8,128)(2,1)}) custom-call(s32[2,512]{1,0:T(2,128)} %pairs.5, s32[3]{0:T(128)} %pad_add_fusion.place, bf16[12,8,128,128]{3,2,1,0:T(8,128)(2,1)} %get-tuple-element.22.z_hbm.refs_1_, f32[8,32,128]{2,1,0:T(8,128)} %copy.20.rest_0_, bf16[8,16,16,128]{3,2,1,0:T(8,128)(2,1)} %copy-done, ...), custom_call_target="tpu_custom_call" | custom-call | flops 1000000000 | bytes 8388608 | tf_op jit(solution)/shard_map/mix_edges/pallas_call | solution.py:286
  44.0 3.5 %collective-permute-start.4 = (bf16[3,96,128]{2,1,0:T(8,128)(2,1)}, bf16[3,96,128]{2,1,0:T(8,128)(2,1)S(1)}, u32[]{:S(2)}, u32[]{:S(2)}) collective-permute-start(bf16[3,96,128]{2,1,0:T(8,128)(2,1)} %get-tuple-element.33), channel_id=1, source_target_pairs={{0,1},{1,2},{2,3},{4,5},{5,6},{6,7},{8,9},{9,10},{10,11},{12,13},{... | collective-permute-start | bytes 221192 | tf_op jit(solution)/shard_map/ppermute | solution.py:551
  47.5 1.3 %collective-permute-start.5 = (bf16[3,96,128]{2,1,0:T(8,128)(2,1)}, bf16[3,96,128]{2,1,0:T(8,128)(2,1)S(1)}, u32[]{:S(2)}, u32[]{:S(2)}) collective-permute-start(bf16[3,96,128]{2,1,0:T(8,128)(2,1)} %get-tuple-element.34), channel_id=1, source_target_pairs={{1,0},{2,1},{3,2},{5,4},{6,5},{7,6},{9,8},{10,9},{11,10},{13,12},{... | collective-permute-start | bytes 221192 | tf_op jit(solution)/shard_map/ppermute | solution.py:552
  48.8 6.9 %mix.1.refs_0_ = bf16[8,8,128,128]{3,2,1,0:T(8,128)(2,1)} custom-call(s32[2,512]{1,0:T(2,128)} %pairs.5, s32[3]{0:T(128)} %pad_add_fusion.place, bf16[12,8,128,128]{3,2,1,0:T(8,128)(2,1)} %get-tuple-element.22.z_hbm.refs_1_, f32[8,32,128]{2,1,0:T(8,128)} %copy.20.rest_0_, bf16[8,16,16,128]{3,2,1,0:T(8,128)(2,1)} %copy-done, ...), custom_call_target="tpu_custom_call" | custom-call | flops 1000000000 | bytes 8388608 | tf_op jit(solution)/shard_map/mix/pallas_call | solution.py:286
  55.7 0.6 copy-done.5
  56.4 28.0 %block.2 = (bf16[12,8,128,128]{3,2,1,0:T(8,128)(2,1)}, bf16[3,96,128]{2,1,0:T(8,128)(2,1)}, bf16[3,96,128]{2,1,0:T(8,128)(2,1)}) custom-call(bf16[8,8,128,128]{3,2,1,0:T(8,128)(2,1)} %mix.1.refs_0_, bf16[12,8,128,128]{3,2,1,0:T(8,128)(2,1)} %get-tuple-element.22.z_hbm.refs_1_, bf16[3,96,128]{2,1,0:T(8,128)(2,1)} %copy-done.5, bf16[3,96,128]{2,1,0:T(8,128)(2,1)} %copy-done.6, ...), custom_call_target="tpu_custom_call" | custom-call | tf_op jit(solution)/shard_map/block/pallas_call | solution.py:504
  84.4 4.5 %collective-permute-start.6 = (bf16[3,96,128]{2,1,0:T(8,128)(2,1)}, bf16[3,96,128]{2,1,0:T(8,128)(2,1)S(1)}, u32[]{:S(2)}, u32[]{:S(2)}) collective-permute-start(bf16[3,96,128]{2,1,0:T(8,128)(2,1)} %get-tuple-element.37), channel_id=1, source_target_pairs={{0,1},{1,2},{2,3},{4,5},{5,6},{6,7},{8,9},{9,10},{10,11},{12,13},{... | collective-permute-start | bytes 221192 | tf_op jit(solution)/shard_map/ppermute | solution.py:551
  88.8 1.3 %collective-permute-start.7 = (bf16[3,96,128]{2,1,0:T(8,128)(2,1)}, bf16[3,96,128]{2,1,0:T(8,128)(2,1)S(1)}, u32[]{:S(2)}, u32[]{:S(2)}) collective-permute-start(bf16[3,96,128]{2,1,0:T(8,128)(2,1)} %get-tuple-element.38), channel_id=1, source_target_pairs={{1,0},{2,1},{3,2},{5,4},{6,5},{7,6},{9,8},{10,9},{11,10},{13,12},{... | collective-permute-start | bytes 221192 | tf_op jit(solution)/shard_map/ppermute | solution.py:552
  90.3 0.7 tile.28.refs_5_
  91.1 4.2 %collective-permute-done.7.refs_2_ = bf16[3,96,128]{2,1,0:T(8,128)(2,1)S(1)} collective-permute-done((bf16[3,96,128]{2,1,0:T(8,128)(2,1)}, bf16[3,96,128]{2,1,0:T(8,128)(2,1)S(1)}, u32[]{:S(2)}, u32[]{:S(2)}) %collective-permute-start.7) | collective-permute-done | bytes 73760 | tf_op jit(solution)/shard_map/ppermute | solution.py:552
  95.3 0.6 copy-done.8
  95.9 25.5 %block.3 = bf16[128,12288]{1,0:T(8,128)(2,1)} custom-call(bf16[12,8,128,128]{3,2,1,0:T(8,128)(2,1)} %get-tuple-element.36.refs_0_, bf16[3,96,128]{2,1,0:T(8,128)(2,1)} %copy-done.7, bf16[3,96,128]{2,1,0:T(8,128)(2,1)} %copy-done.8, f32[1,1]{1,0:T(1,128)} %bitcast.14.refs_3_, bf16[24,1792,128]{2,1,0:T(8,128)(2,1)} %band.1.refs_5_.refs_4_, ...), custom_call_target="tpu_custom_call" | custom-call | tf_op jit(solution)/shard_map/block/pallas_call | solution.py:504
  (46 shorter events, 4.3 us)
Async XLA Ops:
  0.6 13.3 %copy-start.4 = (f32[3,7,7,192]{3,2,1,0:T(8,128)S(1)}, f32[3,7,7,192]{3,2,1,0:T(8,128)}, u32[]{:S(2)}) copy-start(f32[3,7,7,192]{3,2,1,0:T(8,128)} %param.12) | copy-start | bytes 338692
  9.5 22.4 %collective-permute-start = (bf16[8,16,16,128]{3,2,1,0:T(8,128)(2,1)}, bf16[8,16,16,128]{3,2,1,0:T(8,128)(2,1)S(1)}, u32[]{:S(2)}, u32[]{:S(2)}) collective-permute-start(bf16[8,16,16,128]{3,2,1,0:T(8,128)(2,1)} %get-tuple-element.23), channel_id=1, source_target_pairs={{0,16},{4,20},{8,24},{12,28},{16,0},{20,4},{24,8},{28,12},{1,17},{... | collective-permute-start | bytes 1572872 | tf_op jit(solution)/shard_map/ppermute | solution.py:560
  10.0 21.9 %collective-permute-start.1 = (bf16[8,16,16,128]{3,2,1,0:T(8,128)(2,1)}, bf16[8,16,16,128]{3,2,1,0:T(8,128)(2,1)}, u32[]{:S(2)}, u32[]{:S(2)}) collective-permute-start(bf16[8,16,16,128]{3,2,1,0:T(8,128)(2,1)} %get-tuple-element.24), channel_id=1, source_target_pairs={{0,20},{4,16},{8,28},{12,24},{16,4},{20,0},{24,12},{28,8},{1,21},{... | collective-permute-start | bytes 1572872 | tf_op jit(solution)/shard_map/ppermute | solution.py:560
  12.6 25.5 %collective-permute-start.2 = (bf16[8,16,16,128]{3,2,1,0:T(8,128)(2,1)}, bf16[8,16,16,128]{3,2,1,0:T(8,128)(2,1)}, u32[]{:S(2)}, u32[]{:S(2)}) collective-permute-start(bf16[8,16,16,128]{3,2,1,0:T(8,128)(2,1)} %get-tuple-element.25), channel_id=1, source_target_pairs={{0,24},{4,28},{8,16},{12,20},{16,8},{20,12},{24,0},{28,4},{1,25},{... | collective-permute-start | bytes 1572872 | tf_op jit(solution)/shard_map/ppermute | solution.py:560
  13.8 24.3 %collective-permute-start.3 = (bf16[8,16,16,128]{3,2,1,0:T(8,128)(2,1)}, bf16[8,16,16,128]{3,2,1,0:T(8,128)(2,1)}, u32[]{:S(2)}, u32[]{:S(2)}) collective-permute-start(bf16[8,16,16,128]{3,2,1,0:T(8,128)(2,1)} %get-tuple-element.26), channel_id=1, source_target_pairs={{0,28},{4,24},{8,20},{12,16},{16,12},{20,8},{24,4},{28,0},{1,29},{... | collective-permute-start | bytes 1572872 | tf_op jit(solution)/shard_map/ppermute | solution.py:560
  15.7 1.0 copy-start.1
  17.7 8.2 %copy-start.9 = (bf16[2,8,32,16]{2,3,1,0:T(8,128)(2,1)S(1)}, bf16[2,8,32,16]{2,3,1,0:T(8,128)(2,1)}, u32[]{:S(2)}) copy-start(bf16[2,8,32,16]{2,3,1,0:T(8,128)(2,1)} %param.11) | copy-start | bytes 49156
  26.0 1.2 copy-start.3
  26.0 1.7 %copy-start.10 = (f32[3,192]{1,0:T(4,128)S(1)}, f32[3,192]{1,0:T(4,128)}, u32[]{:S(2)}) copy-start(f32[3,192]{1,0:T(4,128)} %param.13) | copy-start | bytes 6916
  27.1 2.2 %copy-start.2 = (bf16[3,192,768]{2,1,0:T(8,128)(2,1)S(1)}, bf16[3,192,768]{2,1,0:T(8,128)(2,1)}, u32[]{:S(2)}) copy-start(bf16[3,192,768]{2,1,0:T(8,128)(2,1)} %param.14) | copy-start | bytes 2654212
  31.9 6.3 %copy-start = (bf16[8,16,16,128]{3,2,1,0:T(8,128)(2,1)}, bf16[8,16,16,128]{3,2,1,0:T(8,128)(2,1)S(1)}, u32[]{:S(2)}) copy-start(bf16[8,16,16,128]{3,2,1,0:T(8,128)(2,1)S(1)} %collective-permute-done.rest_1_) | copy-start | bytes 1572868
  44.0 11.7 %collective-permute-start.4 = (bf16[3,96,128]{2,1,0:T(8,128)(2,1)}, bf16[3,96,128]{2,1,0:T(8,128)(2,1)S(1)}, u32[]{:S(2)}, u32[]{:S(2)}) collective-permute-start(bf16[3,96,128]{2,1,0:T(8,128)(2,1)} %get-tuple-element.33), channel_id=1, source_target_pairs={{0,1},{1,2},{2,3},{4,5},{5,6},{6,7},{8,9},{9,10},{10,11},{12,13},{... | collective-permute-start | bytes 221192 | tf_op jit(solution)/shard_map/ppermute | solution.py:551
  47.5 8.2 %collective-permute-start.5 = (bf16[3,96,128]{2,1,0:T(8,128)(2,1)}, bf16[3,96,128]{2,1,0:T(8,128)(2,1)S(1)}, u32[]{:S(2)}, u32[]{:S(2)}) collective-permute-start(bf16[3,96,128]{2,1,0:T(8,128)(2,1)} %get-tuple-element.34), channel_id=1, source_target_pairs={{1,0},{2,1},{3,2},{5,4},{6,5},{7,6},{9,8},{10,9},{11,10},{13,12},{... | collective-permute-start | bytes 221192 | tf_op jit(solution)/shard_map/ppermute | solution.py:552
  55.7 0.6 copy-start.5
  55.7 0.6 copy-start.6
  84.4 6.8 %collective-permute-start.6 = (bf16[3,96,128]{2,1,0:T(8,128)(2,1)}, bf16[3,96,128]{2,1,0:T(8,128)(2,1)S(1)}, u32[]{:S(2)}, u32[]{:S(2)}) collective-permute-start(bf16[3,96,128]{2,1,0:T(8,128)(2,1)} %get-tuple-element.37), channel_id=1, source_target_pairs={{0,1},{1,2},{2,3},{4,5},{5,6},{6,7},{8,9},{9,10},{10,11},{12,13},{... | collective-permute-start | bytes 221192 | tf_op jit(solution)/shard_map/ppermute | solution.py:551
  88.8 6.5 %collective-permute-start.7 = (bf16[3,96,128]{2,1,0:T(8,128)(2,1)}, bf16[3,96,128]{2,1,0:T(8,128)(2,1)S(1)}, u32[]{:S(2)}, u32[]{:S(2)}) collective-permute-start(bf16[3,96,128]{2,1,0:T(8,128)(2,1)} %get-tuple-element.38), channel_id=1, source_target_pairs={{1,0},{2,1},{3,2},{5,4},{6,5},{7,6},{9,8},{10,9},{11,10},{13,12},{... | collective-permute-start | bytes 221192 | tf_op jit(solution)/shard_map/ppermute | solution.py:552
  91.1 4.2 %copy-start.7 = (bf16[3,96,128]{2,1,0:T(8,128)(2,1)}, bf16[3,96,128]{2,1,0:T(8,128)(2,1)S(1)}, u32[]{:S(2)}) copy-start(bf16[3,96,128]{2,1,0:T(8,128)(2,1)S(1)} %collective-permute-done.6.refs_1_) | copy-start | bytes 221188
  95.3 0.6 copy-start.8

commit v3 on v2

--- a/solution.py
+++ b/solution.py
@@ -11,6 +11,7 @@
 LG = 16
 LN = 128
 bf, f32 = jnp.bfloat16, jnp.float32
+HALO = 3
 AHEAD = 3
 PARAMS = pltpu.CompilerParams(vmem_limit_bytes=56 * 2**20)
 
@@ -127,9 +128,9 @@
         for g in range(ng):
             zs[g, j] = zz[g]
         for g in range(mixed, ng):
-            for r in range(3):
+            for r in range(2 * HALO):
                 top_ref[r, pl.ds((g - mixed) * nj + j, 1), :] = zz[g][r:r + 1].astype(f32)
-                bot_ref[r, pl.ds((g - mixed) * nj + j, 1), :] = zz[g][rows - 3 + r:rows - 2 + r].astype(f32)
+                bot_ref[r, pl.ds((g - mixed) * nj + j, 1), :] = zz[g][rows - 2 * HALO + r:rows - 2 * HALO + r + 1].astype(f32)
         zcopy(j).start()
 
     @pl.loop(0, hold)
@@ -157,7 +158,7 @@
     vm = pl.BlockSpec(memory_space=VM)
     sm = pl.BlockSpec(memory_space=pltpu.SMEM)
     hbm = pl.BlockSpec(memory_space=pl.ANY)
-    edge = jax.ShapeDtypeStruct((3, (ng - mixed) * nj, LN), f32)
+    edge = jax.ShapeDtypeStruct((2 * HALO, (ng - mixed) * nj, LN), f32)
     return pl.pallas_call(
         functools.partial(pack_kernel, mixed=mixed, tiles=tiles),
         out_shape=(jax.ShapeDtypeStruct((ng, nj, rows, LN), bf), edge, edge)
@@ -258,9 +259,10 @@
             ocopy(g).start()
             return
         for j in range(nj):
-            for r in range(3):
+            for r in range(2 * HALO):
+                low = rows - 2 * HALO + r
                 top_ref[r, pl.ds(g * nj + j, 1), :] = new[j, r:r + 1].astype(f32)
-                bot_ref[r, pl.ds(g * nj + j, 1), :] = new[j, rows - 3 + r:rows - 2 + r].astype(f32)
+                bot_ref[r, pl.ds(g * nj + j, 1), :] = new[j, low:low + 1].astype(f32)
 
     if edges:
         top_ref[:, mixed * nj:, :] = etop_ref[...]
@@ -281,7 +283,7 @@
     vm = pl.BlockSpec(memory_space=VM)
     sm = pl.BlockSpec(memory_space=pltpu.SMEM)
     hbm = pl.BlockSpec(memory_space=pl.ANY)
-    edge = jax.ShapeDtypeStruct((3, ng * nj, LN), bf)
+    edge = jax.ShapeDtypeStruct((2 * HALO, ng * nj, LN), bf)
     here = 32 if edges else rows
     return pl.pallas_call(
         functools.partial(mix_kernel, mixed=mixed, tiles=tiles, edges=edges),
@@ -343,12 +345,16 @@
     rest = rest[8:]
     out_hbm = rest.pop(0) if want_out else None
     outz_hbm, otop_ref, obot_ref = (rest.pop(0) for _ in range(3)) if want_z else (None,) * 3
-    zs, zf, lhs, wt, spr, ssum, nrm, xe, xo, upd, out, outz, wi_ref, woe_ref, woo_ref, tops, bots, zsem, wsem, osem, msem = rest
+    zs, zf, lhs, wt, spr, ssum, nrm, upd, out, outz, wi_ref, woe_ref, woo_ref, tops, bots, zsem, wsem, osem, msem = rest
     ng, nj, rows, _ = zs.shape
     hr = rows // 2
     pad = 8
+    have = top_ref.shape[0]
+    extra = have > HALO
+    ends = (-2, -1, hr, hr + 1)
+    beyond = slice(nj * hr, nj * hr + 4 * nj)
     count = ng * LG
-    npair = xe.shape[0] // rows
+    npair = PC // 2
     per = 3 * npair * LN
 
     def zcopy(g, source):
@@ -387,7 +393,7 @@
             zf[j, pl.ds(pad, rows), :] = zs[g, j].astype(f32)
         for r in range(3):
             hs = pl.ds(pl.multiple_of(g * nj, nj), nj)
-            zf[:, pad - 3 + r, :] = top_ref[r, hs, :].astype(f32)
+            zf[:, pad - 3 + r, :] = top_ref[have - 3 + r, hs, :].astype(f32)
             zf[:, pad + rows + r, :] = bot_ref[r, hs, :].astype(f32)
         m64 = lane_bit((hr, LN), 64)
         zero = jnp.zeros((hr, LN), bf)
@@ -399,6 +405,29 @@
                 lhs[j * hr:(j + 1) * hr, a * 256:a * 256 + LN] = v[j]
                 lhs[j * hr:(j + 1) * hr, a * 256 + LN:a * 256 + 256] = jnp.where(m64, nxt, prv)
 
+        if extra:
+            m64 = lane_bit((nj, LN), 64)
+            sub = lax.broadcasted_iota(jnp.int32, (nj, LN), 0)
+            got = {}
+
+            def row_of(at):
+                if at not in got:
+                    if 0 <= at < rows:
+                        v = zf[:, pad + at, :]
+                    elif -have <= at < 0:
+                        v = top_ref[at + have, hs, :].astype(f32)
+                    elif rows <= at < rows + have:
+                        v = bot_ref[at - rows, hs, :].astype(f32)
+                    else:
+                        v = jnp.zeros((nj, LN), f32)
+                    nxt = jnp.where(sub < nj - 1, pltpu.roll(v, nj - 1, 0), 0.0)
+                    prv = jnp.where(sub > 0, pltpu.roll(v, 1, 0), 0.0)
+                    got[at] = v, jnp.where(m64, nxt, prv)
+                return got[at]
+            for a in range(8):
+                for n in range(2):
+                    v = jnp.concatenate([row_of(2 * r - 3 + a)[n] for r in ends], 0).astype(bf)
+                    lhs[beyond, a * 256 + n * LN:a * 256 + (n + 1) * LN] = v
         band_g, zero_g = wt[g], jnp.zeros((256, LN), bf)
         rhs = jnp.concatenate([jnp.concatenate([band_g, zero_g], 0), jnp.concatenate([zero_g, band_g], 0)], 1)
         sp = jnp.dot(lhs[...], rhs, preferred_element_type=f32)
@@ -417,15 +446,15 @@
 
     nrm[...] = lane_mean(ssum[...])
 
-    @pl.loop(0, nj)
-    def _(j):
-        js = pl.ds(pl.multiple_of(j * hr, hr), hr)
-        mean = nrm[js, :]
-        q = jnp.zeros((hr, 256), f32)
+    @pl.loop(0, ssum.shape[0] // 32)
+    def _(n):
+        rs = pl.ds(pl.multiple_of(n * 32, 32), 32)
+        mean = nrm[rs, :]
+        q = jnp.zeros((32, 256), f32)
         for g in range(ng):
-            c = spr[g, js, :] - mean
+            c = spr[g, rs, :] - mean
             q = q + c * c
-        ssum[js, :] = q
+        ssum[rs, :] = q
     ssum[...] = lax.rsqrt(lane_mean(ssum[...]) + 1e-06)
 
     def outcopy(j):
@@ -437,34 +466,33 @@
             cs.append(pltpu.make_async_copy(outz.at[:, j], outz_hbm.at[:, j], osem.at[1, j]))
         return cs
 
-    @pl.loop(0, nj)
-    def _(j):
-        js = pl.ds(pl.multiple_of(j * hr, hr), hr)
-
+    fac = fac_ref[0, 0]
+
+    def update(js):
         mean, rstd = nrm[js, :], ssum[js, :]
         zz = [((spr[g, js, :] - mean) * rstd * gain_ref[g:g + 1, :]).astype(bf) for g in range(ng)]
-        for p in range(2):
-            nat = from_patch([t[:, p * LN:(p + 1) * LN] for t in zz])
-            for i in range(npair):
-                rs = slice(i * rows + p * hr, i * rows + (p + 1) * hr)
-                xe[rs, :LN] = nat[3 * i]
-                xe[rs, LN:] = nat[3 * i + 1]
-                xo[rs, :LN] = nat[3 * i + 1]
-                xo[rs, LN:] = nat[3 * i + 2]
+        nat = [from_patch([t[:, p * LN:(p + 1) * LN] for t in zz]) for p in range(2)]
+        nat = [jnp.concatenate([a, b], 0) for a, b in zip(*nat)]
+        many = nat[0].shape[0]
+        xe = jnp.concatenate([jnp.concatenate([nat[3 * i], nat[3 * i + 1]], 1) for i in range(npair)], 0)
+        xo = jnp.concatenate([jnp.concatenate([nat[3 * i + 1], nat[3 * i + 2]], 1) for i in range(npair)], 0)
 
         def mlp(x, wi, wo):
             h = gelu(jnp.dot(x, wi, preferred_element_type=f32).astype(bf))
             return jnp.dot(h, wo, preferred_element_type=f32)
-        ue = mlp(xe[...], wi_ref[64:, :], woe_ref[...])
-        uo = mlp(xo[...], wi_ref[:256, :], woo_ref[...])
+        ue = mlp(xe, wi_ref[64:, :], woe_ref[...])
+        uo = mlp(xo, wi_ref[:256, :], woo_ref[...])
+        res = []
         for i in range(npair):
-            e = ue[i * rows:(i + 1) * rows]
-            o = uo[i * rows:(i + 1) * rows]
-            for t, val in enumerate((e[:, :LN], e[:, LN:] + o[:, :LN], o[:, LN:])):
-                for p in range(2):
-                    upd[3 * i + t, pl.ds(p, hr, stride=2), :] = val[p * hr:(p + 1) * hr]
-
-        fac = fac_ref[0, 0]
+            e, o = ue[i * many:(i + 1) * many], uo[i * many:(i + 1) * many]
+            res += [e[:, :LN], e[:, LN:] + o[:, :LN], o[:, LN:]]
+        return res
+
+    @pl.loop(0, nj)
+    def _(j):
+        for n, val in enumerate(update(pl.ds(pl.multiple_of(j * hr, hr), hr))):
+            for p in range(2):
+                upd[n, pl.ds(p, hr, stride=2), :] = val[p * hr:(p + 1) * hr]
         if want_out:
             own = from_patch([zs[g, j] for g in range(ng)])
             for n in range(3 * npair):
@@ -473,13 +501,17 @@
             for g, part_of in enumerate(to_patch([(fac * upd[n]).astype(bf) for n in range(3 * npair)])):
                 zz = (zs[g, j].astype(f32) + part_of.astype(f32)).astype(bf)
                 outz[g, j] = zz
-                for r in range(3):
-                    tops[r, pl.ds(g * nj + j, 1), :] = zz[r:r + 1].astype(f32)
-                    bots[r, pl.ds(g * nj + j, 1), :] = zz[rows - 3 + r:rows - 2 + r].astype(f32)
         for c in outcopy(j):
             c.start()
 
-    if want_z:
+    if extra:
+        more = to_patch([(fac * val).astype(bf) for val in update(pl.ds(nj * hr, 4 * nj))])
+        for g in range(ng):
+            gs = pl.ds(g * nj, nj)
+            for r in range(HALO):
+                for at, keep, own, to in ((r - HALO, 1, top_ref[have - HALO + r, gs, :], tops), (rows + r, 2, bot_ref[r, gs, :], bots)):
+                    n = at % 2 * 4 * nj + ends.index(at // 2) * nj
+                    to[r, gs, :] = fac_ref[0, keep] * (own.astype(f32) + more[g][n:n + nj].astype(f32))
         otop_ref[...] = tops[...].astype(bf)
         obot_ref[...] = bots[...].astype(bf)
 
@@ -492,6 +524,8 @@
 def block(zs, top, bot, fac, w, gain, wi, woe, woo, layer=0, want_out=True, want_z=True):
     ng, nj, rows, _ = zs[-1].shape
     hr = rows // 2
+    many = nj * hr + (4 * nj if want_z else 0)
+    assert want_z == (top.shape[0] == 2 * HALO)
     per = ng * LG * PC
     vm = pl.BlockSpec(memory_space=VM)
     hbm = pl.BlockSpec(memory_space=pl.ANY)
@@ -499,7 +533,7 @@
     if want_out:
         shapes.append(jax.ShapeDtypeStruct((rows, nj * per), bf))
     if want_z:
-        edge = jax.ShapeDtypeStruct(top.shape, bf)
+        edge = jax.ShapeDtypeStruct((HALO,) + top.shape[1:], bf)
         shapes += [jax.ShapeDtypeStruct((ng, nj, rows, LN), bf), edge, edge]
     return pl.pallas_call(
         functools.partial(block_kernel, parts=len(zs), layer=layer, want_out=want_out, want_z=want_z),
@@ -509,20 +543,19 @@
         scratch_shapes=[
             VM((ng, nj, rows, LN), bf),
             VM((nj, rows + 16, LN), f32),
-            VM((nj * hr, 2048), bf),
+            VM((many, 2048), bf),
             VM((ng, 1792, LN), bf),
-            VM((ng, nj * hr, 256), f32),
-            VM((nj * hr, 256), f32),
-            VM((nj * hr, 256), f32),
-            VM((4 * rows, 256), bf), VM((4 * rows, 256), bf),
+            VM((ng, many, 256), f32),
+            VM((many, 256), f32),
+            VM((many, 256), f32),
             VM((12, rows, LN), f32),
             VM((nj, rows, per), bf) if want_out else VM((8, LN), bf),
             VM((ng, nj, rows, LN), bf) if want_z else VM((8, LN), bf),
             VM(wi.shape, bf),
             VM(woe.shape, bf),
             VM(woo.shape, bf),
-            VM(top.shape, f32),
-            VM(top.shape, f32),
+            VM((HALO,) + top.shape[1:], f32),
+            VM((HALO,) + top.shape[1:], f32),
             pltpu.SemaphoreType.DMA((ng,)),
             pltpu.SemaphoreType.DMA((ng,)),
             pltpu.SemaphoreType.DMA((2, nj)),
@@ -577,9 +610,10 @@
     gots, bands = lax.optimization_barrier((gots, bands))
     top, bot = halo(*mix(pairs, place, z, wmix, gots, (etop, ebot)))
     zc = mix(pairs, place, z, wmix, gots)
-    factor = jnp.where(section == 0, 1.0, wet[0].astype(f32)).reshape(1, 1)
-    z, top, bot = block([zc, z], top, bot, factor, bands, *(pick(w, which) for w in weights), want_out=False)
-    top, bot = halo(top, bot)
+    factor = jnp.where(section == 0, 1.0, wet[0].astype(f32))
+    inside = jnp.stack([place[2] > 0, place[2] < lax.axis_size("row") - 1]).astype(f32)
+    factors = jnp.concatenate([factor.reshape(1, 1), inside.reshape(1, 2)], 1)
+    z, top, bot = block([zc, z], top, bot, factors, bands, *(pick(w, which) for w in weights), want_out=False)
     factor = jnp.where(section == 0, 1.0, 0.0).reshape(1, 1)
     out, = block([z], top, bot, factor, bands, *(w[1] for w in weights), layer=1, want_z=False)
     return out[None, None]

time: 122 us -> 113 us (0.926)
  starting transfers between devices: 14.9 us -> 9.12 us
  waiting for transfers between devices: 10.6 us -> 6.51 us
    ppermute x2 -> x1, starting transfers between devices: 7.96 us -> 3.49 us  [halo(): lax.ppermute(bot, 'row', [(i, i + 1) for i in range(n - 1)])]
    ppermute x2 -> x1, waiting for transfers between devices: 4.18 us -> 0.01 us  [halo(): lax.ppermute(top, 'row', [(i + 1, i) for i in range(n - 1)])]
    ppermute x2 -> x1, starting transfers between devices: 2.58 us -> 1.29 us  [halo(): lax.ppermute(top, 'row', [(i + 1, i) for i in range(n - 1)])]
    unnamed x23 -> x19, local copies, waits for them, and re-layouts: 2.85 us -> 1.94 us
  transfers between devices with their start and end apart: 8 -> 6, of which waited for: 3 -> 1; matrix products, arithmetic and copies ran while one was open for 7% -> 9% of each run, Pallas kernels for 12% -> 13%
where the time goes in v3:
time: 113 us; the launch traced here: 112 us
  Pallas kernels  84.2 us (75%)
  local copies, waits for them, and re-layouts  9.44 us (8%)
  starting transfers between devices  9.12 us (8%)
  waiting for transfers between devices  6.51 us (6%)
  other arithmetic  2.05 us (2%)
    pallas_call x2, Pallas kernels, block(): pl.pallas_call(functools.partial(block_kernel, parts=len(zs), layer=layer...  54.2 us
    pallas_call x2, Pallas kernels, mix(): pl.pallas_call(functools.partial(mix_kernel, mixed=mixed, tiles=tiles, ed...  12.8 us
    pallas_call x1, Pallas kernels, pack(): pl.pallas_call(functools.partial(pack_kernel, mixed=mixed, tiles=tiles),...  8.96 us
    pallas_call x1, Pallas kernels, band(): pl.pallas_call(band_kernel, out_shape=jax.ShapeDtypeStruct((n, 1792, LN),...  8.22 us
    ppermute x4, waiting for transfers between devices, exchange(): lax.ppermute(o, ('comp', 'tile'), [(s * n + t, (1 - s) * n + (t ^ d)) for...  6.5 us
    ppermute x4, starting transfers between devices, exchange(): lax.ppermute(o, ('comp', 'tile'), [(s * n + t, (1 - s) * n + (t ^ d)) for...  4.34 us
    ppermute x1, starting transfers between devices, halo(): lax.ppermute(bot, 'row', [(i, i + 1) for i in range(n - 1)])  3.49 us
    squeeze x2, local copies, waits for them, and re-layouts, on_device(): w[1]  2.54 us
  transfers between devices with their start and end apart: 6, of which 1 were waited for; matrix products, arithmetic and copies ran while one was open for 9% of the time, Pallas kernels for 13%

profile of v3, /device:TPU:0, one launch (start us, length us, event | category | flops | bytes accessed | tf_op | source)
XLA Modules:
  0.0 112.3 jit_solution(13059425293857989675)
XLA Ops:
  0.0 0.6 pad_add_fusion.place
  0.6 9.0 %pack.1 = (bf16[12,8,128,128]{3,2,1,0:T(8,128)(2,1)}, f32[6,32,128]{2,1,0:T(8,128)}, f32[6,32,128]{2,1,0:T(8,128)}, bf16[8,16,16,128]{3,2,1,0:T(8,128)(2,1)}, bf...) custom-call(s32[2,512]{1,0:T(2,128)} %pairs.5, ...), custom_call_target="tpu_custom_call" | custom-call | tf_op jit(solution)/shard_map/pack/pallas_call | solution.py:162
  9.6 0.5 collective-permute-start
  10.1 2.6 %collective-permute-start.1 = (bf16[8,16,16,128]{3,2,1,0:T(8,128)(2,1)}, bf16[8,16,16,128]{3,2,1,0:T(8,128)(2,1)}, u32[]{:S(2)}, u32[]{:S(2)}) collective-permute-start(bf16[8,16,16,128]{3,2,1,0:T(8,128)(2,1)} %get-tuple-element.24), channel_id=1, source_target_pairs={{0,20},{4,16},{8,28},{12,24},{16,4},{20,0},{24,12},{28,8},{1,21},{... | collective-permute-start | bytes 1572872 | tf_op jit(solution)/shard_map/ppermute | solution.py:593
  12.7 1.2 %collective-permute-start.2 = (bf16[8,16,16,128]{3,2,1,0:T(8,128)(2,1)}, bf16[8,16,16,128]{3,2,1,0:T(8,128)(2,1)}, u32[]{:S(2)}, u32[]{:S(2)}) collective-permute-start(bf16[8,16,16,128]{3,2,1,0:T(8,128)(2,1)} %get-tuple-element.25), channel_id=1, source_target_pairs={{0,24},{4,28},{8,16},{12,20},{16,8},{20,12},{24,0},{28,4},{1,25},{... | collective-permute-start | bytes 1572872 | tf_op jit(solution)/shard_map/ppermute | solution.py:593
  14.9 0.8 slice.27
  16.2 0.6 copy-done.1
  17.1 0.6 pad_maximum_fusion.e_ref
  17.8 8.2 %band.1.refs_5_.refs_4_ = bf16[24,1792,128]{2,1,0:T(8,128)(2,1)} custom-call(f32[24,8,128]{2,1,0:T(8,128)} %pad_maximum_fusion.e_ref), custom_call_target="tpu_custom_call" | custom-call | flops 1000000000 | bytes 22020096 | tf_op jit(solution)/shard_map/band/pallas_call | solution.py:332
  26.0 0.8 copy.20.rest_0_
  27.6 0.6 copy.22
  28.4 0.6 dynamic-slice_bitcast_fusion.1.refs_6_
  29.2 1.0 fusion.1
  30.2 1.5 %fusion.5 = (bf16[768,256]{1,0:T(8,128)(2,1)}, bf16[768,256]{1,0:T(8,128)(2,1)}, bf16[768,256]{1,0:T(8,128)(2,1)}, bf16[768,256]{1,0:T(8,128)(2,1)}) fusion(bf16[3,768,192]{2,1,0:T(8,128)(2,1)S(1)} %copy.22, s32[]{:T(128)S(6)} %select_n.26), kind=kLoop, calls=%fused_computation.12 | loop fusion | bytes 2457604 | tf_op jit(solution)/shard_map/squeeze | solution.py:618
  31.7 6.5 %collective-permute-done.2.rest_3_ = bf16[8,16,16,128]{3,2,1,0:T(8,128)(2,1)} collective-permute-done((bf16[8,16,16,128]{3,2,1,0:T(8,128)(2,1)}, bf16[8,16,16,128]{3,2,1,0:T(8,128)(2,1)}, u32[]{:S(2)}, u32[]{:S(2)}) %collective-permute-start.2) | collective-permute-done | bytes 524320 | tf_op jit(solution)/shard_map/ppermute | solution.py:593
  38.2 6.0 %mix_edges.1 = (bf16[6,96,128]{2,1,0:T(8,128)(2,1)}, bf16[6,96,128]{2,1,0:T(8,128)(2,1)}) custom-call(s32[2,512]{1,0:T(2,128)} %pairs.5, s32[3]{0:T(128)} %pad_add_fusion.place, bf16[12,8,128,128]{3,2,1,0:T(8,128)(2,1)} %get-tuple-element.22.z_hbm.refs_1_, f32[8,32,128]{2,1,0:T(8,128)} %copy.20.rest_0_, bf16[8,16,16,128]{3,2,1,0:T(8,128)(2,1)} %copy-done, ...), custom_call_target="tpu_custom_call" | custom-call | flops 1000000000 | bytes 8388608 | tf_op jit(solution)/shard_map/mix_edges/pallas_call | solution.py:288
  44.2 3.5 %collective-permute-start.4 = (bf16[6,96,128]{2,1,0:T(8,128)(2,1)}, bf16[6,96,128]{2,1,0:T(8,128)(2,1)S(1)}, u32[]{:S(2)}, u32[]{:S(2)}) collective-permute-start(bf16[6,96,128]{2,1,0:T(8,128)(2,1)} %get-tuple-element.33), channel_id=1, source_target_pairs={{0,1},{1,2},{2,3},{4,5},{5,6},{6,7},{8,9},{9,10},{10,11},{12,13},{... | collective-permute-start | bytes 442376 | tf_op jit(solution)/shard_map/ppermute | solution.py:584
  47.7 1.3 %collective-permute-start.5 = (bf16[6,96,128]{2,1,0:T(8,128)(2,1)}, bf16[6,96,128]{2,1,0:T(8,128)(2,1)S(1)}, u32[]{:S(2)}, u32[]{:S(2)}) collective-permute-start(bf16[6,96,128]{2,1,0:T(8,128)(2,1)} %get-tuple-element.34), channel_id=1, source_target_pairs={{1,0},{2,1},{3,2},{5,4},{6,5},{7,6},{9,8},{10,9},{11,10},{13,12},{... | collective-permute-start | bytes 442376 | tf_op jit(solution)/shard_map/ppermute | solution.py:585
  49.0 0.7 pad_maximum_fusion.1.refs_4_
  49.8 0.7 tile.28.refs_5_
  50.5 6.8 %mix.1.refs_0_ = bf16[8,8,128,128]{3,2,1,0:T(8,128)(2,1)} custom-call(s32[2,512]{1,0:T(2,128)} %pairs.5, s32[3]{0:T(128)} %pad_add_fusion.place, bf16[12,8,128,128]{3,2,1,0:T(8,128)(2,1)} %get-tuple-element.22.z_hbm.refs_1_, f32[8,32,128]{2,1,0:T(8,128)} %copy.20.rest_0_, bf16[8,16,16,128]{3,2,1,0:T(8,128)(2,1)} %copy-done, ...), custom_call_target="tpu_custom_call" | custom-call | flops 1000000000 | bytes 8388608 | tf_op jit(solution)/shard_map/mix/pallas_call | solution.py:288
  57.3 0.6 copy-done.5
  58.1 28.8 %block.2 = (bf16[12,8,128,128]{3,2,1,0:T(8,128)(2,1)}, bf16[3,96,128]{2,1,0:T(8,128)(2,1)}, bf16[3,96,128]{2,1,0:T(8,128)(2,1)}) custom-call(bf16[8,8,128,128]{3,2,1,0:T(8,128)(2,1)} %mix.1.refs_0_, bf16[12,8,128,128]{3,2,1,0:T(8,128)(2,1)} %get-tuple-element.22.z_hbm.refs_1_, bf16[6,96,128]{2,1,0:T(8,128)(2,1)} %copy-done.5, bf16[6,96,128]{2,1,0:T(8,128)(2,1)} %copy-done.6, ...), custom_call_target="tpu_custom_call" | custom-call | tf_op jit(solution)/shard_map/block/pallas_call | solution.py:538
  86.9 25.4 %block.3 = bf16[128,12288]{1,0:T(8,128)(2,1)} custom-call(bf16[12,8,128,128]{3,2,1,0:T(8,128)(2,1)} %get-tuple-element.36.refs_0_, bf16[3,96,128]{2,1,0:T(8,128)(2,1)} %get-tuple-element.37.refs_1_, bf16[3,96,128]{2,1,0:T(8,128)(2,1)} %get-tuple-element.38.refs_2_, f32[1,1]{1,0:T(1,128)} %bitcast.16.refs_3_, bf16[24,1792,128]{2,1,0:T(8,128)(2,1)} %band.1.refs_5_.refs_4_, ...), custom_call_target="tpu_custom_call" | custom-call | tf_op jit(solution)/shard_map/block/pallas_call | solution.py:538
  (40 shorter events, 2.3 us)
Async XLA Ops:
  0.6 13.3 %copy-start.4 = (f32[3,7,7,192]{3,2,1,0:T(8,128)S(1)}, f32[3,7,7,192]{3,2,1,0:T(8,128)}, u32[]{:S(2)}) copy-start(f32[3,7,7,192]{3,2,1,0:T(8,128)} %param.12) | copy-start | bytes 338692
  9.6 22.2 %collective-permute-start = (bf16[8,16,16,128]{3,2,1,0:T(8,128)(2,1)}, bf16[8,16,16,128]{3,2,1,0:T(8,128)(2,1)S(1)}, u32[]{:S(2)}, u32[]{:S(2)}) collective-permute-start(bf16[8,16,16,128]{3,2,1,0:T(8,128)(2,1)} %get-tuple-element.23), channel_id=1, source_target_pairs={{0,16},{4,20},{8,24},{12,28},{16,0},{20,4},{24,8},{28,12},{1,17},{... | collective-permute-start | bytes 1572872 | tf_op jit(solution)/shard_map/ppermute | solution.py:593
  10.1 21.6 %collective-permute-start.1 = (bf16[8,16,16,128]{3,2,1,0:T(8,128)(2,1)}, bf16[8,16,16,128]{3,2,1,0:T(8,128)(2,1)}, u32[]{:S(2)}, u32[]{:S(2)}) collective-permute-start(bf16[8,16,16,128]{3,2,1,0:T(8,128)(2,1)} %get-tuple-element.24), channel_id=1, source_target_pairs={{0,20},{4,16},{8,28},{12,24},{16,4},{20,0},{24,12},{28,8},{1,21},{... | collective-permute-start | bytes 1572872 | tf_op jit(solution)/shard_map/ppermute | solution.py:593
  12.7 25.5 %collective-permute-start.2 = (bf16[8,16,16,128]{3,2,1,0:T(8,128)(2,1)}, bf16[8,16,16,128]{3,2,1,0:T(8,128)(2,1)}, u32[]{:S(2)}, u32[]{:S(2)}) collective-permute-start(bf16[8,16,16,128]{3,2,1,0:T(8,128)(2,1)} %get-tuple-element.25), channel_id=1, source_target_pairs={{0,24},{4,28},{8,16},{12,20},{16,8},{20,12},{24,0},{28,4},{1,25},{... | collective-permute-start | bytes 1572872 | tf_op jit(solution)/shard_map/ppermute | solution.py:593
  13.9 24.3 %collective-permute-start.3 = (bf16[8,16,16,128]{3,2,1,0:T(8,128)(2,1)}, bf16[8,16,16,128]{3,2,1,0:T(8,128)(2,1)}, u32[]{:S(2)}, u32[]{:S(2)}) collective-permute-start(bf16[8,16,16,128]{3,2,1,0:T(8,128)(2,1)} %get-tuple-element.26), channel_id=1, source_target_pairs={{0,28},{4,24},{8,20},{12,16},{16,12},{20,8},{24,4},{28,0},{1,29},{... | collective-permute-start | bytes 1572872 | tf_op jit(solution)/shard_map/ppermute | solution.py:593
  14.5 1.2 %copy-start.8 = (f32[3,192]{1,0:T(4,128)S(1)}, f32[3,192]{1,0:T(4,128)}, u32[]{:S(2)}) copy-start(f32[3,192]{1,0:T(4,128)} %param.13) | copy-start | bytes 6916
  15.8 1.0 copy-start.1
  17.8 8.2 %copy-start.7 = (bf16[2,8,32,16]{2,3,1,0:T(8,128)(2,1)S(1)}, bf16[2,8,32,16]{2,3,1,0:T(8,128)(2,1)}, u32[]{:S(2)}) copy-start(bf16[2,8,32,16]{2,3,1,0:T(8,128)(2,1)} %param.11) | copy-start | bytes 49156
  26.0 1.6 %copy-start.3 = (bf16[3,768,192]{1,2,0:T(8,128)(2,1)S(1)}, bf16[3,768,192]{1,2,0:T(8,128)(2,1)}, u32[]{:S(2)}) copy-start(bf16[3,768,192]{1,2,0:T(8,128)(2,1)} %param.15) | copy-start | bytes 2654212
  26.9 2.2 %copy-start.2 = (bf16[3,192,768]{2,1,0:T(8,128)(2,1)S(1)}, bf16[3,192,768]{2,1,0:T(8,128)(2,1)}, u32[]{:S(2)}) copy-start(bf16[3,192,768]{2,1,0:T(8,128)(2,1)} %param.14) | copy-start | bytes 2654212
  31.7 6.5 %copy-start = (bf16[8,16,16,128]{3,2,1,0:T(8,128)(2,1)}, bf16[8,16,16,128]{3,2,1,0:T(8,128)(2,1)S(1)}, u32[]{:S(2)}) copy-start(bf16[8,16,16,128]{3,2,1,0:T(8,128)(2,1)S(1)} %collective-permute-done.rest_1_) | copy-start | bytes 1572868
  44.2 13.1 %collective-permute-start.4 = (bf16[6,96,128]{2,1,0:T(8,128)(2,1)}, bf16[6,96,128]{2,1,0:T(8,128)(2,1)S(1)}, u32[]{:S(2)}, u32[]{:S(2)}) collective-permute-start(bf16[6,96,128]{2,1,0:T(8,128)(2,1)} %get-tuple-element.33), channel_id=1, source_target_pairs={{0,1},{1,2},{2,3},{4,5},{5,6},{6,7},{8,9},{9,10},{10,11},{12,13},{... | collective-permute-start | bytes 442376 | tf_op jit(solution)/shard_map/ppermute | solution.py:584
  47.7 9.6 %collective-permute-start.5 = (bf16[6,96,128]{2,1,0:T(8,128)(2,1)}, bf16[6,96,128]{2,1,0:T(8,128)(2,1)S(1)}, u32[]{:S(2)}, u32[]{:S(2)}) collective-permute-start(bf16[6,96,128]{2,1,0:T(8,128)(2,1)} %get-tuple-element.34), channel_id=1, source_target_pairs={{1,0},{2,1},{3,2},{5,4},{6,5},{7,6},{9,8},{10,9},{11,10},{13,12},{... | collective-permute-start | bytes 442376 | tf_op jit(solution)/shard_map/ppermute | solution.py:585
  57.3 0.7 copy-start.5
  57.3 0.7 copy-start.6

commit v4 on v2

--- a/solution.py
+++ b/solution.py
@@ -11,6 +11,7 @@
 LG = 16
 LN = 128
 bf, f32 = jnp.bfloat16, jnp.float32
+HALO = 3
 AHEAD = 3
 PARAMS = pltpu.CompilerParams(vmem_limit_bytes=56 * 2**20)
 
@@ -127,9 +128,9 @@
         for g in range(ng):
             zs[g, j] = zz[g]
         for g in range(mixed, ng):
-            for r in range(3):
+            for r in range(2 * HALO):
                 top_ref[r, pl.ds((g - mixed) * nj + j, 1), :] = zz[g][r:r + 1].astype(f32)
-                bot_ref[r, pl.ds((g - mixed) * nj + j, 1), :] = zz[g][rows - 3 + r:rows - 2 + r].astype(f32)
+                bot_ref[r, pl.ds((g - mixed) * nj + j, 1), :] = zz[g][rows - 2 * HALO + r:rows - 2 * HALO + r + 1].astype(f32)
         zcopy(j).start()
 
     @pl.loop(0, hold)
@@ -157,7 +158,7 @@
     vm = pl.BlockSpec(memory_space=VM)
     sm = pl.BlockSpec(memory_space=pltpu.SMEM)
     hbm = pl.BlockSpec(memory_space=pl.ANY)
-    edge = jax.ShapeDtypeStruct((3, (ng - mixed) * nj, LN), f32)
+    edge = jax.ShapeDtypeStruct((2 * HALO, (ng - mixed) * nj, LN), f32)
     return pl.pallas_call(
         functools.partial(pack_kernel, mixed=mixed, tiles=tiles),
         out_shape=(jax.ShapeDtypeStruct((ng, nj, rows, LN), bf), edge, edge)
@@ -258,9 +259,10 @@
             ocopy(g).start()
             return
         for j in range(nj):
-            for r in range(3):
+            for r in range(2 * HALO):
+                low = rows - 2 * HALO + r
                 top_ref[r, pl.ds(g * nj + j, 1), :] = new[j, r:r + 1].astype(f32)
-                bot_ref[r, pl.ds(g * nj + j, 1), :] = new[j, rows - 3 + r:rows - 2 + r].astype(f32)
+                bot_ref[r, pl.ds(g * nj + j, 1), :] = new[j, low:low + 1].astype(f32)
 
     if edges:
         top_ref[:, mixed * nj:, :] = etop_ref[...]
@@ -281,7 +283,7 @@
     vm = pl.BlockSpec(memory_space=VM)
     sm = pl.BlockSpec(memory_space=pltpu.SMEM)
     hbm = pl.BlockSpec(memory_space=pl.ANY)
-    edge = jax.ShapeDtypeStruct((3, ng * nj, LN), bf)
+    edge = jax.ShapeDtypeStruct((2 * HALO, ng * nj, LN), bf)
     here = 32 if edges else rows
     return pl.pallas_call(
         functools.partial(mix_kernel, mixed=mixed, tiles=tiles, edges=edges),
@@ -304,14 +306,17 @@
     )(pairs, place, z, w, *gots, *ends)
 
 
-def band_kernel(e_ref, w_ref):
+def band_kernel(place, e_ref, w_ref):
     delta = lax.broadcasted_iota(jnp.int32, (LG, LN), 0) == lax.broadcasted_iota(jnp.int32, (LG, LN), 1) % LG
     chunk = lax.broadcasted_iota(jnp.int32, (8, LN), 1) // LG
     zero = jnp.zeros((LG, LN), bf)
 
-    @pl.loop(0, e_ref.shape[0])
+    ng = e_ref.shape[1]
+    first = jnp.where(place[0] == 0, 0, 2)
+
+    @pl.loop(0, 2 * ng)
     def _(g):
-        e = e_ref[g]
+        e = e_ref[jnp.where(g < ng, first, 1), jnp.where(g < ng, g, g - ng)]
         for pos, jr in enumerate(list(range(12)) + list(range(-4, 0))):
             s = jr - 3
             r = lroll(e, s * LG)
@@ -324,89 +329,49 @@
                     w_ref[g, row:row + LG] = jnp.where(delta, jnp.broadcast_to(r[k:k + 1], (LG, LN)), 0.0).astype(bf)
 
 
-def band(e):
+def band(place, e):
     vm = pl.BlockSpec(memory_space=VM)
-    n = e.shape[0]
+    n = 2 * e.shape[1]
     return pl.pallas_call(
         band_kernel,
         out_shape=jax.ShapeDtypeStruct((n, 1792, LN), bf),
-        in_specs=[vm], out_specs=vm,
+        in_specs=[pl.BlockSpec(memory_space=pltpu.SMEM), vm], out_specs=vm,
         cost_estimate=pl.CostEstimate(flops=10**9, bytes_accessed=n * 1792 * LN * 4, transcendentals=0),
         compiler_params=PARAMS,
         name="band",
-    )(e)
-
-
-def block_kernel(*refs, parts, layer, want_out, want_z):
-    z_hbm, rest = refs[:parts], list(refs[parts:])
-    top_ref, bot_ref, fac_ref, w_hbm, gain_ref, wi_hbm, woe_hbm, woo_hbm = rest[:8]
-    rest = rest[8:]
-    out_hbm = rest.pop(0) if want_out else None
-    outz_hbm, otop_ref, obot_ref = (rest.pop(0) for _ in range(3)) if want_z else (None,) * 3
-    zs, zf, lhs, wt, spr, ssum, nrm, xe, xo, upd, out, outz, wi_ref, woe_ref, woo_ref, tops, bots, zsem, wsem, osem, msem = rest
+    )(place, e)
+
+
+def blocks_kernel(place, fac_ref, zc_hbm, z_hbm, top_ref, bot_ref, w_hbm, gain_ref, wi_hbm, woe_hbm, woo_hbm, out_hbm,
+                  zs, zn, zf, lhs, wt, spr, ssum, nrm, upd, out, wi_ref, woe_ref, woo_ref, tops, bots, zsem, wsem, osem, msem):
     ng, nj, rows, _ = zs.shape
     hr = rows // 2
     pad = 8
+    ends = (-2, -1, hr, hr + 1)
     count = ng * LG
-    npair = xe.shape[0] // rows
+    npair = PC // 2
     per = 3 * npair * LN
+    mixed = zc_hbm.shape[0]
+    which = jnp.where(place[0] == 0, 0, 2), 1
 
     def zcopy(g, source):
         return pltpu.make_async_copy(source.at[g], zs.at[g], zsem.at[g])
 
-    def wcopy(g):
+    def wcopy(g, layer):
         return pltpu.make_async_copy(w_hbm.at[layer * ng + g], wt.at[g], wsem.at[g])
 
+    def mcopies(layer):
+        pairs = (wi_hbm, wi_ref), (woe_hbm, woe_ref), (woo_hbm, woo_ref)
+        return [pltpu.make_async_copy(a.at[which[layer]], b.at[layer], msem.at[layer, i]) for i, (a, b) in enumerate(pairs)]
+
     def fetch(g):
-        for n, source in enumerate(z_hbm):
-            inside = g < z_hbm[0].shape[0]
-            if len(z_hbm) > 1:
-                pl.when(inside if n == 0 else jnp.logical_not(inside))(zcopy(g, source).start)
-            else:
-                zcopy(g, source).start()
-        wcopy(g).start()
-
-    for g in range(AHEAD):
-        fetch(jnp.int32(g))
-    weights = [pltpu.make_async_copy(a, b, msem.at[i])
-               for i, (a, b) in enumerate(((wi_hbm, wi_ref), (woe_hbm, woe_ref), (woo_hbm, woo_ref)))]
-    ssum[...] = jnp.zeros_like(ssum)
-
-    @pl.loop(0, ng)
-    def _(g):
-        pl.when(g + AHEAD < ng)(lambda: fetch(g + AHEAD))
-
-        @pl.when(g == ng // 2)
-        def _():
-            for c in weights:
-                c.start()
-        zcopy(g, z_hbm[-1]).wait()
-        wcopy(g).wait()
-
-        for j in range(nj):
-            zf[j, pl.ds(pad, rows), :] = zs[g, j].astype(f32)
-        for r in range(3):
-            hs = pl.ds(pl.multiple_of(g * nj, nj), nj)
-            zf[:, pad - 3 + r, :] = top_ref[r, hs, :].astype(f32)
-            zf[:, pad + rows + r, :] = bot_ref[r, hs, :].astype(f32)
-        m64 = lane_bit((hr, LN), 64)
-        zero = jnp.zeros((hr, LN), bf)
-        for a in range(8):
-            v = [zf[j, pl.ds(pad - 3 + a, hr, stride=2), :].astype(bf) for j in range(nj)]
-            for j in range(nj):
-                nxt = v[j + 1] if j + 1 < nj else zero
-                prv = v[j - 1] if j > 0 else zero
-                lhs[j * hr:(j + 1) * hr, a * 256:a * 256 + LN] = v[j]
-                lhs[j * hr:(j + 1) * hr, a * 256 + LN:a * 256 + 256] = jnp.where(m64, nxt, prv)
-
-        band_g, zero_g = wt[g], jnp.zeros((256, LN), bf)
-        rhs = jnp.concatenate([jnp.concatenate([band_g, zero_g], 0), jnp.concatenate([zero_g, band_g], 0)], 1)
-        sp = jnp.dot(lhs[...], rhs, preferred_element_type=f32)
-        spr[g] = sp
-        ssum[...] += sp
-
-    for c in weights:
-        c.wait()
+        pl.when(g < mixed)(lambda: zcopy(g, zc_hbm).start())
+        pl.when(g >= mixed)(lambda: zcopy(g, z_hbm).start())
+        wcopy(g, 0).start()
+
+    def outcopy(j):
+        return pltpu.make_async_copy(out.at[j], out_hbm.at[:, pl.ds(pl.multiple_of(j * per, LN), per)], osem.at[j])
+
     ones = (lax.broadcasted_iota(jnp.int32, (256, 256), 0) // LG == lax.broadcasted_iota(jnp.int32, (256, 256), 1) // LG)
     ones = ones.astype(f32).astype(bf)
 
@@ -415,122 +380,179 @@
         lo = (s - hi.astype(f32)).astype(bf)
         return (jnp.dot(hi, ones, preferred_element_type=f32) + jnp.dot(lo, ones, preferred_element_type=f32)) * (1.0 / count)
 
-    nrm[...] = lane_mean(ssum[...])
+    for g in range(AHEAD):
+        fetch(jnp.int32(g))
+
+    for layer in range(2):
+        src = (zs, zn)[layer]
+        above, below = ((top_ref, bot_ref), (tops, bots))[layer]
+        have = above.shape[0]
+        many = nj * hr + (4 * nj if layer == 0 else 0)
+        ssum[...] = jnp.zeros_like(ssum)
+
+        @pl.loop(0, ng)
+        def _(g):
+            if layer == 0:
+                pl.when(g + AHEAD < ng)(lambda: fetch(g + AHEAD))
+
+                @pl.when(g == ng // 2)
+                def _():
+                    for c in mcopies(0) + mcopies(1):
+                        c.start()
+                zcopy(g, z_hbm).wait()
+            wcopy(g, layer).wait()
+
+            for j in range(nj):
+                zf[j, pl.ds(pad, rows), :] = src[g, j].astype(f32)
+            hs = pl.ds(pl.multiple_of(g * nj, nj), nj)
+            for r in range(HALO):
+                zf[:, pad - HALO + r, :] = above[have - HALO + r, hs, :].astype(f32)
+                zf[:, pad + rows + r, :] = below[r, hs, :].astype(f32)
+            m64 = lane_bit((hr, LN), 64)
+            zero = jnp.zeros((hr, LN), bf)
+            for a in range(8):
+                v = [zf[j, pl.ds(pad - HALO + a, hr, stride=2), :].astype(bf) for j in range(nj)]
+                for j in range(nj):
+                    nxt = v[j + 1] if j + 1 < nj else zero
+                    prv = v[j - 1] if j > 0 else zero
+                    lhs[j * hr:(j + 1) * hr, a * 256:a * 256 + LN] = v[j]
+                    lhs[j * hr:(j + 1) * hr, a * 256 + LN:a * 256 + 256] = jnp.where(m64, nxt, prv)
+
+            if layer == 0:
+                m64 = lane_bit((nj, LN), 64)
+                sub = lax.broadcasted_iota(jnp.int32, (nj, LN), 0)
+                got = {}
+
+                def row_of(at):
+                    if at not in got:
+                        if 0 <= at < rows:
+                            v = zf[:, pad + at, :]
+                        elif -have <= at < 0:
+                            v = above[at + have, hs, :].astype(f32)
+                        elif rows <= at < rows + have:
+                            v = below[at - rows, hs, :].astype(f32)
+                        else:
+                            v = jnp.zeros((nj, LN), f32)
+                        nxt = jnp.where(sub < nj - 1, pltpu.roll(v, nj - 1, 0), 0.0)
+                        prv = jnp.where(sub > 0, pltpu.roll(v, 1, 0), 0.0)
+                        got[at] = v, jnp.where(m64, nxt, prv)
+                    return got[at]
+                for a in range(8):
+                    for n in range(2):
+                        v = jnp.concatenate([row_of(2 * r - HALO + a)[n] for r in ends], 0).astype(bf)
+                        lhs[nj * hr:many, a * 256 + n * LN:a * 256 + (n + 1) * LN] = v
+            band_g, zero_g = wt[g], jnp.zeros((256, LN), bf)
+            rhs = jnp.concatenate([jnp.concatenate([band_g, zero_g], 0), jnp.concatenate([zero_g, band_g], 0)], 1)
+            sp = jnp.dot(lhs[:many], rhs, preferred_element_type=f32)
+            spr[g, :many] = sp
+            ssum[:many] += sp
+            if layer == 0:
+                wcopy(g, 1).start()
+
+        if layer == 0:
+            for c in mcopies(0) + mcopies(1):
+                c.wait()
+        nrm[:many] = lane_mean(ssum[:many])
+
+        @pl.loop(0, many // 32)
+        def _(n):
+            rs = pl.ds(pl.multiple_of(n * 32, 32), 32)
+            mean = nrm[rs, :]
+            q = jnp.zeros((32, 256), f32)
+            for g in range(ng):
+                c = spr[g, rs, :] - mean
+                q = q + c * c
+            ssum[rs, :] = q
+        ssum[:many] = lax.rsqrt(lane_mean(ssum[:many]) + 1e-06)
+        fac = fac_ref[0, layer]
+        gains = gain_ref[which[layer]]
+
+        def update(js):
+            mean, rstd = nrm[js, :], ssum[js, :]
+            zz = [((spr[g, js, :] - mean) * rstd * gains[g:g + 1, :]).astype(bf) for g in range(ng)]
+            nat = [from_patch([t[:, p * LN:(p + 1) * LN] for t in zz]) for p in range(2)]
+            nat = [jnp.concatenate([a, b], 0) for a, b in zip(*nat)]
+            size = nat[0].shape[0]
+            xe = jnp.concatenate([jnp.concatenate([nat[3 * i], nat[3 * i + 1]], 1) for i in range(npair)], 0)
+            xo = jnp.concatenate([jnp.concatenate([nat[3 * i + 1], nat[3 * i + 2]], 1) for i in range(npair)], 0)
+
+            def mlp(x, wi, wo):
+                h = gelu(jnp.dot(x, wi, preferred_element_type=f32).astype(bf))
+                return jnp.dot(h, wo, preferred_element_type=f32)
+            ue = mlp(xe, wi_ref[layer, 64:, :], woe_ref[layer])
+            uo = mlp(xo, wi_ref[layer, :256, :], woo_ref[layer])
+            res = []
+            for i in range(npair):
+                e, o = ue[i * size:(i + 1) * size], uo[i * size:(i + 1) * size]
+                res += [e[:, :LN], e[:, LN:] + o[:, :LN], o[:, LN:]]
+            return res
+
+        @pl.loop(0, nj)
+        def _(j):
+            for n, val in enumerate(update(pl.ds(pl.multiple_of(j * hr, hr), hr))):
+                for p in range(2):
+                    upd[n, pl.ds(p, hr, stride=2), :] = val[p * hr:(p + 1) * hr]
+            if layer == 0:
+                for g, more in enumerate(to_patch([(fac * upd[n]).astype(bf) for n in range(3 * npair)])):
+                    zn[g, j] = (zs[g, j].astype(f32) + more.astype(f32)).astype(bf)
+            else:
+                own = from_patch([zn[g, j] for g in range(ng)])
+                for n in range(3 * npair):
+                    out[j, :, n * LN:(n + 1) * LN] = (own[n].astype(f32) + fac * upd[n]).astype(bf)
+                outcopy(j).start()
+
+        if layer == 0:
+            more = to_patch([(fac * val).astype(bf) for val in update(pl.ds(nj * hr, 4 * nj))])
+            for g in range(ng):
+                gs = pl.ds(g * nj, nj)
+                for r in range(HALO):
+                    for at, keep, own, to in ((r - HALO, 2, above[have - HALO + r, gs, :], tops), (rows + r, 3, below[r, gs, :], bots)):
+                        n = at % 2 * 4 * nj + ends.index(at // 2) * nj
+                        new = (own.astype(f32) + more[g][n:n + nj].astype(f32)).astype(bf)
+                        to[r, gs, :] = fac_ref[0, keep] * new.astype(f32)
 
     @pl.loop(0, nj)
     def _(j):
-        js = pl.ds(pl.multiple_of(j * hr, hr), hr)
-        mean = nrm[js, :]
-        q = jnp.zeros((hr, 256), f32)
-        for g in range(ng):
-            c = spr[g, js, :] - mean
-            q = q + c * c
-        ssum[js, :] = q
-    ssum[...] = lax.rsqrt(lane_mean(ssum[...]) + 1e-06)
-
-    def outcopy(j):
-        ls = pl.ds(pl.multiple_of(j * per, LN), per)
-        cs = []
-        if want_out:
-            cs.append(pltpu.make_async_copy(out.at[j], out_hbm.at[:, ls], osem.at[0, j]))
-        if want_z:
-            cs.append(pltpu.make_async_copy(outz.at[:, j], outz_hbm.at[:, j], osem.at[1, j]))
-        return cs
-
-    @pl.loop(0, nj)
-    def _(j):
-        js = pl.ds(pl.multiple_of(j * hr, hr), hr)
-
-        mean, rstd = nrm[js, :], ssum[js, :]
-        zz = [((spr[g, js, :] - mean) * rstd * gain_ref[g:g + 1, :]).astype(bf) for g in range(ng)]
-        for p in range(2):
-            nat = from_patch([t[:, p * LN:(p + 1) * LN] for t in zz])
-            for i in range(npair):
-                rs = slice(i * rows + p * hr, i * rows + (p + 1) * hr)
-                xe[rs, :LN] = nat[3 * i]
-                xe[rs, LN:] = nat[3 * i + 1]
-                xo[rs, :LN] = nat[3 * i + 1]
-                xo[rs, LN:] = nat[3 * i + 2]
-
-        def mlp(x, wi, wo):
-            h = gelu(jnp.dot(x, wi, preferred_element_type=f32).astype(bf))
-            return jnp.dot(h, wo, preferred_element_type=f32)
-        ue = mlp(xe[...], wi_ref[64:, :], woe_ref[...])
-        uo = mlp(xo[...], wi_ref[:256, :], woo_ref[...])
-        for i in range(npair):
-            e = ue[i * rows:(i + 1) * rows]
-            o = uo[i * rows:(i + 1) * rows]
-            for t, val in enumerate((e[:, :LN], e[:, LN:] + o[:, :LN], o[:, LN:])):
-                for p in range(2):
-                    upd[3 * i + t, pl.ds(p, hr, stride=2), :] = val[p * hr:(p + 1) * hr]
-
-        fac = fac_ref[0, 0]
-        if want_out:
-            own = from_patch([zs[g, j] for g in range(ng)])
-            for n in range(3 * npair):
-                out[j, :, n * LN:(n + 1) * LN] = (own[n].astype(f32) + fac * upd[n]).astype(bf)
-        if want_z:
-            for g, part_of in enumerate(to_patch([(fac * upd[n]).astype(bf) for n in range(3 * npair)])):
-                zz = (zs[g, j].astype(f32) + part_of.astype(f32)).astype(bf)
-                outz[g, j] = zz
-                for r in range(3):
-                    tops[r, pl.ds(g * nj + j, 1), :] = zz[r:r + 1].astype(f32)
-                    bots[r, pl.ds(g * nj + j, 1), :] = zz[rows - 3 + r:rows - 2 + r].astype(f32)
-        for c in outcopy(j):
-            c.start()
-
-    if want_z:
-        otop_ref[...] = tops[...].astype(bf)
-        obot_ref[...] = bots[...].astype(bf)
-
-    @pl.loop(0, nj)
-    def _(j):
-        for c in outcopy(j):
-            c.wait()
-
-
-def block(zs, top, bot, fac, w, gain, wi, woe, woo, layer=0, want_out=True, want_z=True):
-    ng, nj, rows, _ = zs[-1].shape
+        outcopy(j).wait()
+
+
+def blocks(place, fac, zc, z, top, bot, w, gain, wi, woe, woo):
+    ng, nj, rows, _ = z.shape
     hr = rows // 2
+    many = nj * hr + 4 * nj
     per = ng * LG * PC
     vm = pl.BlockSpec(memory_space=VM)
+    sm = pl.BlockSpec(memory_space=pltpu.SMEM)
     hbm = pl.BlockSpec(memory_space=pl.ANY)
-    shapes = []
-    if want_out:
-        shapes.append(jax.ShapeDtypeStruct((rows, nj * per), bf))
-    if want_z:
-        edge = jax.ShapeDtypeStruct(top.shape, bf)
-        shapes += [jax.ShapeDtypeStruct((ng, nj, rows, LN), bf), edge, edge]
     return pl.pallas_call(
-        functools.partial(block_kernel, parts=len(zs), layer=layer, want_out=want_out, want_z=want_z),
-        out_shape=tuple(shapes),
-        in_specs=[hbm] * len(zs) + [vm, vm, pl.BlockSpec(memory_space=pltpu.SMEM), hbm, vm, hbm, hbm, hbm],
-        out_specs=((hbm,) if want_out else ()) + ((hbm, vm, vm) if want_z else ()),
+        blocks_kernel,
+        out_shape=jax.ShapeDtypeStruct((rows, nj * per), bf),
+        in_specs=[sm, sm, hbm, hbm, vm, vm, hbm, vm, hbm, hbm, hbm],
+        out_specs=hbm,
         scratch_shapes=[
             VM((ng, nj, rows, LN), bf),
+            VM((ng, nj, rows, LN), bf),
             VM((nj, rows + 16, LN), f32),
-            VM((nj * hr, 2048), bf),
+            VM((many, 2048), bf),
             VM((ng, 1792, LN), bf),
-            VM((ng, nj * hr, 256), f32),
-            VM((nj * hr, 256), f32),
-            VM((nj * hr, 256), f32),
-            VM((4 * rows, 256), bf), VM((4 * rows, 256), bf),
+            VM((ng, many, 256), f32),
+            VM((many, 256), f32),
+            VM((many, 256), f32),
             VM((12, rows, LN), f32),
-            VM((nj, rows, per), bf) if want_out else VM((8, LN), bf),
-            VM((ng, nj, rows, LN), bf) if want_z else VM((8, LN), bf),
-            VM(wi.shape, bf),
-            VM(woe.shape, bf),
-            VM(woo.shape, bf),
-            VM(top.shape, f32),
-            VM(top.shape, f32),
+            VM((nj, rows, per), bf),
+            VM((2,) + wi.shape[1:], bf),
+            VM((2,) + woe.shape[1:], bf),
+            VM((2,) + woo.shape[1:], bf),
+            VM((HALO,) + top.shape[1:], f32),
+            VM((HALO,) + top.shape[1:], f32),
             pltpu.SemaphoreType.DMA((ng,)),
             pltpu.SemaphoreType.DMA((ng,)),
-            pltpu.SemaphoreType.DMA((2, nj)),
-            pltpu.SemaphoreType.DMA((3,)),
+            pltpu.SemaphoreType.DMA((nj,)),
+            pltpu.SemaphoreType.DMA((2, 3)),
         ],
         compiler_params=PARAMS,
-        name="block",
-    )(*zs, top, bot, fac, w, gain, wi, woe, woo)
+        name="blocks",
+    )(place, fac, zc, z, top, bot, w, gain, wi, woe, woo)
 
 
 def prep_all(depth, gain, inner, outer):
@@ -571,17 +593,14 @@
     z, etop, ebot, *outs = pack(pairs, place, state[0, 0], tiles, mix_weight.shape[1], norm_gain.shape[1] // LG)
     gots = exchange(outs)
     e, *weights = prep_all(depth_weight, norm_gain, inner_weight, outer_weight)
-    which = jnp.where(section == 0, 0, 2)
     wmix = jnp.tile(pick(mix_weight, section).astype(f32), (1, 1, PC))
-    bands = band(jnp.concatenate([pick(e, which), e[1]]))
-    gots, bands = lax.optimization_barrier((gots, bands))
+    factor = jnp.where(section == 0, 1.0, wet[0].astype(f32))
+    inside = jnp.stack([place[2] > 0, place[2] < lax.axis_size("row") - 1]).astype(f32)
+    factors = jnp.concatenate([jnp.stack([factor, (section == 0).astype(f32)]), inside]).reshape(1, 4)
+    gots, bands, weights, wmix, factors = lax.optimization_barrier((gots, band(place, e), weights, wmix, factors))
     top, bot = halo(*mix(pairs, place, z, wmix, gots, (etop, ebot)))
     zc = mix(pairs, place, z, wmix, gots)
-    factor = jnp.where(section == 0, 1.0, wet[0].astype(f32)).reshape(1, 1)
-    z, top, bot = block([zc, z], top, bot, factor, bands, *(pick(w, which) for w in weights), want_out=False)
-    top, bot = halo(top, bot)
-    factor = jnp.where(section == 0, 1.0, 0.0).reshape(1, 1)
-    out, = block([z], top, bot, factor, bands, *(w[1] for w in weights), layer=1, want_z=False)
+    out = blocks(place, factors, zc, z, top, bot, bands, *weights)
     return out[None, None]
 
 

time: 122 us -> 110 us (0.902)
  starting transfers between devices: 14.9 us -> 9.12 us
  waiting for transfers between devices: 10.6 us -> 6.92 us
  Pallas kernels: 83.3 us -> 81.4 us
  local copies, waits for them, and re-layouts: 10.4 us -> 8.77 us
    ppermute x2 -> x1, starting transfers between devices: 7.96 us -> 3.49 us  [halo(): lax.ppermute(bot, 'row', [(i, i + 1) for i in range(n - 1)])]
    ppermute x2 -> x1, waiting for transfers between devices: 4.18 us -> 0.01 us  [halo(): lax.ppermute(top, 'row', [(i + 1, i) for i in range(n - 1)])]
    squeeze x5 -> x0, local copies, waits for them, and re-layouts: 3.32 us -> none  [the longest x2 2.54 us: on_device(): w[1]]
    pad x0 -> x2, local copies, waits for them, and re-layouts: none -> 3.15 us  [the longest x1 1.94 us: prep_all(): woo = jnp.pad(outer, ((0, 0), (0, 0), (64, 0)))]
    pallas_call x2 -> x1, Pallas kernels: 53.5 us -> 51.3 us  [blocks(): pl.pallas_call(blocks_kernel, out_shape=jax.ShapeDtypeStruct((rows, nj *...]
    ppermute x2 -> x1, starting transfers between devices: 2.58 us -> 1.29 us  [halo(): lax.ppermute(top, 'row', [(i + 1, i) for i in range(n - 1)])]
    unnamed x23 -> x19, local copies, waits for them, and re-layouts: 2.85 us -> 1.93 us
  transfers between devices with their start and end apart: 8 -> 6, of which waited for: 3 -> 1; matrix products, arithmetic and copies ran while one was open for 7% -> 8% of each run, Pallas kernels for 12% -> 14%
where the time goes in v4:
time: 110 us; the launch traced here: 109 us
  Pallas kernels  81.4 us (74%)
  starting transfers between devices  9.12 us (8%)
  local copies, waits for them, and re-layouts  8.77 us (8%)
  waiting for transfers between devices  6.92 us (6%)
  other arithmetic  2.3 us (2%)
    pallas_call x1, Pallas kernels, blocks(): pl.pallas_call(blocks_kernel, out_shape=jax.ShapeDtypeStruct((rows, nj *...  51.3 us
    pallas_call x2, Pallas kernels, mix(): pl.pallas_call(functools.partial(mix_kernel, mixed=mixed, tiles=tiles, ed...  12.8 us
    pallas_call x1, Pallas kernels, pack(): pl.pallas_call(functools.partial(pack_kernel, mixed=mixed, tiles=tiles),...  8.97 us
    pallas_call x1, Pallas kernels, band(): pl.pallas_call(band_kernel, out_shape=jax.ShapeDtypeStruct((n, 1792, LN),...  8.32 us
    ppermute x4, waiting for transfers between devices, exchange(): lax.ppermute(o, ('comp', 'tile'), [(s * n + t, (1 - s) * n + (t ^ d)) for...  6.91 us
    ppermute x4, starting transfers between devices, exchange(): lax.ppermute(o, ('comp', 'tile'), [(s * n + t, (1 - s) * n + (t ^ d)) for...  4.34 us
    ppermute x1, starting transfers between devices, halo(): lax.ppermute(bot, 'row', [(i, i + 1) for i in range(n - 1)])  3.49 us
  transfers between devices with their start and end apart: 6, of which 1 were waited for; matrix products, arithmetic and copies ran while one was open for 8% of the time, Pallas kernels for 14%

profile of v4, /device:TPU:0, one launch (start us, length us, event | category | flops | bytes accessed | tf_op | source)
XLA Modules:
  0.0 109.4 jit_solution(10859848981799344677)
XLA Ops:
  0.0 0.7 pad_add_fusion.place
  0.7 9.0 %pack.1 = (bf16[12,8,128,128]{3,2,1,0:T(8,128)(2,1)}, f32[6,32,128]{2,1,0:T(8,128)}, f32[6,32,128]{2,1,0:T(8,128)}, bf16[8,16,16,128]{3,2,1,0:T(8,128)(2,1)}, bf...) custom-call(s32[2,512]{1,0:T(2,128)} %pairs.5, ...), custom_call_target="tpu_custom_call" | custom-call | tf_op jit(solution)/shard_map/pack/pallas_call | solution.py:162
  9.6 0.5 collective-permute-start
  10.2 2.6 %collective-permute-start.1 = (bf16[8,16,16,128]{3,2,1,0:T(8,128)(2,1)}, bf16[8,16,16,128]{3,2,1,0:T(8,128)(2,1)}, u32[]{:S(2)}, u32[]{:S(2)}) collective-permute-start(bf16[8,16,16,128]{3,2,1,0:T(8,128)(2,1)} %get-tuple-element.26), channel_id=1, source_target_pairs={{0,20},{4,16},{8,28},{12,24},{16,4},{20,0},{24,12},{28,8},{1,21},{... | collective-permute-start | bytes 1572872 | tf_op jit(solution)/shard_map/ppermute | solution.py:582
  12.8 1.2 %collective-permute-start.2 = (bf16[8,16,16,128]{3,2,1,0:T(8,128)(2,1)}, bf16[8,16,16,128]{3,2,1,0:T(8,128)(2,1)}, u32[]{:S(2)}, u32[]{:S(2)}) collective-permute-start(bf16[8,16,16,128]{3,2,1,0:T(8,128)(2,1)} %get-tuple-element.27), channel_id=1, source_target_pairs={{0,24},{4,28},{8,16},{12,20},{16,8},{20,12},{24,0},{28,4},{1,25},{... | collective-permute-start | bytes 1572872 | tf_op jit(solution)/shard_map/ppermute | solution.py:582
  14.1 1.0 broadcast_multiply_fusion
  15.1 0.5 reshape.24
  15.6 0.4 copy.13
  16.0 1.0 reshape.25.e_ref
  17.0 8.3 %band.1.w_hbm = bf16[24,1792,128]{2,1,0:T(8,128)(2,1)} custom-call(s32[3]{0:T(128)} %pad_add_fusion.place, f32[3,12,8,128]{3,2,1,0:T(8,128)} %reshape.25.e_ref), custom_call_target="tpu_custom_call" | custom-call | flops 1000000000 | bytes 22020096 | tf_op jit(solution)/shard_map/band/pallas_call | solution.py:335
  26.1 0.8 tile.20.gain_ref
  26.9 0.6 copy.14
  27.6 1.2 %pad.17.wi_hbm = bf16[3,320,768]{2,1,0:T(8,128)(2,1)} pad(bf16[3,192,768]{2,1,0:T(8,128)(2,1)S(1)} %copy-done, bf16[]{:T(256)} %constant.25.clone.1), padding=0_0x64_64x0_0 | pad | bytes 2359298 | tf_op jit(solution)/shard_map/jit(_pad)/pad | solution.py:564
  28.9 0.6 maximum_bitcast_fusion.fac_ref
  29.4 1.9 %fusion = (bf16[3,768,256]{2,1,0:T(8,128)(2,1)}, bf16[3,768,256]{2,1,0:T(8,128)(2,1)}) fusion(bf16[3,768,192]{2,1,0:T(8,128)(2,1)S(1)} %copy.14), kind=kLoop, calls=%fused_computation.5 | loop fusion | bytes 3244032 | tf_op jit(solution)/shard_map/jit(_pad)/pad | solution.py:566
  31.4 6.9 %collective-permute-done.2.rest_3_ = bf16[8,16,16,128]{3,2,1,0:T(8,128)(2,1)} collective-permute-done((bf16[8,16,16,128]{3,2,1,0:T(8,128)(2,1)}, bf16[8,16,16,128]{3,2,1,0:T(8,128)(2,1)}, u32[]{:S(2)}, u32[]{:S(2)}) %collective-permute-start.2) | collective-permute-done | bytes 524320 | tf_op jit(solution)/shard_map/ppermute | solution.py:582
  38.3 0.8 copy.16.rest_0_
  39.2 6.0 %mix_edges.1 = (bf16[6,96,128]{2,1,0:T(8,128)(2,1)}, bf16[6,96,128]{2,1,0:T(8,128)(2,1)}) custom-call(s32[2,512]{1,0:T(2,128)} %pairs.5, s32[3]{0:T(128)} %pad_add_fusion.place, bf16[12,8,128,128]{3,2,1,0:T(8,128)(2,1)} %get-tuple-element.30.z_hbm, f32[8,32,128]{2,1,0:T(8,128)} %copy.16.rest_0_, bf16[8,16,16,128]{3,2,1,0:T(8,128)(2,1)} %copy-done.1, ...), custom_call_target="tpu_custom_call" | custom-call | flops 1000000000 | bytes 8388608 | tf_op jit(solution)/shard_map/mix_edges/pallas_call | solution.py:288
  45.2 3.5 %collective-permute-start.4 = (bf16[6,96,128]{2,1,0:T(8,128)(2,1)}, bf16[6,96,128]{2,1,0:T(8,128)(2,1)S(1)}, u32[]{:S(2)}, u32[]{:S(2)}) collective-permute-start(bf16[6,96,128]{2,1,0:T(8,128)(2,1)} %get-tuple-element.38), channel_id=1, source_target_pairs={{0,1},{1,2},{2,3},{4,5},{5,6},{6,7},{8,9},{9,10},{10,11},{12,13},{... | collective-permute-start | bytes 442376 | tf_op jit(solution)/shard_map/ppermute | solution.py:573
  48.7 1.3 %collective-permute-start.5 = (bf16[6,96,128]{2,1,0:T(8,128)(2,1)}, bf16[6,96,128]{2,1,0:T(8,128)(2,1)S(1)}, u32[]{:S(2)}, u32[]{:S(2)}) collective-permute-start(bf16[6,96,128]{2,1,0:T(8,128)(2,1)} %get-tuple-element.39), channel_id=1, source_target_pairs={{1,0},{2,1},{3,2},{5,4},{6,5},{7,6},{9,8},{10,9},{11,10},{13,12},{... | collective-permute-start | bytes 442376 | tf_op jit(solution)/shard_map/ppermute | solution.py:574
  50.0 6.8 %mix.1.zc_hbm = bf16[8,8,128,128]{3,2,1,0:T(8,128)(2,1)} custom-call(s32[2,512]{1,0:T(2,128)} %pairs.5, s32[3]{0:T(128)} %pad_add_fusion.place, bf16[12,8,128,128]{3,2,1,0:T(8,128)(2,1)} %get-tuple-element.30.z_hbm, f32[8,32,128]{2,1,0:T(8,128)} %copy.16.rest_0_, bf16[8,16,16,128]{3,2,1,0:T(8,128)(2,1)} %copy-done.1, ...), custom_call_target="tpu_custom_call" | custom-call | flops 1000000000 | bytes 8388608 | tf_op jit(solution)/shard_map/mix/pallas_call | solution.py:288
  56.8 0.6 copy-done.5
  57.5 0.7 copy-done.6
  58.1 51.3 %blocks.1 = bf16[128,12288]{1,0:T(8,128)(2,1)} custom-call(s32[3]{0:T(128)} %pad_add_fusion.place, f32[1,4]{1,0:T(1,128)} %maximum_bitcast_fusion.fac_ref, bf16[8,8,128,128]{3,2,1,0:T(8,128)(2,1)} %mix.1.zc_hbm, bf16[12,8,128,128]{3,2,1,0:T(8,128)(2,1)} %get-tuple-element.30.z_hbm, bf16[6,96,128]{2,1,0:T(8,128)(2,1)} %copy-done.5, ...), custom_call_target="tpu_custom_call" | custom-call | tf_op jit(solution)/shard_map/blocks/pallas_call | solution.py:527
  (29 shorter events, 0.4 us)
Async XLA Ops:
  0.7 13.3 %copy-start.4 = (f32[3,7,7,192]{3,2,1,0:T(8,128)S(1)}, f32[3,7,7,192]{3,2,1,0:T(8,128)}, u32[]{:S(2)}) copy-start(f32[3,7,7,192]{3,2,1,0:T(8,128)} %param.12) | copy-start | bytes 338692
  0.7 13.5 %copy-start.2 = (bf16[3,192,768]{2,1,0:T(8,128)(2,1)S(1)}, bf16[3,192,768]{2,1,0:T(8,128)(2,1)}, u32[]{:S(2)}) copy-start(bf16[3,192,768]{2,1,0:T(8,128)(2,1)} %param.14) | copy-start | bytes 2654212
  9.6 21.8 %collective-permute-start = (bf16[8,16,16,128]{3,2,1,0:T(8,128)(2,1)}, bf16[8,16,16,128]{3,2,1,0:T(8,128)(2,1)S(1)}, u32[]{:S(2)}, u32[]{:S(2)}) collective-permute-start(bf16[8,16,16,128]{3,2,1,0:T(8,128)(2,1)} %get-tuple-element.25), channel_id=1, source_target_pairs={{0,16},{4,20},{8,24},{12,28},{16,0},{20,4},{24,8},{28,12},{1,17},{... | collective-permute-start | bytes 1572872 | tf_op jit(solution)/shard_map/ppermute | solution.py:582
  10.2 21.2 %collective-permute-start.1 = (bf16[8,16,16,128]{3,2,1,0:T(8,128)(2,1)}, bf16[8,16,16,128]{3,2,1,0:T(8,128)(2,1)}, u32[]{:S(2)}, u32[]{:S(2)}) collective-permute-start(bf16[8,16,16,128]{3,2,1,0:T(8,128)(2,1)} %get-tuple-element.26), channel_id=1, source_target_pairs={{0,20},{4,16},{8,28},{12,24},{16,4},{20,0},{24,12},{28,8},{1,21},{... | collective-permute-start | bytes 1572872 | tf_op jit(solution)/shard_map/ppermute | solution.py:582
  12.8 25.5 %collective-permute-start.2 = (bf16[8,16,16,128]{3,2,1,0:T(8,128)(2,1)}, bf16[8,16,16,128]{3,2,1,0:T(8,128)(2,1)}, u32[]{:S(2)}, u32[]{:S(2)}) collective-permute-start(bf16[8,16,16,128]{3,2,1,0:T(8,128)(2,1)} %get-tuple-element.27), channel_id=1, source_target_pairs={{0,24},{4,28},{8,16},{12,20},{16,8},{20,12},{24,0},{28,4},{1,25},{... | collective-permute-start | bytes 1572872 | tf_op jit(solution)/shard_map/ppermute | solution.py:582
  14.0 24.3 %collective-permute-start.3 = (bf16[8,16,16,128]{3,2,1,0:T(8,128)(2,1)}, bf16[8,16,16,128]{3,2,1,0:T(8,128)(2,1)}, u32[]{:S(2)}, u32[]{:S(2)}) collective-permute-start(bf16[8,16,16,128]{3,2,1,0:T(8,128)(2,1)} %get-tuple-element.28), channel_id=1, source_target_pairs={{0,28},{4,24},{8,20},{12,16},{16,12},{20,8},{24,4},{28,0},{1,29},{... | collective-permute-start | bytes 1572872 | tf_op jit(solution)/shard_map/ppermute | solution.py:582
  17.0 9.1 %copy-start.8 = (f32[3,192]{1,0:T(4,128)S(1)}, f32[3,192]{1,0:T(4,128)}, u32[]{:S(2)}) copy-start(f32[3,192]{1,0:T(4,128)} %param.13) | copy-start | bytes 6916
  17.0 10.0 %copy-start.3 = (bf16[3,768,192]{1,2,0:T(8,128)(2,1)S(1)}, bf16[3,768,192]{1,2,0:T(8,128)(2,1)}, u32[]{:S(2)}) copy-start(bf16[3,768,192]{1,2,0:T(8,128)(2,1)} %param.15) | copy-start | bytes 2654212
  25.3 2.3 %copy-start = (bf16[3,192,768]{2,1,0:T(8,128)(2,1)S(1)}, bf16[3,192,768]{2,1,0:T(8,128)(2,1)}, u32[]{:S(2)}) copy-start(bf16[3,192,768]{2,1,0:T(8,128)(2,1)} %broadcast_multiply_fusion) | copy-start | bytes 2654212
  27.5 1.9 %copy-start.7 = (bf16[2,8,32,16]{2,3,1,0:T(8,128)(2,1)S(1)}, bf16[2,8,32,16]{2,3,1,0:T(8,128)(2,1)}, u32[]{:S(2)}) copy-start(bf16[2,8,32,16]{2,3,1,0:T(8,128)(2,1)} %param.11) | copy-start | bytes 49156
  31.4 7.8 %copy-start.1 = (bf16[8,16,16,128]{3,2,1,0:T(8,128)(2,1)}, bf16[8,16,16,128]{3,2,1,0:T(8,128)(2,1)S(1)}, u32[]{:S(2)}) copy-start(bf16[8,16,16,128]{3,2,1,0:T(8,128)(2,1)S(1)} %collective-permute-done.rest_1_) | copy-start | bytes 1572868
  45.2 11.6 %collective-permute-start.4 = (bf16[6,96,128]{2,1,0:T(8,128)(2,1)}, bf16[6,96,128]{2,1,0:T(8,128)(2,1)S(1)}, u32[]{:S(2)}, u32[]{:S(2)}) collective-permute-start(bf16[6,96,128]{2,1,0:T(8,128)(2,1)} %get-tuple-element.38), channel_id=1, source_target_pairs={{0,1},{1,2},{2,3},{4,5},{5,6},{6,7},{8,9},{9,10},{10,11},{12,13},{... | collective-permute-start | bytes 442376 | tf_op jit(solution)/shard_map/ppermute | solution.py:573
  48.7 8.2 %collective-permute-start.5 = (bf16[6,96,128]{2,1,0:T(8,128)(2,1)}, bf16[6,96,128]{2,1,0:T(8,128)(2,1)S(1)}, u32[]{:S(2)}, u32[]{:S(2)}) collective-permute-start(bf16[6,96,128]{2,1,0:T(8,128)(2,1)} %get-tuple-element.39), channel_id=1, source_target_pairs={{1,0},{2,1},{3,2},{5,4},{6,5},{7,6},{9,8},{10,9},{11,10},{13,12},{... | collective-permute-start | bytes 442376 | tf_op jit(solution)/shard_map/ppermute | solution.py:574
  56.8 0.7 copy-start.5
  57.5 0.7 copy-start.6

commit v5 on v4

--- a/solution.py
+++ b/solution.py
@@ -12,6 +12,7 @@
 LN = 128
 bf, f32 = jnp.bfloat16, jnp.float32
 HALO = 3
+SIDE = 8
 AHEAD = 3
 PARAMS = pltpu.CompilerParams(vmem_limit_bytes=56 * 2**20)
 
@@ -180,13 +181,13 @@
 
 
 def mix_kernel(pairs, place, z_hbm, *rest, mixed, tiles, edges):
-    w_ref, *rest = rest
+    wm, *rest = rest
     gots, rest = rest[:tiles], rest[tiles:]
     if edges:
         etop_ref, ebot_ref, otop_ref, obot_ref, top_ref, bot_ref, *rest = rest
     else:
         out_hbm, *rest = rest
-    zs, zp, got, wm, count, zsem, gsem, osem = rest
+    zs, zp, got, count, zsem, gsem, osem = rest
     _, nj, rows, _ = zs.shape
     whole = z_hbm.shape[2]
     hold = got.shape[0]
@@ -213,15 +214,6 @@
     for g in range(mixed):
         for c in zcopy(g):
             c.start()
-    block = lax.broadcasted_iota(jnp.int32, (LG, LN), 1) // LG
-
-    @pl.loop(0, mixed)
-    def _(g):
-        for h in range(2):
-            w = w_ref[g, h * LG:(h + 1) * LG, :]
-            for c in range(PC):
-                at = h * LN + c * LG
-                wm[g, at:at + LG] = jnp.where(block == c, w, 0.0).astype(bf)
     for q in range(tiles):
         count[q] = 0
     for c in gcopy:
@@ -246,23 +238,26 @@
         else:
             put(up)
 
-    @pl.loop(0, mixed)
-    def _(g):
-        for c in zcopy(g):
-            c.wait()
-        own = zs[g].reshape(nj * rows, LN)
-        both = jnp.concatenate([own, zp[g].reshape(nj * rows, LN)], 1)
-        new = own.astype(f32) + jnp.dot(both, wm[g], preferred_element_type=f32)
-        new = new.astype(bf).reshape(nj, rows, LN)
-        if not edges:
-            zs[g] = new
-            ocopy(g).start()
-            return
-        for j in range(nj):
-            for r in range(2 * HALO):
-                low = rows - 2 * HALO + r
-                top_ref[r, pl.ds(g * nj + j, 1), :] = new[j, r:r + 1].astype(f32)
-                bot_ref[r, pl.ds(g * nj + j, 1), :] = new[j, low:low + 1].astype(f32)
+    side = 4 if edges else 1
+
+    @pl.loop(0, mixed // side)
+    def _(gg):
+        for s in range(side):
+            g = gg * side + s
+            for c in zcopy(g):
+                c.wait()
+            own = zs[g].reshape(nj * rows, LN)
+            both = jnp.concatenate([own, zp[g].reshape(nj * rows, LN)], 1)
+            new = own.astype(f32) + jnp.dot(both, wm[g], preferred_element_type=f32)
+            new = new.astype(bf).reshape(nj, rows, LN)
+            if not edges:
+                zs[g] = new
+                ocopy(g).start()
+            for j in range(nj if edges else 0):
+                for r in range(2 * HALO):
+                    low = rows - 2 * HALO + r
+                    top_ref[r, pl.ds(g * nj + j, 1), :] = new[j, r:r + 1].astype(f32)
+                    bot_ref[r, pl.ds(g * nj + j, 1), :] = new[j, low:low + 1].astype(f32)
 
     if edges:
         top_ref[:, mixed * nj:, :] = etop_ref[...]
@@ -294,7 +289,6 @@
             VM((mixed, nj, here, LN), bf),
             VM((mixed, nj, here, LN), bf),
             VM((hold,) + gots[0].shape[1:], bf),
-            VM((mixed, 2 * LN, LN), bf),
             pltpu.SMEM((tiles,), jnp.int32),
             pltpu.SemaphoreType.DMA((mixed, 2)),
             pltpu.SemaphoreType.DMA((tiles,)),
@@ -306,11 +300,17 @@
     )(pairs, place, z, w, *gots, *ends)
 
 
-def band_kernel(place, e_ref, w_ref):
+def band_kernel(place, e_ref, mix_ref, w_ref, wm_ref):
     delta = lax.broadcasted_iota(jnp.int32, (LG, LN), 0) == lax.broadcasted_iota(jnp.int32, (LG, LN), 1) % LG
     chunk = lax.broadcasted_iota(jnp.int32, (8, LN), 1) // LG
     zero = jnp.zeros((LG, LN), bf)
 
+    for g in range(mix_ref.shape[0]):
+        for h in range(2):
+            w = mix_ref[g, h * LG:(h + 1) * LG, :]
+            for c in range(PC):
+                at = h * LN + c * LG
+                wm_ref[g, at:at + LG] = jnp.where(lax.broadcasted_iota(jnp.int32, (LG, LN), 1) // LG == c, w, 0.0).astype(bf)
     ng = e_ref.shape[1]
     first = jnp.where(place[0] == 0, 0, 2)
 
@@ -329,17 +329,17 @@
                     w_ref[g, row:row + LG] = jnp.where(delta, jnp.broadcast_to(r[k:k + 1], (LG, LN)), 0.0).astype(bf)
 
 
-def band(place, e):
+def band(place, e, wmix):
     vm = pl.BlockSpec(memory_space=VM)
     n = 2 * e.shape[1]
     return pl.pallas_call(
         band_kernel,
-        out_shape=jax.ShapeDtypeStruct((n, 1792, LN), bf),
-        in_specs=[pl.BlockSpec(memory_space=pltpu.SMEM), vm], out_specs=vm,
+        out_shape=(jax.ShapeDtypeStruct((n, 1792, LN), bf), jax.ShapeDtypeStruct((wmix.shape[0], 2 * LN, LN), bf)),
+        in_specs=[pl.BlockSpec(memory_space=pltpu.SMEM), vm, vm], out_specs=(vm, vm),
         cost_estimate=pl.CostEstimate(flops=10**9, bytes_accessed=n * 1792 * LN * 4, transcendentals=0),
         compiler_params=PARAMS,
         name="band",
-    )(place, e)
+    )(place, e, wmix)
 
 
 def blocks_kernel(place, fac_ref, zc_hbm, z_hbm, top_ref, bot_ref, w_hbm, gain_ref, wi_hbm, woe_hbm, woo_hbm, out_hbm,
@@ -487,19 +487,21 @@
                 res += [e[:, :LN], e[:, LN:] + o[:, :LN], o[:, LN:]]
             return res
 
-        @pl.loop(0, nj)
-        def _(j):
-            for n, val in enumerate(update(pl.ds(pl.multiple_of(j * hr, hr), hr))):
-                for p in range(2):
-                    upd[n, pl.ds(p, hr, stride=2), :] = val[p * hr:(p + 1) * hr]
-            if layer == 0:
-                for g, more in enumerate(to_patch([(fac * upd[n]).astype(bf) for n in range(3 * npair)])):
-                    zn[g, j] = (zs[g, j].astype(f32) + more.astype(f32)).astype(bf)
-            else:
-                own = from_patch([zn[g, j] for g in range(ng)])
-                for n in range(3 * npair):
-                    out[j, :, n * LN:(n + 1) * LN] = (own[n].astype(f32) + fac * upd[n]).astype(bf)
-                outcopy(j).start()
+        @pl.loop(0, nj // SIDE)
+        def _(jj):
+            for s in range(SIDE):
+                j = jj * SIDE + s
+                for n, val in enumerate(update(pl.ds(pl.multiple_of(j * hr, hr), hr))):
+                    for p in range(2):
+                        upd[s, n, pl.ds(p, hr, stride=2), :] = val[p * hr:(p + 1) * hr]
+                if layer == 0:
+                    for g, more in enumerate(to_patch([(fac * upd[s, n]).astype(bf) for n in range(3 * npair)])):
+                        zn[g, j] = (zs[g, j].astype(f32) + more.astype(f32)).astype(bf)
+                else:
+                    own = from_patch([zn[g, j] for g in range(ng)])
+                    for n in range(3 * npair):
+                        out[j, :, n * LN:(n + 1) * LN] = (own[n].astype(f32) + fac * upd[s, n]).astype(bf)
+                    outcopy(j).start()
 
         if layer == 0:
             more = to_patch([(fac * val).astype(bf) for val in update(pl.ds(nj * hr, 4 * nj))])
@@ -538,7 +540,7 @@
             VM((ng, many, 256), f32),
             VM((many, 256), f32),
             VM((many, 256), f32),
-            VM((12, rows, LN), f32),
+            VM((SIDE, 12, rows, LN), f32),
             VM((nj, rows, per), bf),
             VM((2,) + wi.shape[1:], bf),
             VM((2,) + woe.shape[1:], bf),
@@ -597,7 +599,7 @@
     factor = jnp.where(section == 0, 1.0, wet[0].astype(f32))
     inside = jnp.stack([place[2] > 0, place[2] < lax.axis_size("row") - 1]).astype(f32)
     factors = jnp.concatenate([jnp.stack([factor, (section == 0).astype(f32)]), inside]).reshape(1, 4)
-    gots, bands, weights, wmix, factors = lax.optimization_barrier((gots, band(place, e), weights, wmix, factors))
+    gots, (bands, wmix), weights, factors = lax.optimization_barrier((gots, band(place, e, wmix), weights, factors))
     top, bot = halo(*mix(pairs, place, z, wmix, gots, (etop, ebot)))
     zc = mix(pairs, place, z, wmix, gots)
     out = blocks(place, factors, zc, z, top, bot, bands, *weights)

time: 110 us -> 104 us (0.945)
  Pallas kernels: 81.4 us -> 75.6 us
  waiting for transfers between devices: 6.92 us -> 3.61 us
  local copies, waits for them, and re-layouts: 8.77 us -> 11.2 us
    pallas_call x1, Pallas kernels: 51.3 us -> 44.9 us  [blocks(): pl.pallas_call(blocks_kernel, out_shape=jax.ShapeDtypeStruct((rows, nj *...]
    ppermute x4, waiting for transfers between devices: 6.91 us -> 3.61 us  [exchange(): lax.ppermute(o, ('comp', 'tile'), [(s * n + t, (1 - s) * n + (t ^ d)) for...]
    reshape x1, local copies, waits for them, and re-layouts: 0.99 us -> 2.34 us  [prep_all(): e = e.transpose(0, 3, 1, 2, 4).reshape(nl, ng, 8, LN)]
  transfers between devices with their start and end apart: 6 -> 6, of which waited for: 1 -> 1; matrix products, arithmetic and copies ran while one was open for 8% -> 11% of each run, Pallas kernels for 14% -> 15%
where the time goes in v5:
time: 104 us; the launch traced here: 103 us
  Pallas kernels  75.6 us (73%)
  local copies, waits for them, and re-layouts  11.2 us (11%)
  starting transfers between devices  9.3 us (9%)
  waiting for transfers between devices  3.61 us (3%)
  other arithmetic  2.34 us (2%)
  between operations  1.08 us (1%)
    pallas_call x1, Pallas kernels, blocks(): pl.pallas_call(blocks_kernel, out_shape=jax.ShapeDtypeStruct((rows, nj *...  44.9 us
    pallas_call x2, Pallas kernels, mix(): pl.pallas_call(functools.partial(mix_kernel, mixed=mixed, tiles=tiles, ed...  13.3 us
    pallas_call x1, Pallas kernels, pack(): pl.pallas_call(functools.partial(pack_kernel, mixed=mixed, tiles=tiles),...  9.01 us
    pallas_call x1, Pallas kernels, band(): pl.pallas_call(band_kernel, out_shape=(jax.ShapeDtypeStruct((n, 1792, LN)...  8.37 us
    ppermute x4, starting transfers between devices, exchange(): lax.ppermute(o, ('comp', 'tile'), [(s * n + t, (1 - s) * n + (t ^ d)) for...  4.34 us
    ppermute x4, waiting for transfers between devices, exchange(): lax.ppermute(o, ('comp', 'tile'), [(s * n + t, (1 - s) * n + (t ^ d)) for...  3.61 us
    ppermute x1, starting transfers between devices, halo(): lax.ppermute(bot, 'row', [(i, i + 1) for i in range(n - 1)])  3.49 us
    reshape x1, local copies, waits for them, and re-layouts, prep_all(): e = e.transpose(0, 3, 1, 2, 4).reshape(nl, ng, 8, LN)  2.34 us
  transfers between devices with their start and end apart: 6, of which 1 were waited for; matrix products, arithmetic and copies ran while one was open for 11% of the time, Pallas kernels for 15%

profile of v5, /device:TPU:0, one launch (start us, length us, event | category | flops | bytes accessed | tf_op | source)
XLA Modules:
  0.0 103.2 jit_solution(774698185145998086)
XLA Ops:
  0.0 0.7 pad_add_fusion.place
  0.7 9.0 %pack.1 = (bf16[12,8,128,128]{3,2,1,0:T(8,128)(2,1)}, f32[6,32,128]{2,1,0:T(8,128)}, f32[6,32,128]{2,1,0:T(8,128)}, bf16[8,16,16,128]{3,2,1,0:T(8,128)(2,1)}, bf...) custom-call(s32[2,512]{1,0:T(2,128)} %pairs.5, ...), custom_call_target="tpu_custom_call" | custom-call | tf_op jit(solution)/shard_map/pack/pallas_call | solution.py:163
  9.7 0.5 collective-permute-start
  10.2 2.6 %collective-permute-start.1 = (bf16[8,16,16,128]{3,2,1,0:T(8,128)(2,1)}, bf16[8,16,16,128]{3,2,1,0:T(8,128)(2,1)}, u32[]{:S(2)}, u32[]{:S(2)}) collective-permute-start(bf16[8,16,16,128]{3,2,1,0:T(8,128)(2,1)} %get-tuple-element.28), channel_id=1, source_target_pairs={{0,20},{4,16},{8,28},{12,24},{16,4},{20,0},{24,12},{28,8},{1,21},{... | collective-permute-start | bytes 1572872 | tf_op jit(solution)/shard_map/ppermute | solution.py:584
  12.9 1.2 %collective-permute-start.2 = (bf16[8,16,16,128]{3,2,1,0:T(8,128)(2,1)}, bf16[8,16,16,128]{3,2,1,0:T(8,128)(2,1)}, u32[]{:S(2)}, u32[]{:S(2)}) collective-permute-start(bf16[8,16,16,128]{3,2,1,0:T(8,128)(2,1)} %get-tuple-element.29), channel_id=1, source_target_pairs={{0,24},{4,28},{8,16},{12,20},{16,8},{20,12},{24,0},{28,4},{1,25},{... | collective-permute-start | bytes 1572872 | tf_op jit(solution)/shard_map/ppermute | solution.py:584
  14.1 1.0 broadcast_multiply_fusion
  16.1 0.8 tile.22.gain_ref
  16.9 0.8 copy.14.mix_ref
  17.7 0.6 copy.15
  18.4 0.5 reshape.24
  18.8 1.4 %copy.13 = f32[3,12,8,8,16]{4,3,2,1,0:T(8,128)} copy(f32[3,12,8,8,16]{4,1,3,2,0:T(8,128)S(1)} %bitcast.25) | data formatting | bytes 294912 | tf_op jit(solution)/shard_map/transpose | solution.py:564
  20.2 2.3 %reshape.25.e_ref = f32[3,12,8,128]{3,2,1,0:T(8,128)} reshape(f32[3,12,8,8,16]{4,3,2,1,0:T(8,128)} %copy.13) | data formatting | bytes 294912 | tf_op jit(solution)/shard_map/reshape | solution.py:564
  22.6 1.2 %pad.17.wi_hbm = bf16[3,320,768]{2,1,0:T(8,128)(2,1)} pad(bf16[3,192,768]{2,1,0:T(8,128)(2,1)S(1)} %copy-done, bf16[]{:T(256)} %constant.27.clone.1), padding=0_0x64_64x0_0 | pad | bytes 2359298 | tf_op jit(solution)/shard_map/jit(_pad)/pad | solution.py:566
  23.8 8.4 %band.1 = (bf16[24,1792,128]{2,1,0:T(8,128)(2,1)}, bf16[8,256,128]{2,1,0:T(8,128)(2,1)}) custom-call(s32[3]{0:T(128)} %pad_add_fusion.place, f32[3,12,8,128]{3,2,1,0:T(8,128)} %reshape.25.e_ref, f32[8,32,128]{2,1,0:T(8,128)} %copy.14.mix_ref), custom_call_target="tpu_custom_call" | custom-call | flops 1000000000 | bytes 22020096 | tf_op jit(solution)/shard_map/band/pallas_call | solution.py:335
  32.2 0.6 maximum_bitcast_fusion.fac_ref
  32.8 2.0 %fusion = (bf16[3,768,256]{2,1,0:T(8,128)(2,1)}, bf16[3,768,256]{2,1,0:T(8,128)(2,1)}) fusion(bf16[3,768,192]{2,1,0:T(8,128)(2,1)S(1)} %copy.15), kind=kLoop, calls=%fused_computation.5 | loop fusion | bytes 3244032 | tf_op jit(solution)/shard_map/jit(_pad)/pad | solution.py:568
  34.8 3.6 %collective-permute-done.2.rest_3_ = bf16[8,16,16,128]{3,2,1,0:T(8,128)(2,1)} collective-permute-done((bf16[8,16,16,128]{3,2,1,0:T(8,128)(2,1)}, bf16[8,16,16,128]{3,2,1,0:T(8,128)(2,1)}, u32[]{:S(2)}, u32[]{:S(2)}) %collective-permute-start.2) | collective-permute-done | bytes 524320 | tf_op jit(solution)/shard_map/ppermute | solution.py:584
  38.4 6.3 %mix_edges.1 = (bf16[6,96,128]{2,1,0:T(8,128)(2,1)}, bf16[6,96,128]{2,1,0:T(8,128)(2,1)}) custom-call(s32[2,512]{1,0:T(2,128)} %pairs.5, s32[3]{0:T(128)} %pad_add_fusion.place, bf16[12,8,128,128]{3,2,1,0:T(8,128)(2,1)} %get-tuple-element.34.z_hbm, bf16[8,256,128]{2,1,0:T(8,128)(2,1)} %get-tuple-element.35.rest_0_, bf16[8,16,16,128]{3,2,1,0:T(8,128)(2,1)} %copy-done.1, ...), custom_call_target="tpu_custom_call" | custom-call | flops 1000000000 | bytes 8388608 | tf_op jit(solution)/shard_map/mix_edges/pallas_call | solution.py:283
  44.7 3.5 %collective-permute-start.4 = (bf16[6,96,128]{2,1,0:T(8,128)(2,1)}, bf16[6,96,128]{2,1,0:T(8,128)(2,1)S(1)}, u32[]{:S(2)}, u32[]{:S(2)}) collective-permute-start(bf16[6,96,128]{2,1,0:T(8,128)(2,1)} %get-tuple-element.42), channel_id=1, source_target_pairs={{0,1},{1,2},{2,3},{4,5},{5,6},{6,7},{8,9},{9,10},{10,11},{12,13},{... | collective-permute-start | bytes 442376 | tf_op jit(solution)/shard_map/ppermute | solution.py:575
  48.2 1.5 %collective-permute-start.5 = (bf16[6,96,128]{2,1,0:T(8,128)(2,1)}, bf16[6,96,128]{2,1,0:T(8,128)(2,1)S(1)}, u32[]{:S(2)}, u32[]{:S(2)}) collective-permute-start(bf16[6,96,128]{2,1,0:T(8,128)(2,1)} %get-tuple-element.43), channel_id=1, source_target_pairs={{1,0},{2,1},{3,2},{5,4},{6,5},{7,6},{9,8},{10,9},{11,10},{13,12},{... | collective-permute-start | bytes 442376 | tf_op jit(solution)/shard_map/ppermute | solution.py:576
  49.7 7.0 %mix.1.zc_hbm = bf16[8,8,128,128]{3,2,1,0:T(8,128)(2,1)} custom-call(s32[2,512]{1,0:T(2,128)} %pairs.5, s32[3]{0:T(128)} %pad_add_fusion.place, bf16[12,8,128,128]{3,2,1,0:T(8,128)(2,1)} %get-tuple-element.34.z_hbm, bf16[8,256,128]{2,1,0:T(8,128)(2,1)} %get-tuple-element.35.rest_0_, bf16[8,16,16,128]{3,2,1,0:T(8,128)(2,1)} %copy-done.1, ...), custom_call_target="tpu_custom_call" | custom-call | flops 1000000000 | bytes 8388608 | tf_op jit(solution)/shard_map/mix/pallas_call | solution.py:283
  56.8 0.6 copy-done.5
  57.4 0.6 copy-done.6
  58.1 44.9 %blocks.1 = bf16[128,12288]{1,0:T(8,128)(2,1)} custom-call(s32[3]{0:T(128)} %pad_add_fusion.place, f32[1,4]{1,0:T(1,128)} %maximum_bitcast_fusion.fac_ref, bf16[8,8,128,128]{3,2,1,0:T(8,128)(2,1)} %mix.1.zc_hbm, bf16[12,8,128,128]{3,2,1,0:T(8,128)(2,1)} %get-tuple-element.34.z_hbm, bf16[6,96,128]{2,1,0:T(8,128)(2,1)} %copy-done.5, ...), custom_call_target="tpu_custom_call" | custom-call | tf_op jit(solution)/shard_map/blocks/pallas_call | solution.py:529
  (29 shorter events, 0.4 us)
Async XLA Ops:
  0.7 13.4 %copy-start.2 = (bf16[3,192,768]{2,1,0:T(8,128)(2,1)S(1)}, bf16[3,192,768]{2,1,0:T(8,128)(2,1)}, u32[]{:S(2)}) copy-start(bf16[3,192,768]{2,1,0:T(8,128)(2,1)} %param.14) | copy-start | bytes 2654212
  9.7 5.4 %copy-start.7 = (bf16[2,8,32,16]{2,3,1,0:T(8,128)(2,1)S(1)}, bf16[2,8,32,16]{2,3,1,0:T(8,128)(2,1)}, u32[]{:S(2)}) copy-start(bf16[2,8,32,16]{2,3,1,0:T(8,128)(2,1)} %param.11) | copy-start | bytes 49156
  9.7 6.1 %copy-start.8 = (f32[3,192]{1,0:T(4,128)S(1)}, f32[3,192]{1,0:T(4,128)}, u32[]{:S(2)}) copy-start(f32[3,192]{1,0:T(4,128)} %param.13) | copy-start | bytes 6916
  9.7 6.2 %copy-start.4 = (f32[3,7,7,192]{3,2,1,0:T(8,128)S(1)}, f32[3,7,7,192]{3,2,1,0:T(8,128)}, u32[]{:S(2)}) copy-start(f32[3,7,7,192]{3,2,1,0:T(8,128)} %param.12) | copy-start | bytes 338692
  9.7 25.1 %collective-permute-start = (bf16[8,16,16,128]{3,2,1,0:T(8,128)(2,1)}, bf16[8,16,16,128]{3,2,1,0:T(8,128)(2,1)S(1)}, u32[]{:S(2)}, u32[]{:S(2)}) collective-permute-start(bf16[8,16,16,128]{3,2,1,0:T(8,128)(2,1)} %get-tuple-element.27), channel_id=1, source_target_pairs={{0,16},{4,20},{8,24},{12,28},{16,0},{20,4},{24,8},{28,12},{1,17},{... | collective-permute-start | bytes 1572872 | tf_op jit(solution)/shard_map/ppermute | solution.py:584
  10.2 24.5 %collective-permute-start.1 = (bf16[8,16,16,128]{3,2,1,0:T(8,128)(2,1)}, bf16[8,16,16,128]{3,2,1,0:T(8,128)(2,1)}, u32[]{:S(2)}, u32[]{:S(2)}) collective-permute-start(bf16[8,16,16,128]{3,2,1,0:T(8,128)(2,1)} %get-tuple-element.28), channel_id=1, source_target_pairs={{0,20},{4,16},{8,28},{12,24},{16,4},{20,0},{24,12},{28,8},{1,21},{... | collective-permute-start | bytes 1572872 | tf_op jit(solution)/shard_map/ppermute | solution.py:584
  12.9 25.5 %collective-permute-start.2 = (bf16[8,16,16,128]{3,2,1,0:T(8,128)(2,1)}, bf16[8,16,16,128]{3,2,1,0:T(8,128)(2,1)}, u32[]{:S(2)}, u32[]{:S(2)}) collective-permute-start(bf16[8,16,16,128]{3,2,1,0:T(8,128)(2,1)} %get-tuple-element.29), channel_id=1, source_target_pairs={{0,24},{4,28},{8,16},{12,20},{16,8},{20,12},{24,0},{28,4},{1,25},{... | collective-permute-start | bytes 1572872 | tf_op jit(solution)/shard_map/ppermute | solution.py:584
  14.0 24.3 %collective-permute-start.3 = (bf16[8,16,16,128]{3,2,1,0:T(8,128)(2,1)}, bf16[8,16,16,128]{3,2,1,0:T(8,128)(2,1)}, u32[]{:S(2)}, u32[]{:S(2)}) collective-permute-start(bf16[8,16,16,128]{3,2,1,0:T(8,128)(2,1)} %get-tuple-element.30), channel_id=1, source_target_pairs={{0,28},{4,24},{8,20},{12,16},{16,12},{20,8},{24,4},{28,0},{1,29},{... | collective-permute-start | bytes 1572872 | tf_op jit(solution)/shard_map/ppermute | solution.py:584
  15.1 2.6 %copy-start.3 = (bf16[3,768,192]{1,2,0:T(8,128)(2,1)S(1)}, bf16[3,768,192]{1,2,0:T(8,128)(2,1)}, u32[]{:S(2)}) copy-start(bf16[3,768,192]{1,2,0:T(8,128)(2,1)} %param.15) | copy-start | bytes 2654212
  20.2 2.3 %copy-start = (bf16[3,192,768]{2,1,0:T(8,128)(2,1)S(1)}, bf16[3,192,768]{2,1,0:T(8,128)(2,1)}, u32[]{:S(2)}) copy-start(bf16[3,192,768]{2,1,0:T(8,128)(2,1)} %broadcast_multiply_fusion) | copy-start | bytes 2654212
  34.8 3.6 %copy-start.1 = (bf16[8,16,16,128]{3,2,1,0:T(8,128)(2,1)}, bf16[8,16,16,128]{3,2,1,0:T(8,128)(2,1)S(1)}, u32[]{:S(2)}) copy-start(bf16[8,16,16,128]{3,2,1,0:T(8,128)(2,1)S(1)} %collective-permute-done.rest_1_) | copy-start | bytes 1572868
  44.7 12.0 %collective-permute-start.4 = (bf16[6,96,128]{2,1,0:T(8,128)(2,1)}, bf16[6,96,128]{2,1,0:T(8,128)(2,1)S(1)}, u32[]{:S(2)}, u32[]{:S(2)}) collective-permute-start(bf16[6,96,128]{2,1,0:T(8,128)(2,1)} %get-tuple-element.42), channel_id=1, source_target_pairs={{0,1},{1,2},{2,3},{4,5},{5,6},{6,7},{8,9},{9,10},{10,11},{12,13},{... | collective-permute-start | bytes 442376 | tf_op jit(solution)/shard_map/ppermute | solution.py:575
  48.2 8.5 %collective-permute-start.5 = (bf16[6,96,128]{2,1,0:T(8,128)(2,1)}, bf16[6,96,128]{2,1,0:T(8,128)(2,1)S(1)}, u32[]{:S(2)}, u32[]{:S(2)}) collective-permute-start(bf16[6,96,128]{2,1,0:T(8,128)(2,1)} %get-tuple-element.43), channel_id=1, source_target_pairs={{1,0},{2,1},{3,2},{5,4},{6,5},{7,6},{9,8},{10,9},{11,10},{13,12},{... | collective-permute-start | bytes 442376 | tf_op jit(solution)/shard_map/ppermute | solution.py:576
  56.7 0.7 copy-start.5
  57.4 0.6 copy-start.6

commit v6 on v5

--- a/solution.py
+++ b/solution.py
@@ -91,7 +91,7 @@
     return lax.div(i, n), lax.rem(i, n)
 
 
-def pack_kernel(pairs, place, x_hbm, z_hbm, top_ref, bot_ref, *rest, mixed, tiles):
+def pack_kernel(pairs, x_hbm, z_hbm, top_ref, bot_ref, *rest, mixed, tiles):
     outs = rest[:tiles]
     xs, zs, send, order, xsem, zsem, ssem = rest[tiles:]
     ng, nj, rows, _ = zs.shape
@@ -100,7 +100,7 @@
     peer = hold // tiles
     of_tile = pairs.shape[1] // tiles
     ncb = nj // 2
-    section, tile, band_at = place[0], place[1], place[2]
+    section, tile, band_at = lax.axis_index("comp"), lax.axis_index("tile"), lax.axis_index("row")
 
     def xcopy(j):
         return pltpu.make_async_copy(x_hbm.at[:, pl.ds(pl.multiple_of(j * per, LN), per)], xs.at[j], xsem.at[j])
@@ -134,24 +134,23 @@
                 bot_ref[r, pl.ds((g - mixed) * nj + j, 1), :] = zz[g][rows - 2 * HALO + r:rows - 2 * HALO + r + 1].astype(f32)
         zcopy(j).start()
 
-    @pl.loop(0, hold)
-    def _(at):
-        up, side = part(order[at], ncb)
-        row = pl.ds(pl.multiple_of(up * 16, 16), 16)
-        for g in range(mixed):
-            for h in range(2):
-                send[at, 2 * g + h] = zs[g, 2 * side + h, row, :]
-
     copies = [pltpu.make_async_copy(send.at[pl.ds(d * peer, peer)], outs[d], ssem.at[d]) for d in range(tiles)]
-    for c in copies:
-        c.start()
+    for d in range(tiles):
+        @pl.loop(d * peer, (d + 1) * peer)
+        def _(at):
+            up, side = part(order[at], ncb)
+            row = pl.ds(pl.multiple_of(up * 16, 16), 16)
+            for g in range(mixed):
+                for h in range(2):
+                    send[at, 2 * g + h] = zs[g, 2 * side + h, row, :]
+        copies[d].start()
     for c in copies:
         c.wait()
     for j in range(nj):
         zcopy(j).wait()
 
 
-def pack(pairs, place, x, tiles, mixed, ng):
+def pack(pairs, x, tiles, mixed, ng):
     rows, width = x.shape
     per = ng * LG * PC
     nj = width // per
@@ -164,7 +163,7 @@
         functools.partial(pack_kernel, mixed=mixed, tiles=tiles),
         out_shape=(jax.ShapeDtypeStruct((ng, nj, rows, LN), bf), edge, edge)
         + (jax.ShapeDtypeStruct((hold // tiles, 2 * mixed, 16, LN), bf),) * tiles,
-        in_specs=[sm, sm, hbm],
+        in_specs=[sm, hbm],
         out_specs=(hbm, vm, vm) + (hbm,) * tiles,
         scratch_shapes=[
             VM((nj, rows, per), bf),
@@ -177,19 +176,13 @@
         ],
         compiler_params=PARAMS,
         name="pack",
-    )(pairs, place, x)
-
-
-def mix_kernel(pairs, place, z_hbm, *rest, mixed, tiles, edges):
-    wm, *rest = rest
+    )(pairs, x)
+
+
+def mix_kernel(pairs, place, z_hbm, wm, *rest, mixed, tiles):
     gots, rest = rest[:tiles], rest[tiles:]
-    if edges:
-        etop_ref, ebot_ref, otop_ref, obot_ref, top_ref, bot_ref, *rest = rest
-    else:
-        out_hbm, *rest = rest
-    zs, zp, got, count, zsem, gsem, osem = rest
+    etop_ref, ebot_ref, out_hbm, otop_ref, obot_ref, top_ref, bot_ref, zs, zp, got, count, zsem, gsem, osem = rest
     _, nj, rows, _ = zs.shape
-    whole = z_hbm.shape[2]
     hold = got.shape[0]
     peer = hold // tiles
     of_tile = pairs.shape[1] // tiles
@@ -201,19 +194,13 @@
         c.start()
 
     def zcopy(g):
-        if not edges:
-            return [pltpu.make_async_copy(z_hbm.at[g], zs.at[g], zsem.at[g, 0])]
-        return [
-            pltpu.make_async_copy(z_hbm.at[g, :, pl.ds(at, 16), :], zs.at[g, :, pl.ds(n * 16, 16), :], zsem.at[g, n])
-            for n, at in enumerate((0, whole - 16))
-        ]
+        return pltpu.make_async_copy(z_hbm.at[g], zs.at[g], zsem.at[g])
 
     def ocopy(g):
         return pltpu.make_async_copy(zs.at[g], out_hbm.at[g], osem.at[g])
 
     for g in range(mixed):
-        for c in zcopy(g):
-            c.start()
+        zcopy(g).start()
     for q in range(tiles):
         count[q] = 0
     for c in gcopy:
@@ -227,51 +214,37 @@
         at = lax.bitwise_xor(q, tile) * peer + rank
         up, side = part(slot, ncb)
 
-        def put(up):
-            row = pl.ds(pl.multiple_of(up * 16, 16), 16)
-            for g in range(mixed):
-                for h in range(2):
-                    zp[g, 2 * side + h, row, :] = got[at, 2 * g + h]
-        if edges:
-            pl.when(up == 0)(lambda: put(0))
-            pl.when(up == whole // 16 - 1)(lambda: put(1))
-        else:
-            put(up)
-
-    side = 4 if edges else 1
-
-    @pl.loop(0, mixed // side)
-    def _(gg):
-        for s in range(side):
-            g = gg * side + s
-            for c in zcopy(g):
-                c.wait()
-            own = zs[g].reshape(nj * rows, LN)
-            both = jnp.concatenate([own, zp[g].reshape(nj * rows, LN)], 1)
-            new = own.astype(f32) + jnp.dot(both, wm[g], preferred_element_type=f32)
-            new = new.astype(bf).reshape(nj, rows, LN)
-            if not edges:
-                zs[g] = new
-                ocopy(g).start()
-            for j in range(nj if edges else 0):
-                for r in range(2 * HALO):
-                    low = rows - 2 * HALO + r
-                    top_ref[r, pl.ds(g * nj + j, 1), :] = new[j, r:r + 1].astype(f32)
-                    bot_ref[r, pl.ds(g * nj + j, 1), :] = new[j, low:low + 1].astype(f32)
-
-    if edges:
-        top_ref[:, mixed * nj:, :] = etop_ref[...]
-        bot_ref[:, mixed * nj:, :] = ebot_ref[...]
-        otop_ref[...] = top_ref[...].astype(bf)
-        obot_ref[...] = bot_ref[...].astype(bf)
-    else:
+        row = pl.ds(pl.multiple_of(up * 16, 16), 16)
         for g in range(mixed):
-            ocopy(g).wait()
-
-
-def mix(pairs, place, z, w, gots, ends=()):
+            for h in range(2):
+                zp[g, 2 * side + h, row, :] = got[at, 2 * g + h]
+
+    @pl.loop(0, mixed)
+    def _(g):
+        zcopy(g).wait()
+        own = zs[g].reshape(nj * rows, LN)
+        both = jnp.concatenate([own, zp[g].reshape(nj * rows, LN)], 1)
+        new = own.astype(f32) + jnp.dot(both, wm[g], preferred_element_type=f32)
+        new = new.astype(bf).reshape(nj, rows, LN)
+        zs[g] = new
+        ocopy(g).start()
+        for j in range(nj):
+            head, tail = new[j, :16].astype(f32), new[j, rows - 16:].astype(f32)
+            for r in range(2 * HALO):
+                low = 16 - 2 * HALO + r
+                top_ref[r, pl.ds(g * nj + j, 1), :] = head[r:r + 1]
+                bot_ref[r, pl.ds(g * nj + j, 1), :] = tail[low:low + 1]
+
+    top_ref[:, mixed * nj:, :] = etop_ref[...]
+    bot_ref[:, mixed * nj:, :] = ebot_ref[...]
+    otop_ref[...] = top_ref[...].astype(bf)
+    obot_ref[...] = bot_ref[...].astype(bf)
+    for g in range(mixed):
+        ocopy(g).wait()
+
+
+def mix(pairs, place, z, w, gots, ends):
     ng, nj, rows, _ = z.shape
-    edges = len(ends) > 0
     mixed = w.shape[0]
     tiles = len(gots)
     hold = gots[0].shape[0] * tiles
@@ -279,24 +252,25 @@
     sm = pl.BlockSpec(memory_space=pltpu.SMEM)
     hbm = pl.BlockSpec(memory_space=pl.ANY)
     edge = jax.ShapeDtypeStruct((2 * HALO, ng * nj, LN), bf)
-    here = 32 if edges else rows
     return pl.pallas_call(
-        functools.partial(mix_kernel, mixed=mixed, tiles=tiles, edges=edges),
-        out_shape=(edge, edge) if edges else jax.ShapeDtypeStruct((mixed, nj, rows, LN), bf),
+        functools.partial(mix_kernel, mixed=mixed, tiles=tiles),
+        out_shape=(jax.ShapeDtypeStruct((mixed, nj, rows, LN), bf), edge, edge),
         in_specs=[sm, sm, hbm, vm] + [hbm] * tiles + [vm] * len(ends),
-        out_specs=(vm, vm) if edges else hbm,
-        scratch_shapes=([VM(edge.shape, f32)] * 2 if edges else []) + [
-            VM((mixed, nj, here, LN), bf),
-            VM((mixed, nj, here, LN), bf),
+        out_specs=(hbm, vm, vm),
+        scratch_shapes=[
+            VM(edge.shape, f32),
+            VM(edge.shape, f32),
+            VM((mixed, nj, rows, LN), bf),
+            VM((mixed, nj, rows, LN), bf),
             VM((hold,) + gots[0].shape[1:], bf),
             pltpu.SMEM((tiles,), jnp.int32),
-            pltpu.SemaphoreType.DMA((mixed, 2)),
+            pltpu.SemaphoreType.DMA((mixed,)),
             pltpu.SemaphoreType.DMA((tiles,)),
             pltpu.SemaphoreType.DMA((mixed,)),
         ],
         compiler_params=PARAMS,
         cost_estimate=pl.CostEstimate(flops=10**9, bytes_accessed=2**23, transcendentals=0),
-        name="mix_edges" if edges else "mix",
+        name="mix",
     )(pairs, place, z, w, *gots, *ends)
 
 
@@ -592,7 +566,7 @@
     tiles = lax.axis_size("tile")
     place = jnp.stack([section, lax.axis_index("tile"), lax.axis_index("row")]).astype(jnp.int32)
     pick = lambda w, i: lax.dynamic_index_in_dim(w, i, 0, keepdims=False)
-    z, etop, ebot, *outs = pack(pairs, place, state[0, 0], tiles, mix_weight.shape[1], norm_gain.shape[1] // LG)
+    z, etop, ebot, *outs = pack(pairs, state[0, 0], tiles, mix_weight.shape[1], norm_gain.shape[1] // LG)
     gots = exchange(outs)
     e, *weights = prep_all(depth_weight, norm_gain, inner_weight, outer_weight)
     wmix = jnp.tile(pick(mix_weight, section).astype(f32), (1, 1, PC))
@@ -600,8 +574,8 @@
     inside = jnp.stack([place[2] > 0, place[2] < lax.axis_size("row") - 1]).astype(f32)
     factors = jnp.concatenate([jnp.stack([factor, (section == 0).astype(f32)]), inside]).reshape(1, 4)
     gots, (bands, wmix), weights, factors = lax.optimization_barrier((gots, band(place, e, wmix), weights, factors))
-    top, bot = halo(*mix(pairs, place, z, wmix, gots, (etop, ebot)))
-    zc = mix(pairs, place, z, wmix, gots)
+    zc, top, bot = mix(pairs, place, z, wmix, gots, (etop, ebot))
+    top, bot = halo(top, bot)
     out = blocks(place, factors, zc, z, top, bot, bands, *weights)
     return out[None, None]
 

time: 104 us -> 102 us (0.981)
  Pallas kernels: 75.6 us -> 69.6 us
  waiting for transfers between devices: 3.61 us -> 9.25 us
    pallas_call x2 -> x1, Pallas kernels: 13.3 us -> 7.73 us  [mix(): pl.pallas_call(functools.partial(mix_kernel, mixed=mixed, tiles=tiles), o...]
    ppermute x1, waiting for transfers between devices: 0.01 us -> 4.01 us  [halo(): lax.ppermute(top, 'row', [(i + 1, i) for i in range(n - 1)])]
    ppermute x1, waiting for transfers between devices: 0.01 us -> 2.2 us  [halo(): lax.ppermute(bot, 'row', [(i, i + 1) for i in range(n - 1)])]
  transfers between devices with their start and end apart: 6 -> 6, of which waited for: 1 -> 3; matrix products, arithmetic and copies ran while one was open for 11% -> 12% of each run, Pallas kernels for 15% -> 8%
where the time goes in v6:
time: 102 us
  Pallas kernels  69.6 us (68%)
  local copies, waits for them, and re-layouts  10.5 us (10%)
  starting transfers between devices  9.3 us (9%)
  waiting for transfers between devices  9.25 us (9%)
  other arithmetic  2.33 us (2%)
    pallas_call x1, Pallas kernels, blocks(): pl.pallas_call(blocks_kernel, out_shape=jax.ShapeDtypeStruct((rows, nj *...  44.9 us
    pallas_call x1, Pallas kernels, pack(): pl.pallas_call(functools.partial(pack_kernel, mixed=mixed, tiles=tiles),...  8.56 us
    pallas_call x1, Pallas kernels, band(): pl.pallas_call(band_kernel, out_shape=(jax.ShapeDtypeStruct((n, 1792, LN)...  8.43 us
    pallas_call x1, Pallas kernels, mix(): pl.pallas_call(functools.partial(mix_kernel, mixed=mixed, tiles=tiles), o...  7.73 us
    ppermute x4, starting transfers between devices, exchange(): lax.ppermute(o, ('comp', 'tile'), [(s * n + t, (1 - s) * n + (t ^ d)) for...  4.34 us
    ppermute x1, waiting for transfers between devices, halo(): lax.ppermute(top, 'row', [(i + 1, i) for i in range(n - 1)])  4.01 us
    ppermute x1, starting transfers between devices, halo(): lax.ppermute(bot, 'row', [(i, i + 1) for i in range(n - 1)])  3.48 us
    ppermute x4, waiting for transfers between devices, exchange(): lax.ppermute(o, ('comp', 'tile'), [(s * n + t, (1 - s) * n + (t ^ d)) for...  3.04 us
  transfers between devices with their start and end apart: 6, of which 3 were waited for; matrix products, arithmetic and copies ran while one was open for 12% of the time, Pallas kernels for 8%

profile of v6, /device:TPU:0, one launch (start us, length us, event | category | flops | bytes accessed | tf_op | source)
XLA Modules:
  0.0 102.0 jit_solution(6413786195639310664)
XLA Ops:
  0.0 8.6 %pack.1 = (bf16[12,8,128,128]{3,2,1,0:T(8,128)(2,1)}, f32[6,32,128]{2,1,0:T(8,128)}, f32[6,32,128]{2,1,0:T(8,128)}, bf16[8,16,16,128]{3,2,1,0:T(8,128)(2,1)}, bf...) custom-call(s32[2,512]{1,0:T(2,128)} %pairs.3, ...), custom_call_target="tpu_custom_call" | custom-call | tf_op jit(solution)/shard_map/pack/pallas_call | solution.py:162
  8.6 0.5 collective-permute-start
  9.1 2.6 %collective-permute-start.1 = (bf16[8,16,16,128]{3,2,1,0:T(8,128)(2,1)}, bf16[8,16,16,128]{3,2,1,0:T(8,128)(2,1)}, u32[]{:S(2)}, u32[]{:S(2)}) collective-permute-start(bf16[8,16,16,128]{3,2,1,0:T(8,128)(2,1)} %get-tuple-element.29), channel_id=1, source_target_pairs={{0,20},{4,16},{8,28},{12,24},{16,4},{20,0},{24,12},{28,8},{1,21},{... | collective-permute-start | bytes 1572872 | tf_op jit(solution)/shard_map/ppermute | solution.py:558
  11.7 1.2 %collective-permute-start.2 = (bf16[8,16,16,128]{3,2,1,0:T(8,128)(2,1)}, bf16[8,16,16,128]{3,2,1,0:T(8,128)(2,1)}, u32[]{:S(2)}, u32[]{:S(2)}) collective-permute-start(bf16[8,16,16,128]{3,2,1,0:T(8,128)(2,1)} %get-tuple-element.30), channel_id=1, source_target_pairs={{0,24},{4,28},{8,16},{12,20},{16,8},{20,12},{24,0},{28,4},{1,25},{... | collective-permute-start | bytes 1572872 | tf_op jit(solution)/shard_map/ppermute | solution.py:558
  13.0 1.0 broadcast_multiply_fusion
  14.0 0.6 pad_add_fusion.place
  15.5 0.8 tile.22.gain_ref
  16.3 0.8 copy.14.mix_ref
  17.2 0.6 copy.15
  17.8 0.5 reshape.24
  18.3 1.4 %copy.13 = f32[3,12,8,8,16]{4,3,2,1,0:T(8,128)} copy(f32[3,12,8,8,16]{4,1,3,2,0:T(8,128)S(1)} %bitcast.25) | data formatting | bytes 294912 | tf_op jit(solution)/shard_map/transpose | solution.py:538
  19.6 2.3 %reshape.25.e_ref = f32[3,12,8,128]{3,2,1,0:T(8,128)} reshape(f32[3,12,8,8,16]{4,3,2,1,0:T(8,128)} %copy.13) | data formatting | bytes 294912 | tf_op jit(solution)/shard_map/reshape | solution.py:538
  22.0 1.2 %pad.17.wi_hbm = bf16[3,320,768]{2,1,0:T(8,128)(2,1)} pad(bf16[3,192,768]{2,1,0:T(8,128)(2,1)S(1)} %copy-done, bf16[]{:T(256)} %constant.27.clone.1), padding=0_0x64_64x0_0 | pad | bytes 2359298 | tf_op jit(solution)/shard_map/jit(_pad)/pad | solution.py:540
  23.2 8.4 %band.1 = (bf16[24,1792,128]{2,1,0:T(8,128)(2,1)}, bf16[8,256,128]{2,1,0:T(8,128)(2,1)}) custom-call(s32[3]{0:T(128)} %pad_add_fusion.place, f32[3,12,8,128]{3,2,1,0:T(8,128)} %reshape.25.e_ref, f32[8,32,128]{2,1,0:T(8,128)} %copy.14.mix_ref), custom_call_target="tpu_custom_call" | custom-call | flops 1000000000 | bytes 22020096 | tf_op jit(solution)/shard_map/band/pallas_call | solution.py:309
  31.7 0.6 maximum_bitcast_fusion.fac_ref
  32.3 1.9 %fusion = (bf16[3,768,256]{2,1,0:T(8,128)(2,1)}, bf16[3,768,256]{2,1,0:T(8,128)(2,1)}) fusion(bf16[3,768,192]{2,1,0:T(8,128)(2,1)S(1)} %copy.15), kind=kLoop, calls=%fused_computation.5 | loop fusion | bytes 3244032 | tf_op jit(solution)/shard_map/jit(_pad)/pad | solution.py:542
  34.2 3.0 %collective-permute-done.2.rest_2_ = bf16[8,16,16,128]{3,2,1,0:T(8,128)(2,1)} collective-permute-done((bf16[8,16,16,128]{3,2,1,0:T(8,128)(2,1)}, bf16[8,16,16,128]{3,2,1,0:T(8,128)(2,1)}, u32[]{:S(2)}, u32[]{:S(2)}) %collective-permute-start.2) | collective-permute-done | bytes 524320 | tf_op jit(solution)/shard_map/ppermute | solution.py:558
  37.3 7.7 %mix.1 = (bf16[8,8,128,128]{3,2,1,0:T(8,128)(2,1)}, bf16[6,96,128]{2,1,0:T(8,128)(2,1)}, bf16[6,96,128]{2,1,0:T(8,128)(2,1)}) custom-call(s32[2,512]{1,0:T(2,128)} %pairs.3, s32[3]{0:T(128)} %pad_add_fusion.place, bf16[12,8,128,128]{3,2,1,0:T(8,128)(2,1)} %get-tuple-element.35.z_hbm, bf16[8,256,128]{2,1,0:T(8,128)(2,1)} %get-tuple-element.36.wm, ...), custom_call_target="tpu_custom_call" | custom-call | flops 1000000000 | bytes 8388608 | tf_op jit(solution)/shard_map/mix/pallas_call | solution.py:255
  45.0 3.5 %collective-permute-start.4 = (bf16[6,96,128]{2,1,0:T(8,128)(2,1)}, bf16[6,96,128]{2,1,0:T(8,128)(2,1)S(1)}, u32[]{:S(2)}, u32[]{:S(2)}) collective-permute-start(bf16[6,96,128]{2,1,0:T(8,128)(2,1)} %get-tuple-element.44), channel_id=1, source_target_pairs={{0,1},{1,2},{2,3},{4,5},{5,6},{6,7},{8,9},{9,10},{10,11},{12,13},{... | collective-permute-start | bytes 442376 | tf_op jit(solution)/shard_map/ppermute | solution.py:549
  48.5 1.5 %collective-permute-start.5 = (bf16[6,96,128]{2,1,0:T(8,128)(2,1)}, bf16[6,96,128]{2,1,0:T(8,128)(2,1)S(1)}, u32[]{:S(2)}, u32[]{:S(2)}) collective-permute-start(bf16[6,96,128]{2,1,0:T(8,128)(2,1)} %get-tuple-element.45), channel_id=1, source_target_pairs={{1,0},{2,1},{3,2},{5,4},{6,5},{7,6},{9,8},{10,9},{11,10},{13,12},{... | collective-permute-start | bytes 442376 | tf_op jit(solution)/shard_map/ppermute | solution.py:550
  50.0 2.2 %collective-permute-done.4.top_ref = bf16[6,96,128]{2,1,0:T(8,128)(2,1)S(1)} collective-permute-done((bf16[6,96,128]{2,1,0:T(8,128)(2,1)}, bf16[6,96,128]{2,1,0:T(8,128)(2,1)S(1)}, u32[]{:S(2)}, u32[]{:S(2)}) %collective-permute-start.4) | collective-permute-done | bytes 147488 | tf_op jit(solution)/shard_map/ppermute | solution.py:549
  52.2 4.0 %collective-permute-done.5.bot_ref = bf16[6,96,128]{2,1,0:T(8,128)(2,1)S(1)} collective-permute-done((bf16[6,96,128]{2,1,0:T(8,128)(2,1)}, bf16[6,96,128]{2,1,0:T(8,128)(2,1)S(1)}, u32[]{:S(2)}, u32[]{:S(2)}) %collective-permute-start.5) | collective-permute-done | bytes 147488 | tf_op jit(solution)/shard_map/ppermute | solution.py:550
  56.2 0.6 copy-done.6
  56.9 44.9 %blocks.1 = bf16[128,12288]{1,0:T(8,128)(2,1)} custom-call(s32[3]{0:T(128)} %pad_add_fusion.place, f32[1,4]{1,0:T(1,128)} %maximum_bitcast_fusion.fac_ref, bf16[8,8,128,128]{3,2,1,0:T(8,128)(2,1)} %get-tuple-element.43.zc_hbm, bf16[12,8,128,128]{3,2,1,0:T(8,128)(2,1)} %get-tuple-element.35.z_hbm, bf16[6,96,128]{2,1,0:T(8,128)(2,1)} %copy-done.5, ...), custom_call_target="tpu_custom_call" | custom-call | tf_op jit(solution)/shard_map/blocks/pallas_call | solution.py:503
  (28 shorter events, 0.4 us)
Async XLA Ops:
  0.0 13.0 %copy-start.1 = (bf16[3,192,768]{2,1,0:T(8,128)(2,1)S(1)}, bf16[3,192,768]{2,1,0:T(8,128)(2,1)}, u32[]{:S(2)}) copy-start(bf16[3,192,768]{2,1,0:T(8,128)(2,1)} %param.14) | copy-start | bytes 2654212
  8.6 5.4 %copy-start.7 = (bf16[2,8,32,16]{2,3,1,0:T(8,128)(2,1)S(1)}, bf16[2,8,32,16]{2,3,1,0:T(8,128)(2,1)}, u32[]{:S(2)}) copy-start(bf16[2,8,32,16]{2,3,1,0:T(8,128)(2,1)} %param.11) | copy-start | bytes 49156
  8.6 6.7 %copy-start.8 = (f32[3,192]{1,0:T(4,128)S(1)}, f32[3,192]{1,0:T(4,128)}, u32[]{:S(2)}) copy-start(f32[3,192]{1,0:T(4,128)} %param.13) | copy-start | bytes 6916
  8.6 6.8 %copy-start.4 = (f32[3,7,7,192]{3,2,1,0:T(8,128)S(1)}, f32[3,7,7,192]{3,2,1,0:T(8,128)}, u32[]{:S(2)}) copy-start(f32[3,7,7,192]{3,2,1,0:T(8,128)} %param.12) | copy-start | bytes 338692
  8.6 25.6 %collective-permute-start = (bf16[8,16,16,128]{3,2,1,0:T(8,128)(2,1)}, bf16[8,16,16,128]{3,2,1,0:T(8,128)(2,1)S(1)}, u32[]{:S(2)}, u32[]{:S(2)}) collective-permute-start(bf16[8,16,16,128]{3,2,1,0:T(8,128)(2,1)} %get-tuple-element.28), channel_id=1, source_target_pairs={{0,16},{4,20},{8,24},{12,28},{16,0},{20,4},{24,8},{28,12},{1,17},{... | collective-permute-start | bytes 1572872 | tf_op jit(solution)/shard_map/ppermute | solution.py:558
  9.1 25.1 %collective-permute-start.1 = (bf16[8,16,16,128]{3,2,1,0:T(8,128)(2,1)}, bf16[8,16,16,128]{3,2,1,0:T(8,128)(2,1)}, u32[]{:S(2)}, u32[]{:S(2)}) collective-permute-start(bf16[8,16,16,128]{3,2,1,0:T(8,128)(2,1)} %get-tuple-element.29), channel_id=1, source_target_pairs={{0,20},{4,16},{8,28},{12,24},{16,4},{20,0},{24,12},{28,8},{1,21},{... | collective-permute-start | bytes 1572872 | tf_op jit(solution)/shard_map/ppermute | solution.py:558
  11.7 25.5 %collective-permute-start.2 = (bf16[8,16,16,128]{3,2,1,0:T(8,128)(2,1)}, bf16[8,16,16,128]{3,2,1,0:T(8,128)(2,1)}, u32[]{:S(2)}, u32[]{:S(2)}) collective-permute-start(bf16[8,16,16,128]{3,2,1,0:T(8,128)(2,1)} %get-tuple-element.30), channel_id=1, source_target_pairs={{0,24},{4,28},{8,16},{12,20},{16,8},{20,12},{24,0},{28,4},{1,25},{... | collective-permute-start | bytes 1572872 | tf_op jit(solution)/shard_map/ppermute | solution.py:558
  12.9 24.3 %collective-permute-start.3 = (bf16[8,16,16,128]{3,2,1,0:T(8,128)(2,1)}, bf16[8,16,16,128]{3,2,1,0:T(8,128)(2,1)}, u32[]{:S(2)}, u32[]{:S(2)}) collective-permute-start(bf16[8,16,16,128]{3,2,1,0:T(8,128)(2,1)} %get-tuple-element.31), channel_id=1, source_target_pairs={{0,28},{4,24},{8,20},{12,16},{16,12},{20,8},{24,4},{28,0},{1,29},{... | collective-permute-start | bytes 1572872 | tf_op jit(solution)/shard_map/ppermute | solution.py:558
  14.0 3.2 %copy-start.2 = (bf16[3,768,192]{1,2,0:T(8,128)(2,1)S(1)}, bf16[3,768,192]{1,2,0:T(8,128)(2,1)}, u32[]{:S(2)}) copy-start(bf16[3,768,192]{1,2,0:T(8,128)(2,1)} %param.15) | copy-start | bytes 2654212
  19.6 2.3 %copy-start = (bf16[3,192,768]{2,1,0:T(8,128)(2,1)S(1)}, bf16[3,192,768]{2,1,0:T(8,128)(2,1)}, u32[]{:S(2)}) copy-start(bf16[3,192,768]{2,1,0:T(8,128)(2,1)} %broadcast_multiply_fusion) | copy-start | bytes 2654212
  34.2 3.0 %copy-start.3 = (bf16[8,16,16,128]{3,2,1,0:T(8,128)(2,1)}, bf16[8,16,16,128]{3,2,1,0:T(8,128)(2,1)S(1)}, u32[]{:S(2)}) copy-start(bf16[8,16,16,128]{3,2,1,0:T(8,128)(2,1)S(1)} %collective-permute-done.rest_0_) | copy-start | bytes 1572868
  45.0 7.2 %collective-permute-start.4 = (bf16[6,96,128]{2,1,0:T(8,128)(2,1)}, bf16[6,96,128]{2,1,0:T(8,128)(2,1)S(1)}, u32[]{:S(2)}, u32[]{:S(2)}) collective-permute-start(bf16[6,96,128]{2,1,0:T(8,128)(2,1)} %get-tuple-element.44), channel_id=1, source_target_pairs={{0,1},{1,2},{2,3},{4,5},{5,6},{6,7},{8,9},{9,10},{10,11},{12,13},{... | collective-permute-start | bytes 442376 | tf_op jit(solution)/shard_map/ppermute | solution.py:549
  48.5 7.7 %collective-permute-start.5 = (bf16[6,96,128]{2,1,0:T(8,128)(2,1)}, bf16[6,96,128]{2,1,0:T(8,128)(2,1)S(1)}, u32[]{:S(2)}, u32[]{:S(2)}) collective-permute-start(bf16[6,96,128]{2,1,0:T(8,128)(2,1)} %get-tuple-element.45), channel_id=1, source_target_pairs={{1,0},{2,1},{3,2},{5,4},{6,5},{7,6},{9,8},{10,9},{11,10},{13,12},{... | collective-permute-start | bytes 442376 | tf_op jit(solution)/shard_map/ppermute | solution.py:550
  52.2 4.0 %copy-start.5 = (bf16[6,96,128]{2,1,0:T(8,128)(2,1)}, bf16[6,96,128]{2,1,0:T(8,128)(2,1)S(1)}, u32[]{:S(2)}) copy-start(bf16[6,96,128]{2,1,0:T(8,128)(2,1)S(1)} %collective-permute-done.4.top_ref) | copy-start | bytes 442372
  56.2 0.7 copy-start.6

commit v7 on v6

--- a/solution.py
+++ b/solution.py
@@ -129,9 +129,11 @@
         for g in range(ng):
             zs[g, j] = zz[g]
         for g in range(mixed, ng):
+            head, tail = zz[g][:16].astype(f32), zz[g][rows - 16:].astype(f32)
             for r in range(2 * HALO):
-                top_ref[r, pl.ds((g - mixed) * nj + j, 1), :] = zz[g][r:r + 1].astype(f32)
-                bot_ref[r, pl.ds((g - mixed) * nj + j, 1), :] = zz[g][rows - 2 * HALO + r:rows - 2 * HALO + r + 1].astype(f32)
+                low = 16 - 2 * HALO + r
+                top_ref[r, pl.ds((g - mixed) * nj + j, 1), :] = head[r:r + 1]
+                bot_ref[r, pl.ds((g - mixed) * nj + j, 1), :] = tail[low:low + 1]
         zcopy(j).start()
 
     copies = [pltpu.make_async_copy(send.at[pl.ds(d * peer, peer)], outs[d], ssem.at[d]) for d in range(tiles)]
@@ -317,7 +319,7 @@
 
 
 def blocks_kernel(place, fac_ref, zc_hbm, z_hbm, top_ref, bot_ref, w_hbm, gain_ref, wi_hbm, woe_hbm, woo_hbm, out_hbm,
-                  zs, zn, zf, lhs, wt, spr, ssum, nrm, upd, out, wi_ref, woe_ref, woo_ref, tops, bots, zsem, wsem, osem, msem):
+                  zs, zn, zf, lhs, wt, spr, ssum, nrm, upd, out, wi_ref, woe_ref, woo_ref, tops, bots, over, under, zsem, wsem, osem, msem):
     ng, nj, rows, _ = zs.shape
     hr = rows // 2
     pad = 8
@@ -357,9 +359,12 @@
     for g in range(AHEAD):
         fetch(jnp.int32(g))
 
+    over[...] = top_ref[...].astype(f32)
+    under[...] = bot_ref[...].astype(f32)
+
     for layer in range(2):
         src = (zs, zn)[layer]
-        above, below = ((top_ref, bot_ref), (tops, bots))[layer]
+        above, below = ((over, under), (tops, bots))[layer]
         have = above.shape[0]
         many = nj * hr + (4 * nj if layer == 0 else 0)
         ssum[...] = jnp.zeros_like(ssum)
@@ -380,8 +385,8 @@
                 zf[j, pl.ds(pad, rows), :] = src[g, j].astype(f32)
             hs = pl.ds(pl.multiple_of(g * nj, nj), nj)
             for r in range(HALO):
-                zf[:, pad - HALO + r, :] = above[have - HALO + r, hs, :].astype(f32)
-                zf[:, pad + rows + r, :] = below[r, hs, :].astype(f32)
+                zf[:, pad - HALO + r, :] = above[have - HALO + r, hs, :]
+                zf[:, pad + rows + r, :] = below[r, hs, :]
             m64 = lane_bit((hr, LN), 64)
             zero = jnp.zeros((hr, LN), bf)
             for a in range(8):
@@ -402,9 +407,9 @@
                         if 0 <= at < rows:
                             v = zf[:, pad + at, :]
                         elif -have <= at < 0:
-                            v = above[at + have, hs, :].astype(f32)
+                            v = above[at + have, hs, :]
                         elif rows <= at < rows + have:
-                            v = below[at - rows, hs, :].astype(f32)
+                            v = below[at - rows, hs, :]
                         else:
                             v = jnp.zeros((nj, LN), f32)
                         nxt = jnp.where(sub < nj - 1, pltpu.roll(v, nj - 1, 0), 0.0)
@@ -478,13 +483,13 @@
                     outcopy(j).start()
 
         if layer == 0:
-            more = to_patch([(fac * val).astype(bf) for val in update(pl.ds(nj * hr, 4 * nj))])
+            more = [t.astype(f32) for t in to_patch([(fac * val).astype(bf) for val in update(pl.ds(nj * hr, 4 * nj))])]
             for g in range(ng):
                 gs = pl.ds(g * nj, nj)
                 for r in range(HALO):
                     for at, keep, own, to in ((r - HALO, 2, above[have - HALO + r, gs, :], tops), (rows + r, 3, below[r, gs, :], bots)):
                         n = at % 2 * 4 * nj + ends.index(at // 2) * nj
-                        new = (own.astype(f32) + more[g][n:n + nj].astype(f32)).astype(bf)
+                        new = (own + more[g][n:n + nj]).astype(bf)
                         to[r, gs, :] = fac_ref[0, keep] * new.astype(f32)
 
     @pl.loop(0, nj)
@@ -521,6 +526,8 @@
             VM((2,) + woo.shape[1:], bf),
             VM((HALO,) + top.shape[1:], f32),
             VM((HALO,) + top.shape[1:], f32),
+            VM(top.shape, f32),
+            VM(top.shape, f32),
             pltpu.SemaphoreType.DMA((ng,)),
             pltpu.SemaphoreType.DMA((ng,)),
             pltpu.SemaphoreType.DMA((nj,)),

time: 102 us -> 102 us (level)
  no operation moved by 1% of the time
where the time goes in v7:
time: 102 us
  Pallas kernels  69.4 us (68%)
  local copies, waits for them, and re-layouts  10.5 us (10%)
  starting transfers between devices  9.3 us (9%)
  waiting for transfers between devices  9.25 us (9%)
  other arithmetic  2.33 us (2%)
    pallas_call x1, Pallas kernels, blocks(): pl.pallas_call(blocks_kernel, out_shape=jax.ShapeDtypeStruct((rows, nj *...  44.7 us
    pallas_call x1, Pallas kernels, pack(): pl.pallas_call(functools.partial(pack_kernel, mixed=mixed, tiles=tiles),...  8.56 us
    pallas_call x1, Pallas kernels, band(): pl.pallas_call(band_kernel, out_shape=(jax.ShapeDtypeStruct((n, 1792, LN)...  8.43 us
    pallas_call x1, Pallas kernels, mix(): pl.pallas_call(functools.partial(mix_kernel, mixed=mixed, tiles=tiles), o...  7.73 us
    ppermute x4, starting transfers between devices, exchange(): lax.ppermute(o, ('comp', 'tile'), [(s * n + t, (1 - s) * n + (t ^ d)) for...  4.34 us
    ppermute x1, waiting for transfers between devices, halo(): lax.ppermute(top, 'row', [(i + 1, i) for i in range(n - 1)])  4.01 us
    ppermute x1, starting transfers between devices, halo(): lax.ppermute(bot, 'row', [(i, i + 1) for i in range(n - 1)])  3.48 us
    ppermute x4, waiting for transfers between devices, exchange(): lax.ppermute(o, ('comp', 'tile'), [(s * n + t, (1 - s) * n + (t ^ d)) for...  3.04 us
  transfers between devices with their start and end apart: 6, of which 3 were waited for; matrix products, arithmetic and copies ran while one was open for 12% of the time, Pallas kernels for 8%

profile of v7, /device:TPU:0, one launch (start us, length us, event | category | flops | bytes accessed | tf_op | source)
XLA Modules:
  0.0 101.7 jit_solution(10986057701465488611)
XLA Ops:
  0.0 8.6 %pack.1 = (bf16[12,8,128,128]{3,2,1,0:T(8,128)(2,1)}, f32[6,32,128]{2,1,0:T(8,128)}, f32[6,32,128]{2,1,0:T(8,128)}, bf16[8,16,16,128]{3,2,1,0:T(8,128)(2,1)}, bf...) custom-call(s32[2,512]{1,0:T(2,128)} %pairs.3, ...), custom_call_target="tpu_custom_call" | custom-call | tf_op jit(solution)/shard_map/pack/pallas_call | solution.py:164
  8.6 0.5 collective-permute-start
  9.1 2.6 %collective-permute-start.1 = (bf16[8,16,16,128]{3,2,1,0:T(8,128)(2,1)}, bf16[8,16,16,128]{3,2,1,0:T(8,128)(2,1)}, u32[]{:S(2)}, u32[]{:S(2)}) collective-permute-start(bf16[8,16,16,128]{3,2,1,0:T(8,128)(2,1)} %get-tuple-element.29), channel_id=1, source_target_pairs={{0,20},{4,16},{8,28},{12,24},{16,4},{20,0},{24,12},{28,8},{1,21},{... | collective-permute-start | bytes 1572872 | tf_op jit(solution)/shard_map/ppermute | solution.py:565
  11.7 1.2 %collective-permute-start.2 = (bf16[8,16,16,128]{3,2,1,0:T(8,128)(2,1)}, bf16[8,16,16,128]{3,2,1,0:T(8,128)(2,1)}, u32[]{:S(2)}, u32[]{:S(2)}) collective-permute-start(bf16[8,16,16,128]{3,2,1,0:T(8,128)(2,1)} %get-tuple-element.30), channel_id=1, source_target_pairs={{0,24},{4,28},{8,16},{12,20},{16,8},{20,12},{24,0},{28,4},{1,25},{... | collective-permute-start | bytes 1572872 | tf_op jit(solution)/shard_map/ppermute | solution.py:565
  13.0 1.0 broadcast_multiply_fusion
  14.0 0.6 pad_add_fusion.place
  15.5 0.8 tile.22.gain_ref
  16.3 0.8 copy.14.mix_ref
  17.2 0.6 copy.15
  17.8 0.5 reshape.24
  18.3 1.4 %copy.13 = f32[3,12,8,8,16]{4,3,2,1,0:T(8,128)} copy(f32[3,12,8,8,16]{4,1,3,2,0:T(8,128)S(1)} %bitcast.25) | data formatting | bytes 294912 | tf_op jit(solution)/shard_map/transpose | solution.py:545
  19.6 2.3 %reshape.25.e_ref = f32[3,12,8,128]{3,2,1,0:T(8,128)} reshape(f32[3,12,8,8,16]{4,3,2,1,0:T(8,128)} %copy.13) | data formatting | bytes 294912 | tf_op jit(solution)/shard_map/reshape | solution.py:545
  22.0 1.2 %pad.17.wi_hbm = bf16[3,320,768]{2,1,0:T(8,128)(2,1)} pad(bf16[3,192,768]{2,1,0:T(8,128)(2,1)S(1)} %copy-done, bf16[]{:T(256)} %constant.27.clone.1), padding=0_0x64_64x0_0 | pad | bytes 2359298 | tf_op jit(solution)/shard_map/jit(_pad)/pad | solution.py:547
  23.2 8.4 %band.1 = (bf16[24,1792,128]{2,1,0:T(8,128)(2,1)}, bf16[8,256,128]{2,1,0:T(8,128)(2,1)}) custom-call(s32[3]{0:T(128)} %pad_add_fusion.place, f32[3,12,8,128]{3,2,1,0:T(8,128)} %reshape.25.e_ref, f32[8,32,128]{2,1,0:T(8,128)} %copy.14.mix_ref), custom_call_target="tpu_custom_call" | custom-call | flops 1000000000 | bytes 22020096 | tf_op jit(solution)/shard_map/band/pallas_call | solution.py:311
  31.7 0.6 maximum_bitcast_fusion.fac_ref
  32.3 1.9 %fusion = (bf16[3,768,256]{2,1,0:T(8,128)(2,1)}, bf16[3,768,256]{2,1,0:T(8,128)(2,1)}) fusion(bf16[3,768,192]{2,1,0:T(8,128)(2,1)S(1)} %copy.15), kind=kLoop, calls=%fused_computation.5 | loop fusion | bytes 3244032 | tf_op jit(solution)/shard_map/jit(_pad)/pad | solution.py:549
  34.2 3.0 %collective-permute-done.2.rest_2_ = bf16[8,16,16,128]{3,2,1,0:T(8,128)(2,1)} collective-permute-done((bf16[8,16,16,128]{3,2,1,0:T(8,128)(2,1)}, bf16[8,16,16,128]{3,2,1,0:T(8,128)(2,1)}, u32[]{:S(2)}, u32[]{:S(2)}) %collective-permute-start.2) | collective-permute-done | bytes 524320 | tf_op jit(solution)/shard_map/ppermute | solution.py:565
  37.3 7.7 %mix.1 = (bf16[8,8,128,128]{3,2,1,0:T(8,128)(2,1)}, bf16[6,96,128]{2,1,0:T(8,128)(2,1)}, bf16[6,96,128]{2,1,0:T(8,128)(2,1)}) custom-call(s32[2,512]{1,0:T(2,128)} %pairs.3, s32[3]{0:T(128)} %pad_add_fusion.place, bf16[12,8,128,128]{3,2,1,0:T(8,128)(2,1)} %get-tuple-element.35.z_hbm, bf16[8,256,128]{2,1,0:T(8,128)(2,1)} %get-tuple-element.36.wm, ...), custom_call_target="tpu_custom_call" | custom-call | flops 1000000000 | bytes 8388608 | tf_op jit(solution)/shard_map/mix/pallas_call | solution.py:257
  45.0 3.5 %collective-permute-start.4 = (bf16[6,96,128]{2,1,0:T(8,128)(2,1)}, bf16[6,96,128]{2,1,0:T(8,128)(2,1)S(1)}, u32[]{:S(2)}, u32[]{:S(2)}) collective-permute-start(bf16[6,96,128]{2,1,0:T(8,128)(2,1)} %get-tuple-element.44), channel_id=1, source_target_pairs={{0,1},{1,2},{2,3},{4,5},{5,6},{6,7},{8,9},{9,10},{10,11},{12,13},{... | collective-permute-start | bytes 442376 | tf_op jit(solution)/shard_map/ppermute | solution.py:556
  48.5 1.5 %collective-permute-start.5 = (bf16[6,96,128]{2,1,0:T(8,128)(2,1)}, bf16[6,96,128]{2,1,0:T(8,128)(2,1)S(1)}, u32[]{:S(2)}, u32[]{:S(2)}) collective-permute-start(bf16[6,96,128]{2,1,0:T(8,128)(2,1)} %get-tuple-element.45), channel_id=1, source_target_pairs={{1,0},{2,1},{3,2},{5,4},{6,5},{7,6},{9,8},{10,9},{11,10},{13,12},{... | collective-permute-start | bytes 442376 | tf_op jit(solution)/shard_map/ppermute | solution.py:557
  50.0 2.2 %collective-permute-done.4.top_ref = bf16[6,96,128]{2,1,0:T(8,128)(2,1)S(1)} collective-permute-done((bf16[6,96,128]{2,1,0:T(8,128)(2,1)}, bf16[6,96,128]{2,1,0:T(8,128)(2,1)S(1)}, u32[]{:S(2)}, u32[]{:S(2)}) %collective-permute-start.4) | collective-permute-done | bytes 147488 | tf_op jit(solution)/shard_map/ppermute | solution.py:556
  52.2 4.0 %collective-permute-done.5.bot_ref = bf16[6,96,128]{2,1,0:T(8,128)(2,1)S(1)} collective-permute-done((bf16[6,96,128]{2,1,0:T(8,128)(2,1)}, bf16[6,96,128]{2,1,0:T(8,128)(2,1)S(1)}, u32[]{:S(2)}, u32[]{:S(2)}) %collective-permute-start.5) | collective-permute-done | bytes 147488 | tf_op jit(solution)/shard_map/ppermute | solution.py:557
  56.2 0.6 copy-done.6
  56.9 44.7 %blocks.1 = bf16[128,12288]{1,0:T(8,128)(2,1)} custom-call(s32[3]{0:T(128)} %pad_add_fusion.place, f32[1,4]{1,0:T(1,128)} %maximum_bitcast_fusion.fac_ref, bf16[8,8,128,128]{3,2,1,0:T(8,128)(2,1)} %get-tuple-element.43.zc_hbm, bf16[12,8,128,128]{3,2,1,0:T(8,128)(2,1)} %get-tuple-element.35.z_hbm, bf16[6,96,128]{2,1,0:T(8,128)(2,1)} %copy-done.5, ...), custom_call_target="tpu_custom_call" | custom-call | tf_op jit(solution)/shard_map/blocks/pallas_call | solution.py:508
  (28 shorter events, 0.4 us)
Async XLA Ops:
  0.0 13.0 %copy-start.1 = (bf16[3,192,768]{2,1,0:T(8,128)(2,1)S(1)}, bf16[3,192,768]{2,1,0:T(8,128)(2,1)}, u32[]{:S(2)}) copy-start(bf16[3,192,768]{2,1,0:T(8,128)(2,1)} %param.14) | copy-start | bytes 2654212
  8.6 5.4 %copy-start.7 = (bf16[2,8,32,16]{2,3,1,0:T(8,128)(2,1)S(1)}, bf16[2,8,32,16]{2,3,1,0:T(8,128)(2,1)}, u32[]{:S(2)}) copy-start(bf16[2,8,32,16]{2,3,1,0:T(8,128)(2,1)} %param.11) | copy-start | bytes 49156
  8.6 6.7 %copy-start.8 = (f32[3,192]{1,0:T(4,128)S(1)}, f32[3,192]{1,0:T(4,128)}, u32[]{:S(2)}) copy-start(f32[3,192]{1,0:T(4,128)} %param.13) | copy-start | bytes 6916
  8.6 6.8 %copy-start.4 = (f32[3,7,7,192]{3,2,1,0:T(8,128)S(1)}, f32[3,7,7,192]{3,2,1,0:T(8,128)}, u32[]{:S(2)}) copy-start(f32[3,7,7,192]{3,2,1,0:T(8,128)} %param.12) | copy-start | bytes 338692
  8.6 25.6 %collective-permute-start = (bf16[8,16,16,128]{3,2,1,0:T(8,128)(2,1)}, bf16[8,16,16,128]{3,2,1,0:T(8,128)(2,1)S(1)}, u32[]{:S(2)}, u32[]{:S(2)}) collective-permute-start(bf16[8,16,16,128]{3,2,1,0:T(8,128)(2,1)} %get-tuple-element.28), channel_id=1, source_target_pairs={{0,16},{4,20},{8,24},{12,28},{16,0},{20,4},{24,8},{28,12},{1,17},{... | collective-permute-start | bytes 1572872 | tf_op jit(solution)/shard_map/ppermute | solution.py:565
  9.1 25.1 %collective-permute-start.1 = (bf16[8,16,16,128]{3,2,1,0:T(8,128)(2,1)}, bf16[8,16,16,128]{3,2,1,0:T(8,128)(2,1)}, u32[]{:S(2)}, u32[]{:S(2)}) collective-permute-start(bf16[8,16,16,128]{3,2,1,0:T(8,128)(2,1)} %get-tuple-element.29), channel_id=1, source_target_pairs={{0,20},{4,16},{8,28},{12,24},{16,4},{20,0},{24,12},{28,8},{1,21},{... | collective-permute-start | bytes 1572872 | tf_op jit(solution)/shard_map/ppermute | solution.py:565
  11.7 25.5 %collective-permute-start.2 = (bf16[8,16,16,128]{3,2,1,0:T(8,128)(2,1)}, bf16[8,16,16,128]{3,2,1,0:T(8,128)(2,1)}, u32[]{:S(2)}, u32[]{:S(2)}) collective-permute-start(bf16[8,16,16,128]{3,2,1,0:T(8,128)(2,1)} %get-tuple-element.30), channel_id=1, source_target_pairs={{0,24},{4,28},{8,16},{12,20},{16,8},{20,12},{24,0},{28,4},{1,25},{... | collective-permute-start | bytes 1572872 | tf_op jit(solution)/shard_map/ppermute | solution.py:565
  12.9 24.3 %collective-permute-start.3 = (bf16[8,16,16,128]{3,2,1,0:T(8,128)(2,1)}, bf16[8,16,16,128]{3,2,1,0:T(8,128)(2,1)}, u32[]{:S(2)}, u32[]{:S(2)}) collective-permute-start(bf16[8,16,16,128]{3,2,1,0:T(8,128)(2,1)} %get-tuple-element.31), channel_id=1, source_target_pairs={{0,28},{4,24},{8,20},{12,16},{16,12},{20,8},{24,4},{28,0},{1,29},{... | collective-permute-start | bytes 1572872 | tf_op jit(solution)/shard_map/ppermute | solution.py:565
  14.0 3.2 %copy-start.2 = (bf16[3,768,192]{1,2,0:T(8,128)(2,1)S(1)}, bf16[3,768,192]{1,2,0:T(8,128)(2,1)}, u32[]{:S(2)}) copy-start(bf16[3,768,192]{1,2,0:T(8,128)(2,1)} %param.15) | copy-start | bytes 2654212
  19.6 2.3 %copy-start = (bf16[3,192,768]{2,1,0:T(8,128)(2,1)S(1)}, bf16[3,192,768]{2,1,0:T(8,128)(2,1)}, u32[]{:S(2)}) copy-start(bf16[3,192,768]{2,1,0:T(8,128)(2,1)} %broadcast_multiply_fusion) | copy-start | bytes 2654212
  34.2 3.0 %copy-start.3 = (bf16[8,16,16,128]{3,2,1,0:T(8,128)(2,1)}, bf16[8,16,16,128]{3,2,1,0:T(8,128)(2,1)S(1)}, u32[]{:S(2)}) copy-start(bf16[8,16,16,128]{3,2,1,0:T(8,128)(2,1)S(1)} %collective-permute-done.rest_0_) | copy-start | bytes 1572868
  45.0 7.2 %collective-permute-start.4 = (bf16[6,96,128]{2,1,0:T(8,128)(2,1)}, bf16[6,96,128]{2,1,0:T(8,128)(2,1)S(1)}, u32[]{:S(2)}, u32[]{:S(2)}) collective-permute-start(bf16[6,96,128]{2,1,0:T(8,128)(2,1)} %get-tuple-element.44), channel_id=1, source_target_pairs={{0,1},{1,2},{2,3},{4,5},{5,6},{6,7},{8,9},{9,10},{10,11},{12,13},{... | collective-permute-start | bytes 442376 | tf_op jit(solution)/shard_map/ppermute | solution.py:556
  48.5 7.7 %collective-permute-start.5 = (bf16[6,96,128]{2,1,0:T(8,128)(2,1)}, bf16[6,96,128]{2,1,0:T(8,128)(2,1)S(1)}, u32[]{:S(2)}, u32[]{:S(2)}) collective-permute-start(bf16[6,96,128]{2,1,0:T(8,128)(2,1)} %get-tuple-element.45), channel_id=1, source_target_pairs={{1,0},{2,1},{3,2},{5,4},{6,5},{7,6},{9,8},{10,9},{11,10},{13,12},{... | collective-permute-start | bytes 442376 | tf_op jit(solution)/shard_map/ppermute | solution.py:557
  52.2 4.0 %copy-start.5 = (bf16[6,96,128]{2,1,0:T(8,128)(2,1)}, bf16[6,96,128]{2,1,0:T(8,128)(2,1)S(1)}, u32[]{:S(2)}) copy-start(bf16[6,96,128]{2,1,0:T(8,128)(2,1)S(1)} %collective-permute-done.4.top_ref) | copy-start | bytes 442372
  56.2 0.7 copy-start.6
